TPU v7x, 32 devices: a whole 2x2x4 slice. The times are simulated.
32 devices in a mesh: gx: 8 (over z, y), gy: 4 (over x, core).
Axes of the slice: x: 2, y: 2, z: 4, core: 2. Of those that a mesh axis runs over, the one named last changes fastest.
Arguments:
- modes: bfloat16 [128, 64, 2, 3, 128], P('gx', 'gy'), may hold values from -8 to 8
Outputs:
- convective: float32 [128, 128, 128], P('gx', 'gy')
- viscous: float32 [128, 128], P('gx', 'gy')
All inputs are finite; a program needn't handle non-finite values.
Results may differ from a plain program's by a relative error of at most 0.004.
Values may be sent and summed in bfloat16 or wider, within the bound.
No kernel may reach another device: no remote copies, remote signals or barrier semaphores. Data moves between devices by JAX's collectives and lax.ppermute only.
A program may use at most 64 MiB of HBM per device.

v0:
```python
import math

import jax
import jax.numpy as jnp
from jax import lax
from jax.sharding import PartitionSpec as P


def padded_2(x, sides, width):
    for axis, dim in sides:
        peers, length = (lax.axis_size(axis), x.shape[dim])
        up = [(i, (i + 1) % peers) for i in range(peers)]
        down = [(j, i) for i, j in up]
        last = lax.slice_in_dim(x, length - width, length, axis=dim)
        initial = lax.slice_in_dim(x, 0, width, axis=dim)
        before = lax.ppermute(last, axis, up)
        after = lax.ppermute(initial, axis, down)
        x = jnp.concatenate([before, x, after], axis=dim)
    return x


def fourth(padded, axis, count):

    def cut(offset):
        return lax.slice_in_dim(padded, 2 + offset, 2 + offset + count, axis=axis)

    return (8.0 * (cut(1) - cut(-1)) - (cut(2) - cut(-2))) / 12.0


def block_terms(count, make_pair, right_side, width):
    block_rows = math.gcd(count, 4)
    starts_list = block_rows * jnp.arange(count // block_rows, dtype=jnp.int32)

    def one_block(low):
        pair = make_pair(low, block_rows)
        term = jnp.dot(
            pair.reshape(block_rows * width, -1), right_side, preferred_element_type=jnp.float32
        )
        return term.reshape(block_rows, width, width)

    return lax.map(one_block, starts_list).reshape(count, width, width)


def body(modes):
    cells_x, cells_y, cells_z, comps, width = modes.shape
    points = cells_x * cells_y * cells_z
    total_points = points * lax.axis_size("gx") * lax.axis_size("gy")
    padded = padded_2(modes, (("gx", 0), ("gy", 1)), 2).astype(jnp.float32)
    inner = padded[2:-2, 2:-2]
    grad_x = fourth(padded[:, 2:-2], 0, cells_x)
    grad_y = fourth(padded[2:-2], 1, cells_y)
    grad_z = fourth(jnp.pad(inner, ((0, 0), (0, 0), (2, 2), (0, 0), (0, 0))), 2, cells_z)
    gradient = jnp.stack([grad_x, grad_y, grad_z]).astype(jnp.bfloat16)
    flat_modes = modes.reshape(points, comps, width)
    by_comp = flat_modes.transpose(1, 2, 0)
    right_side = flat_modes.transpose(1, 0, 2).reshape(comps * points, width)
    spread = gradient.reshape(3, points, comps, width).transpose(2, 3, 0, 1)
    stacked = gradient.reshape(-1, width)
    visc_part = -lax.dot_general(
        stacked, stacked, (((0,), (0,)), ((), ())), preferred_element_type=jnp.float32
    )

    def pair_second(low, block_rows):
        rows = lax.dynamic_slice_in_dim(spread, low, block_rows, 1)
        product = rows[:, :, None].astype(jnp.float32) * by_comp[:, None, :, None, :].astype(
            jnp.float32
        )
        return jnp.sum(product, axis=0).astype(jnp.bfloat16)

    conv_cols = lax.psum_scatter(
        block_terms(
            width // lax.axis_size("gy") * lax.axis_size("gy"), pair_second, right_side, width
        ),
        "gy",
        scatter_dimension=0,
        tiled=True,
    )
    visc_cols = lax.psum_scatter(
        visc_part.T.astype(jnp.bfloat16), "gy", scatter_dimension=0, tiled=True
    ).astype(jnp.float32)
    conv_turned, visc_turned = (
        lax.psum_scatter(conv_cols, "gx", scatter_dimension=1, tiled=True),
        lax.psum_scatter(visc_cols, "gx", scatter_dimension=1, tiled=True),
    )
    conv_own = conv_turned.transpose(1, 0, 2)
    visc_own = visc_turned.T
    convective = conv_own * (-1.0 / math.sqrt(total_points))
    viscous = visc_own / total_points
    return (convective, viscous)


def solution(mesh):
    in_specs = (P("gx", "gy", None, None, None),)
    out_specs = (P("gx", "gy", None), P("gx", "gy"))
    return jax.shard_map(body, mesh=mesh, in_specs=in_specs, out_specs=out_specs, check_vma=False)
```

profile of v0, /device:TPU:0, one launch (start us, length us, event | category | flops | bytes accessed | tf_op | source)
XLA Modules:
  0.0 447.4 jit_solution(16397138387852923574)
XLA Ops:
  7.2 0.9 fusion.29
  8.2 3.0 collective-permute-start
  11.2 3.1 collective-permute-start.1
  14.3 1.3 copy.42
  16.7 1.7 collective-permute-start.3
  18.4 1.9 collective-permute-done.2
  22.4 1.1 fusion.13
  23.7 2.5 copy.43
  26.2 203.8 %while.10 = (s32[]{:T(128)}, f32[32,4,128,128]{3,1,0,2:T(4,128)}, s32[32]{0:T(128)S(1)}, bf16[3,128,3,512]{3,2,1,0:T(4,128)(2,1)}, bf16[3,128,512]{2,1,0:T(8,128...) while((s32[]{:T(128)}, f32[32,4,128,128]{3,1,0,2:T(4,128)}, ...), condition=%wide.region_2.3_spmd, body=%wide.region_0.2_spmd.sunk | while | flops 205473792 | bytes 12767443 | solution.py:41
  31.7 0.9 copy_dynamic-update-slice_fusion.2
  38.0 0.9 copy_dynamic-update-slice_fusion.2
  50.8 1.0 copy_dynamic-update-slice_fusion.2
  89.0 0.9 copy_dynamic-update-slice_fusion.2
  120.8 1.0 copy_dynamic-update-slice_fusion.2
  146.3 0.9 copy_dynamic-update-slice_fusion.2
  159.0 1.0 copy_dynamic-update-slice_fusion.2
  165.4 1.0 copy_dynamic-update-slice_fusion.2
  203.6 0.9 copy_dynamic-update-slice_fusion.2
  229.0 0.9 copy_dynamic-update-slice_fusion.2
  230.1 1.4 copy.49
  231.6 72.1 %reduce-scatter.7.cloned.1.call-done = f32[32,128,128]{2,0,1:T(8,128)} async-done(((f32[128,128,128]{2,0,1:T(8,128)}), f32[32,128,128]{2,0,1:T(8,128)}) %reduce-scatter.7.cloned.1.call-update) | async-done | bytes 2097168 | tf_op jit(solution)/shard_map/reduce_scatter | solution.py:70
  303.7 65.2 %reduce-scatter.13.cloned.1.call-done = f32[16,32]{1,0:T(8,128)} async-done(((f32[128,32]{1,0:T(8,128)}), f32[16,32]{1,0:T(8,128)}) %reduce-scatter.13.cloned.1.call-update) | async-done | bytes 2064
  370.4 68.9 %reduce-scatter.9.cloned.1.call-done = f32[32,16,128]{2,0,1:T(8,128)} async-done(((f32[32,128,128]{2,0,1:T(8,128)}), f32[32,16,128]{2,0,1:T(8,128)}) %reduce-scatter.9.cloned.1.call-update) | async-done | bytes 262160 | tf_op jit(solution)/shard_map/reduce_scatter | solution.py:82
  439.2 1.7 multiply_bitcast_fusion
  (377 shorter events, 145.2 us)
Async XLA Ops:
  7.2 9.2 %copy-start.2 = (bf16[16,16,2,3,128]{4,2,3,1,0:T(2,128)(2,1)S(1)}, bf16[16,16,2,3,128]{4,2,3,1,0:T(2,128)(2,1)}, u32[]{:S(2)}) copy-start(bf16[16,16,2,3,128]{4,2,3,1,0:T(2,128)(2,1)} %param.3) | copy-start | bytes 1179652
  7.2 222.9 %reduce-scatter.11.cloned.1.call-start = ((), (), s32[]{:S(2)}) async-start(), calls=%async_computation.6 | async-start | bytes 40960 | tf_op jit(solution)/shard_map/reduce_scatter | solution.py:78
  8.2 8.2 %collective-permute-start = (bf16[2,16,2,3,128]{4,1,3,2,0:T(8,128)(2,1)S(1)}, bf16[2,16,2,3,128]{4,1,3,2,0:T(8,128)(2,1)S(1)}, u32[]{:S(2)}, u32[]{:S(2)}) collective-permute-start(bf16[2,16,2,3,128]{4,1,3,2,0:T(8,128)(2,1)S(1)} %copy.56), channel_id=1, source_target_pairs={{0,4},{4,8},{8,12},{12,16},{16,20},{20,24},{24,28},{28,0},{1,5},{5... | collective-permute-start | bytes 147464 | tf_op jit(solution)/shard_map/ppermute | solution.py:16
  11.2 5.3 %collective-permute-start.1 = (bf16[2,16,2,3,128]{4,1,3,2,0:T(8,128)(2,1)S(1)}, bf16[2,16,2,3,128]{4,1,3,2,0:T(8,128)(2,1)S(1)}, u32[]{:S(2)}, u32[]{:S(2)}) collective-permute-start(bf16[2,16,2,3,128]{4,1,3,2,0:T(8,128)(2,1)S(1)} %copy.57), channel_id=1, source_target_pairs={{4,0},{8,4},{12,8},{16,12},{20,16},{24,20},{28,24},{0,28},{5,1},{9... | collective-permute-start | bytes 147464 | tf_op jit(solution)/shard_map/ppermute | solution.py:17
  16.6 3.7 collective-permute-start.2
  16.7 3.6 collective-permute-start.3
  23.5 280.1 %reduce-scatter.7.cloned.1.call-start = ((), (), s32[]{:S(2)}) async-start(), calls=%async_computation.4 | async-start | bytes 10485760 | tf_op jit(solution)/shard_map/reduce_scatter | solution.py:70
  32.6 3.1 copy-start
  39.0 3.1 copy-start
  45.3 3.1 copy-start
  51.7 3.1 copy-start
  58.1 3.1 copy-start
  64.4 3.1 copy-start
  70.8 3.1 copy-start
  77.2 3.1 copy-start
  83.5 3.1 copy-start
  89.9 3.1 copy-start
  96.3 3.1 copy-start
  102.6 3.1 copy-start
  109.0 3.1 copy-start
  115.3 3.1 copy-start
  128.1 3.1 copy-start
  230.0 138.9 %reduce-scatter.13.cloned.1.call-start = ((), (), s32[]{:S(2)}) async-start(), calls=%async_computation.7 | async-start | bytes 73728
  231.5 207.7 %reduce-scatter.9.cloned.1.call-start = ((), (), s32[]{:S(2)}) async-start(), calls=%async_computation.5 | async-start | bytes 2359296 | tf_op jit(solution)/shard_map/reduce_scatter | solution.py:82
  (49 other events, 101.6 us)
Sparse Core Ops, SparseCore 0:
  23.7 21.1 reduce-scatter.10
  230.1 73.4 reduce-scatter.6
  307.6 61.2 reduce-scatter.12
  372.3 66.8 reduce-scatter.8
where the time goes:
time: 450 us; the launch traced here: 447 us
  waiting for transfers between devices  209 us (46%)
  local copies, waits for them, and re-layouts  86.7 us (19%)
  other arithmetic  55.4 us (12%)
  loops' own time  54 us (12%)
  matrix products  20.6 us (5%)
  between operations  13.9 us (3%)
  starting transfers between devices  8.08 us (2%)
    reduce_scatter x1, waiting for transfers between devices, body(): lax.psum_scatter(block_terms(width // lax.axis_size('gy') * lax.axis_size...  72.1 us
    reduce_scatter x1, waiting for transfers between devices, body(): lax.psum_scatter(conv_cols, 'gx', scatter_dimension=1, tiled=True)  68.9 us
    unnamed x5, waiting for transfers between devices  65.3 us
    another operation x1, loops' own time, block_terms(): return lax.map(one_block, starts_list).reshape(count, width, width)  54 us
    dynamic_update_slice x32, local copies, waits for them, and re-layouts, block_terms(): return lax.map(one_block, starts_list).reshape(count, width, width)  29.5 us
    convert_element_type x32, local copies, waits for them, and re-layouts, pair_second(): return jnp.sum(product, axis=0).astype(jnp.bfloat16)  28.8 us
    convert_element_type x32, other arithmetic, pair_second(): rows[:, :, None].astype(jnp.float32)  26.1 us
    reduce_sum x32, other arithmetic, pair_second(): return jnp.sum(product, axis=0).astype(jnp.bfloat16)  23.8 us
  transfers between devices with their start and end apart: 8, of which 5 were waited for; matrix products, arithmetic and copies ran while one was open for 35% of the time, Pallas kernels for 0%

commit v1 on v0

v1 whole, which is shorter than its diff:
```python
import functools
import math

import jax
import jax.numpy as jnp
from jax import lax
from jax.experimental import pallas as pl
from jax.experimental.pallas import tpu as pltpu
from jax.sharding import PartitionSpec as P

BF16, F32 = jnp.bfloat16, jnp.float32
VMEM = pl.BlockSpec(memory_space=pltpu.VMEM)
SMEM = pl.BlockSpec(memory_space=pltpu.SMEM)
CHUNKS = 2
GROUP = 16
K_ROWS = 4


def swap(x, axis, mask):
    return lax.ppermute(x, axis, [(i, i ^ mask) for i in range(lax.axis_size(axis))])


def gathered(x, axis):
    pieces, mask = [x], lax.axis_size(axis) // 2
    masks = [0]
    while mask:
        pieces += [swap(piece, axis, mask) for piece in pieces]
        masks += [m ^ mask for m in masks]
        mask //= 2
    return pieces, masks


def derivatives(fetch, row, cells_z):
    mid = fetch(row)
    lanes = mid.shape[-1]

    def moved(points):
        return pltpu.roll(mid, (-points) % lanes, 1)

    def stencil(p1, m1, p2, m2):
        return (8.0 * (p1 - m1) - (p2 - m2)) * (1.0 / 12.0)

    grad_x = stencil(fetch(row + 1), fetch(row - 1), fetch(row + 2), fetch(row - 2))
    grad_y = stencil(
        moved(cells_z), moved(-cells_z), moved(2 * cells_z), moved(-2 * cells_z)
    )
    level = lax.broadcasted_iota(jnp.int32, mid.shape, 1) % cells_z
    grad_z = jnp.zeros_like(mid)
    for step, weight in ((1, 8.0 / 12.0), (-1, -8.0 / 12.0), (2, -1.0 / 12.0), (-2, 1.0 / 12.0)):
        if abs(step) < cells_z:
            inside = (level + step >= 0) & (level + step < cells_z)
            grad_z = grad_z + jnp.where(inside, moved(step) * weight, 0.0)
    return grad_x, grad_y, grad_z


def prepare_kernel(plan, masks, cells_z, repeat, idx_ref, *refs):
    copies, interior, count_sources = plan
    pieces = len(masks)
    sources = [refs[s * pieces:(s + 1) * pieces] for s in range(count_sources)]
    full_ref, turned_ref, grad_ref, visc_ref = refs[count_sources * pieces:]
    rows, comps, lanes, width = full_ref.shape
    part = lanes // pieces
    me = idx_ref[0]
    own = width // pieces
    for q, mask in enumerate(masks):
        slot = pl.multiple_of((me ^ mask) * part, part)
        for source, start, stop, at in copies:
            full_ref[at:at + stop - start, :, pl.ds(slot, part), :] = sources[source][q][start:stop]

    def turn(row, carry):
        for comp in range(comps):
            flat = full_ref[row, comp].astype(F32).T
            turned_ref[row, comp] = flat.reshape(width // 8, 8, lanes)
        return carry

    lax.fori_loop(0, rows, turn, 0)
    visc_ref[...] = jnp.zeros_like(visc_ref)

    def slopes(at, row):
        mine, every = [], []
        for comp in range(comps):
            def fetch_own(r):
                block = turned_ref[r, comp, pl.ds(me * (own // 8), own // 8)]
                return block.reshape(own, lanes)

            def fetch_all(r):
                return turned_ref[r, comp].reshape(width, lanes)

            for b, value in enumerate(derivatives(fetch_own, row, cells_z)):
                value = value.astype(BF16)
                mine.append(value)
                grad_ref[at, b, comp] = jnp.concatenate([value] * repeat, 0)
            every += [v.astype(BF16) for v in derivatives(fetch_all, row, cells_z)]
        visc_ref[...] += lax.dot_general(
            jnp.concatenate(every, 1), jnp.concatenate(mine, 1), (((1,), (1,)), ((), ())),
            preferred_element_type=F32,
        )

    at = 0
    for start, stop in interior:
        def one(step, carry, start=start, at=at):
            slopes(at + step, start + step)
            return carry

        lax.fori_loop(0, stop - start, one, 0)
        at += stop - start


def main_kernel(plan, own, chunk, idx_ref, full_ref, turned_ref, grad_ref, visc_ref,
                send_ref, keep_ref, *bufs):
    interior = [r for start, stop in plan[1] for r in range(start, stop)]
    _, comps, lanes, width = full_ref.shape
    halves, block_rows = send_ref.shape[:2]
    peers = 2 * halves
    i_block = width // peers
    i_part = i_block // CHUNKS
    tile = grad_ref.shape[3]
    joint = tile // own
    me = idx_ref[1]
    depth = comps * lanes
    dests = max(1, min(halves, GROUP // i_part))

    def group(low, flip):
        def source(i):
            dest = me ^ (flip + 2 * (low + i // i_part))
            row = dest * i_block + chunk * i_part
            if i_part % 8 == 0:
                return row // 8 + (i % i_part) // 8, (i % i_part) % 8
            return row // 8, (chunk * i_part) % 8 + i % i_part

        total = None
        for first in range(0, len(interior), K_ROWS):
            buf = bufs[(first // K_ROWS) % len(bufs)]
            count = min(K_ROWS, len(interior) - first)
            for x in range(first, first + count):
                for lane in range(0, lanes, 128):
                    cut = slice(lane, lane + 128)
                    grads = [[grad_ref[x, b, a, :, cut] for a in range(comps)] for b in range(comps)]
                    for i in range(0, dests * i_part, joint):
                        phis = []
                        for a in range(comps):
                            parts = []
                            for j in range(joint):
                                lead, sub = source(i + j)
                                line = turned_ref[interior[x], a, lead, sub:sub + 1, cut]
                                parts.append(jnp.broadcast_to(line, (own if joint > 1 else 16, 128)))
                            wide = jnp.concatenate(parts, 0).astype(BF16) if joint > 1 else parts[0].astype(BF16)
                            phis.append(jnp.concatenate([wide] * (tile // wide.shape[0]), 0))
                        for b in range(comps):
                            pair = phis[0] * grads[b][0]
                            for a in range(1, comps):
                                pair = pair + phis[a] * grads[b][a]
                            column = (x - first) * depth + b * lanes + lane
                            buf[i * own:i * own + tile, column:column + 128] = pair
            right = full_ref[interior[first]:interior[first] + count].reshape(count * depth, width)
            term = jnp.dot(buf[:, :count * depth], right, preferred_element_type=F32)
            total = term if total is None else total + term
        return total.reshape(dests, i_part * own, width)

    def send_step(step, carry):
        low = step * dests
        send_ref[pl.ds(low, dests), :i_part * own] = group(low, 1).astype(BF16)
        return carry

    def keep_step(step, carry):
        low = step * dests
        keep_ref[pl.ds(low, dests), :i_part * own] = group(low, 0)
        return carry

    lax.fori_loop(0, halves // dests, send_step, 0)
    lax.fori_loop(0, halves // dests, keep_step, 0)
    if block_rows > i_part * own:
        for low in range(halves):
            for flip, ref in ((1, send_ref), (0, keep_ref)):
                dest = me ^ (flip + 2 * low)
                rows = visc_ref[pl.ds(pl.multiple_of(dest * i_block, i_block), i_block), :]
                rows = jnp.concatenate([rows, jnp.zeros((i_block, width - own), F32)], 1)
                fill = block_rows - i_part * own - i_block
                if fill:
                    rows = jnp.concatenate([rows, jnp.zeros((fill, width), F32)], 0)
                ref[low, i_part * own:] = rows.astype(ref.dtype)


def prepare(plan, masks, cells_z, idx, sources, own):
    copies, interior, _ = plan
    rows = max(at + stop - start for _, start, stop, at in copies)
    count = sum(stop - start for start, stop in interior)
    _, comps, part, width = sources[0].shape
    lanes = part * len(masks)
    tile = max(own, 16)
    return pl.pallas_call(
        functools.partial(prepare_kernel, plan, masks, cells_z, tile // own),
        out_shape=(
            jax.ShapeDtypeStruct((rows, comps, lanes, width), BF16),
            jax.ShapeDtypeStruct((rows, comps, width // 8, 8, lanes), F32),
            jax.ShapeDtypeStruct((count, comps, comps, tile, lanes), BF16),
            jax.ShapeDtypeStruct((width, own), F32),
        ),
        in_specs=[SMEM] + [VMEM] * len(sources),
        out_specs=(VMEM,) * 4,
        compiler_params=pltpu.CompilerParams(vmem_limit_bytes=48 * 2**20),
        name="prepare",
    )(idx, *sources)


def project(plan, chunk, idx, state, own, peers):
    full, turned, grad, visc = state
    _, comps, lanes, width = full.shape
    halves, i_block = peers // 2, width // peers
    i_part = i_block // CHUNKS
    rows = i_part * own + (max(16, i_block) if chunk == CHUNKS - 1 else 0)
    dests = max(1, min(halves, GROUP // i_part))
    buf = pltpu.VMEM((dests * i_part * own, K_ROWS * comps * lanes), BF16)
    flops = 2 * halves * 2 * i_part * own * grad.shape[0] * comps * lanes * width
    return pl.pallas_call(
        functools.partial(main_kernel, plan, own, chunk),
        out_shape=(
            jax.ShapeDtypeStruct((halves, rows, width), BF16),
            jax.ShapeDtypeStruct((halves, rows, width), F32),
        ),
        in_specs=[SMEM] + [VMEM] * 4,
        out_specs=(VMEM,) * 2,
        scratch_shapes=[buf] * 2,
        compiler_params=pltpu.CompilerParams(vmem_limit_bytes=48 * 2**20),
        cost_estimate=pl.CostEstimate(flops=4 * flops, bytes_accessed=4 * 2**20, transcendentals=0),
        name="project",
    )(idx, full, turned, grad, visc)


def body(modes):
    cells_x, cells_y, cells_z, comps, width = modes.shape
    peers_x, peers_y = lax.axis_size("gx"), lax.axis_size("gy")
    total_points = cells_x * cells_y * cells_z * peers_x * peers_y
    own = width // peers_y
    i_block = width // peers_x
    i_part = i_block // CHUNKS
    idx = jnp.stack([lax.axis_index("gy"), lax.axis_index("gx")]).astype(jnp.int32)
    block = modes.transpose(0, 3, 1, 2, 4).reshape(cells_x, comps, cells_y * cells_z, width)
    up = [(i, (i + 1) % peers_x) for i in range(peers_x)]
    down = [(j, i) for i, j in up]
    before = lax.ppermute(block[-2:], "gx", up)
    after = lax.ppermute(block[:2], "gx", down)
    padded = jnp.concatenate([before, block, after], 0)
    pieces, masks = gathered(padded, "gy")
    plan = (((0, 0, cells_x + 4, 0),), ((2, cells_x + 2),), 1)
    state = prepare(plan, masks, cells_z, idx, pieces, own)
    finals = []
    for chunk in range(CHUNKS):
        send, keep = project(plan, chunk, idx, state, own, peers_x)
        got = swap(send, "gx", 1)
        sums = keep + got.astype(F32)
        final = sums[0]
        for q in range(1, peers_x // 2):
            final = final + swap(sums[q].astype(BF16), "gx", 2 * q).astype(F32)
        finals.append(final)
    convective = jnp.concatenate(
        [f[:i_part * own].reshape(i_part, own, width) for f in finals], 0
    ) * (-1.0 / math.sqrt(total_points))
    viscous = finals[-1][i_part * own:i_part * own + i_block, :own] * (-1.0 / total_points)
    return (convective, viscous)


def solution(mesh):
    in_specs = (P("gx", "gy", None, None, None),)
    out_specs = (P("gx", "gy", None), P("gx", "gy"))
    return jax.shard_map(body, mesh=mesh, in_specs=in_specs, out_specs=out_specs, check_vma=False)
```

time: 450 us -> 93.7 us (0.21)
  waiting for transfers between devices: 209 us -> 25.9 us
  local copies, waits for them, and re-layouts: 86.7 us -> 2.28 us
  loops' own time: 54 us -> 0 us
  other arithmetic: 55.4 us -> 1.68 us
  Pallas kernels: 0 us -> 45.9 us
  matrix products: 20.6 us -> 0 us
  between operations: 13.9 us -> 0.75 us
  starting transfers between devices: 8.08 us -> 16.9 us
    reduce_scatter x3 -> x0, waiting for transfers between devices: 141 us -> none  [the longest x1 72.1 us: body(): lax.psum_scatter(block_terms(width // lax.axis_size('gy') * lax.axis_size...]
    unnamed x5 -> x0, waiting for transfers between devices: 65.3 us -> none
    another operation x1 -> x0, loops' own time: 54 us -> none  [block_terms(): return lax.map(one_block, starts_list).reshape(count, width, width)]
    pallas_call x0 -> x3, Pallas kernels: none -> 45.9 us  [the longest x2 32.3 us: project(): pl.pallas_call(functools.partial(main_kernel, plan, own, chunk), out_shap...]
    dynamic_update_slice x32 -> x0, local copies, waits for them, and re-layouts: 29.5 us -> none  [block_terms(): return lax.map(one_block, starts_list).reshape(count, width, width)]
    convert_element_type x65 -> x0, other arithmetic: 29.1 us -> none  [the longest x32 26.1 us: pair_second(): rows[:, :, None].astype(jnp.float32)]
    convert_element_type x32 -> x2, local copies, waits for them, and re-layouts: 28.8 us -> 0.03 us  [body(): final = final + swap(sums[q].astype(BF16), 'gx', 2 * q).astype(F32)]
    reduce_sum x32 -> x0, other arithmetic: 23.8 us -> none  [pair_second(): return jnp.sum(product, axis=0).astype(jnp.bfloat16)]
  transfers between devices with their start and end apart: 8 -> 13, of which waited for: 5 -> 8; matrix products, arithmetic and copies ran while one was open for 35% -> 2% of each run, Pallas kernels for 0% -> 17%
where the time goes in v1:
time: 93.7 us; the launch traced here: 93.4 us
  Pallas kernels  45.9 us (49%)
  waiting for transfers between devices  25.9 us (28%)
  starting transfers between devices  16.9 us (18%)
  local copies, waits for them, and re-layouts  2.28 us (2%)
  other arithmetic  1.68 us (2%)
    pallas_call x2, Pallas kernels, project(): pl.pallas_call(functools.partial(main_kernel, plan, own, chunk), out_shap...  32.3 us
    ppermute x11, waiting for transfers between devices, swap(): lax.ppermute(x, axis, [(i, i ^ mask) for i in range(lax.axis_size(axis))])  20.4 us
    pallas_call x1, Pallas kernels, prepare(): pl.pallas_call(functools.partial(prepare_kernel, plan, masks, cells_z, ti...  13.6 us
    ppermute x11, starting transfers between devices, swap(): lax.ppermute(x, axis, [(i, i ^ mask) for i in range(lax.axis_size(axis))])  10.8 us
    ppermute x1, starting transfers between devices, body(): after = lax.ppermute(block[:2], 'gx', down)  6.06 us
    ppermute x1, waiting for transfers between devices, body(): before = lax.ppermute(block[-2:], 'gx', up)  5.13 us
  transfers between devices with their start and end apart: 13, of which 8 were waited for; matrix products, arithmetic and copies ran while one was open for 2% of the time, Pallas kernels for 17%

profile of v1, /device:TPU:0, one launch (start us, length us, event | category | flops | bytes accessed | tf_op | source)
XLA Modules:
  0.0 93.4 jit_solution(17767732258854416658)
XLA Ops:
  0.6 0.9 fusion.8
  1.6 6.1 %collective-permute-start.1 = (bf16[2,3,32,128]{3,2,1,0:T(8,128)(2,1)S(1)}, bf16[2,3,32,128]{3,2,1,0:T(8,128)(2,1)S(1)}, u32[]{:S(2)}, u32[]{:S(2)}) collective-permute-start(bf16[2,3,32,128]{3,2,1,0:T(8,128)(2,1)S(1)} %bitcast.41), channel_id=1, source_target_pairs={{4,0},{8,4},{12,8},{16,12},{20,16},{24,20},{28,24},{0,28},{5,1},{9... | collective-permute-start | bytes 147464 | tf_op jit(solution)/shard_map/ppermute | solution.py:242
  7.7 1.3 %copy.4 = bf16[16,3,16,2,128]{4,3,2,1,0:T(2,128)(2,1)S(1)} copy(bf16[16,3,16,2,128]{4,3,1,2,0:T(2,128)(2,1)} %bitcast.38) | data formatting | bytes 786432 | tf_op jit(solution)/shard_map/transpose | solution.py:238
  9.0 0.4 collective-permute-done.1
  9.4 5.1 %collective-permute-done = bf16[2,3,32,128]{3,2,1,0:T(8,128)(2,1)S(1)} collective-permute-done((bf16[2,3,32,128]{3,2,1,0:T(8,128)(2,1)S(1)}, bf16[2,3,32,128]{3,2,1,0:T(8,128)(2,1)S(1)}, u32[]{:S(2)}, u32[]{:S(2)}) %collective-permute-start) | collective-permute-done | bytes 49184 | tf_op jit(solution)/shard_map/ppermute | solution.py:241
  14.6 1.6 %collective-permute-start.2 = (bf16[20,3,32,128]{3,2,1,0:T(8,128)(2,1)S(1)}, bf16[20,3,32,128]{3,2,1,0:T(8,128)(2,1)S(1)}, u32[]{:S(2)}, u32[]{:S(2)}) collective-permute-start(bf16[20,3,32,128]{3,2,1,0:T(8,128)(2,1)S(1)} %pad_maximum_fusion.refs_0_), channel_id=1, source_target_pairs={{0,2},{1,3},{2,0},{3,1},{4,6},{5,7},{6,4},{7,5},{8,10},{9,11},{10,... | collective-permute-start | bytes 1474568 | tf_op jit(solution)/shard_map/ppermute | solution.py:20
  16.1 10.0 %collective-permute-done.2.refs_1_ = bf16[20,3,32,128]{3,2,1,0:T(8,128)(2,1)S(1)} collective-permute-done((bf16[20,3,32,128]{3,2,1,0:T(8,128)(2,1)S(1)}, bf16[20,3,32,128]{3,2,1,0:T(8,128)(2,1)S(1)}, u32[]{:S(2)}, u32[]{:S(2)}) %collective-permute-start.2) | collective-permute-done | bytes 491552 | tf_op jit(solution)/shard_map/ppermute | solution.py:20
  26.2 0.1 pad_add_fusion.idx_ref
  26.3 1.8 %collective-permute-done.4.refs_3_ = bf16[20,3,32,128]{3,2,1,0:T(8,128)(2,1)S(1)} collective-permute-done((bf16[20,3,32,128]{3,2,1,0:T(8,128)(2,1)S(1)}, bf16[20,3,32,128]{3,2,1,0:T(8,128)(2,1)S(1)}, u32[]{:S(2)}, u32[]{:S(2)}) %collective-permute-start.4) | collective-permute-done | bytes 491552 | tf_op jit(solution)/shard_map/ppermute | solution.py:20
  28.0 13.6 %prepare.1 = (bf16[20,3,128,128]{3,2,1,0:T(8,128)(2,1)S(1)}, f32[20,3,16,8,128]{4,3,2,1,0:T(8,128)}, bf16[16,3,3,32,128]{4,3,2,1,0:T(8,128)(2,1)S(1)}, f32[128,32]{1,0:T(8,128)S(1)}) custom-call(s32[2]{0:T(128)S(1)} %pad_add_fusion.idx_ref, bf16[20,3,32,128]{3,2,1,0:T(8,128)(2,1)S(1)} %pad_maximum_fusion.refs_0_, ...), custom_call_target="tpu_custom_call" | custom-call | tf_op jit(solution)/shard_map/prepare/pallas_call | solution.py:191
  41.6 16.1 %project.2 = (bf16[4,256,128]{2,1,0:T(8,128)(2,1)S(1)}, f32[4,256,128]{2,1,0:T(8,128)S(1)}) custom-call(s32[2]{0:T(128)S(1)} %pad_add_fusion.idx_ref, bf16[20,3,128,128]{3,2,1,0:T(8,128)(2,1)S(1)} %get-tuple-element.10.full_ref, f32[20,3,16,8,128]{4,3,2,1,0:T(8,128)} %get-tuple-element.11.turned_ref, ...), custom_call_target="tpu_custom_call" | custom-call | flops 12884901888 | bytes 4194304 | tf_op jit(solution)/shard_map/project/pallas_call | solution.py:215
  57.8 16.2 %project.3 = (bf16[4,272,128]{2,1,0:T(8,128)(2,1)S(1)}, f32[4,272,128]{2,1,0:T(8,128)S(1)}) custom-call(s32[2]{0:T(128)S(1)} %pad_add_fusion.idx_ref, bf16[20,3,128,128]{3,2,1,0:T(8,128)(2,1)S(1)} %get-tuple-element.10.full_ref, f32[20,3,16,8,128]{4,3,2,1,0:T(8,128)} %get-tuple-element.11.turned_ref, ...), custom_call_target="tpu_custom_call" | custom-call | flops 12884901888 | bytes 4194304 | tf_op jit(solution)/shard_map/project/pallas_call | solution.py:215
  74.0 2.1 %collective-permute-start.9 = (bf16[4,272,128]{2,1,0:T(8,128)(2,1)S(1)}, bf16[4,272,128]{2,1,0:T(8,128)(2,1)S(1)}, u32[]{:S(2)}, u32[]{:S(2)}) collective-permute-start(bf16[4,272,128]{2,1,0:T(8,128)(2,1)S(1)} %get-tuple-element.17), channel_id=1, source_target_pairs={{0,4},{4,0},{8,12},{12,8},{16,20},{20,16},{24,28},{28,24},{1,5},{5... | collective-permute-start | bytes 835592 | tf_op jit(solution)/shard_map/ppermute | solution.py:20
  76.1 0.1 fusion.6
  76.4 3.4 %collective-permute-start.7 = (bf16[256,128]{1,0:T(8,128)(2,1)S(1)}, bf16[256,128]{1,0:T(8,128)(2,1)S(1)}, u32[]{:S(2)}, u32[]{:S(2)}) collective-permute-start(bf16[256,128]{1,0:T(8,128)(2,1)S(1)} %get-tuple-element.29), channel_id=1, source_target_pairs={{0,16},{4,20},{8,24},{12,28},{16,0},{20,4},{24,8},{28,12},{1,17},{... | collective-permute-start | bytes 196616 | tf_op jit(solution)/shard_map/ppermute | solution.py:20
  79.8 3.0 %collective-permute-done.9 = bf16[4,272,128]{2,1,0:T(8,128)(2,1)S(1)} collective-permute-done((bf16[4,272,128]{2,1,0:T(8,128)(2,1)S(1)}, bf16[4,272,128]{2,1,0:T(8,128)(2,1)S(1)}, u32[]{:S(2)}, u32[]{:S(2)}) %collective-permute-start.9) | collective-permute-done | bytes 278560 | tf_op jit(solution)/shard_map/ppermute | solution.py:20
  82.8 0.1 fusion.7
  83.0 0.5 collective-permute-start.12
  83.5 2.9 %collective-permute-start.11 = (bf16[272,128]{1,0:T(8,128)(2,1)S(1)}, bf16[272,128]{1,0:T(8,128)(2,1)S(1)}, u32[]{:S(2)}, u32[]{:S(2)}) collective-permute-start(bf16[272,128]{1,0:T(8,128)(2,1)S(1)} %get-tuple-element.26), channel_id=1, source_target_pairs={{0,16},{4,20},{8,24},{12,28},{16,0},{20,4},{24,8},{28,12},{1,17},{... | collective-permute-start | bytes 208904 | tf_op jit(solution)/shard_map/ppermute | solution.py:20
  86.5 1.6 %collective-permute-done.10 = bf16[272,128]{1,0:T(8,128)(2,1)S(1)} collective-permute-done((bf16[272,128]{1,0:T(8,128)(2,1)S(1)}, bf16[272,128]{1,0:T(8,128)(2,1)S(1)}, u32[]{:S(2)}, u32[]{:S(2)}) %collective-permute-start.10) | collective-permute-done | bytes 69664 | tf_op jit(solution)/shard_map/ppermute | solution.py:20
  88.1 1.1 %collective-permute-done.12 = bf16[272,128]{1,0:T(8,128)(2,1)S(1)} collective-permute-done((bf16[272,128]{1,0:T(8,128)(2,1)S(1)}, bf16[272,128]{1,0:T(8,128)(2,1)S(1)}, u32[]{:S(2)}, u32[]{:S(2)}) %collective-permute-start.12) | collective-permute-done | bytes 69664 | tf_op jit(solution)/shard_map/ppermute | solution.py:20
  89.2 2.9 %collective-permute-done.11 = bf16[272,128]{1,0:T(8,128)(2,1)S(1)} collective-permute-done((bf16[272,128]{1,0:T(8,128)(2,1)S(1)}, bf16[272,128]{1,0:T(8,128)(2,1)S(1)}, u32[]{:S(2)}, u32[]{:S(2)}) %collective-permute-start.11) | collective-permute-done | bytes 69664 | tf_op jit(solution)/shard_map/ppermute | solution.py:20
  92.1 0.6 slice_multiply_fusion
  92.7 0.7 maximum_multiply_fusion
  (20 shorter events, 0.6 us)
Async XLA Ops:
  1.6 7.8 %collective-permute-start.1 = (bf16[2,3,32,128]{3,2,1,0:T(8,128)(2,1)S(1)}, bf16[2,3,32,128]{3,2,1,0:T(8,128)(2,1)S(1)}, u32[]{:S(2)}, u32[]{:S(2)}) collective-permute-start(bf16[2,3,32,128]{3,2,1,0:T(8,128)(2,1)S(1)} %bitcast.41), channel_id=1, source_target_pairs={{4,0},{8,4},{12,8},{16,12},{20,16},{24,20},{28,24},{0,28},{5,1},{9... | collective-permute-start | bytes 147464 | tf_op jit(solution)/shard_map/ppermute | solution.py:242
  7.7 6.8 %collective-permute-start = (bf16[2,3,32,128]{3,2,1,0:T(8,128)(2,1)S(1)}, bf16[2,3,32,128]{3,2,1,0:T(8,128)(2,1)S(1)}, u32[]{:S(2)}, u32[]{:S(2)}) collective-permute-start(bf16[2,3,32,128]{3,2,1,0:T(8,128)(2,1)S(1)} %bitcast.42), channel_id=1, source_target_pairs={{0,4},{4,8},{8,12},{12,16},{16,20},{20,24},{24,28},{28,0},{1,5},{5... | collective-permute-start | bytes 147464 | tf_op jit(solution)/shard_map/ppermute | solution.py:241
  14.6 11.6 %collective-permute-start.2 = (bf16[20,3,32,128]{3,2,1,0:T(8,128)(2,1)S(1)}, bf16[20,3,32,128]{3,2,1,0:T(8,128)(2,1)S(1)}, u32[]{:S(2)}, u32[]{:S(2)}) collective-permute-start(bf16[20,3,32,128]{3,2,1,0:T(8,128)(2,1)S(1)} %pad_maximum_fusion.refs_0_), channel_id=1, source_target_pairs={{0,2},{1,3},{2,0},{3,1},{4,6},{5,7},{6,4},{7,5},{8,10},{9,11},{10,... | collective-permute-start | bytes 1474568 | tf_op jit(solution)/shard_map/ppermute | solution.py:20
  16.1 10.1 %collective-permute-start.3 = (bf16[20,3,32,128]{3,2,1,0:T(8,128)(2,1)S(1)}, bf16[20,3,32,128]{3,2,1,0:T(8,128)(2,1)S(1)}, u32[]{:S(2)}, u32[]{:S(2)}) collective-permute-start(bf16[20,3,32,128]{3,2,1,0:T(8,128)(2,1)S(1)} %pad_maximum_fusion.refs_0_), channel_id=1, source_target_pairs={{0,1},{1,0},{2,3},{3,2},{4,5},{5,4},{6,7},{7,6},{8,9},{9,8},{10,11... | collective-permute-start | bytes 1474568 | tf_op jit(solution)/shard_map/ppermute | solution.py:20
  26.2 1.9 %collective-permute-start.4 = (bf16[20,3,32,128]{3,2,1,0:T(8,128)(2,1)S(1)}, bf16[20,3,32,128]{3,2,1,0:T(8,128)(2,1)S(1)}, u32[]{:S(2)}, u32[]{:S(2)}) collective-permute-start(bf16[20,3,32,128]{3,2,1,0:T(8,128)(2,1)S(1)} %collective-permute-done.2.refs_1_), channel_id=1, source_target_pairs={{0,1},{1,0},{2,3},{3,2},{4,5},{5,4},{6,7},{7,6},{8,9},{9,8},{10,11... | collective-permute-start | bytes 1474568 | tf_op jit(solution)/shard_map/ppermute | solution.py:20
  57.8 18.3 %collective-permute-start.5 = (bf16[4,256,128]{2,1,0:T(8,128)(2,1)S(1)}, bf16[4,256,128]{2,1,0:T(8,128)(2,1)S(1)}, u32[]{:S(2)}, u32[]{:S(2)}) collective-permute-start(bf16[4,256,128]{2,1,0:T(8,128)(2,1)S(1)} %get-tuple-element.15), channel_id=1, source_target_pairs={{0,4},{4,0},{8,12},{12,8},{16,20},{20,16},{24,28},{28,24},{1,5},{5... | collective-permute-start | bytes 786440 | tf_op jit(solution)/shard_map/ppermute | solution.py:20
  74.0 8.8 %collective-permute-start.9 = (bf16[4,272,128]{2,1,0:T(8,128)(2,1)S(1)}, bf16[4,272,128]{2,1,0:T(8,128)(2,1)S(1)}, u32[]{:S(2)}, u32[]{:S(2)}) collective-permute-start(bf16[4,272,128]{2,1,0:T(8,128)(2,1)S(1)} %get-tuple-element.17), channel_id=1, source_target_pairs={{0,4},{4,0},{8,12},{12,8},{16,20},{20,16},{24,28},{28,24},{1,5},{5... | collective-permute-start | bytes 835592 | tf_op jit(solution)/shard_map/ppermute | solution.py:20
  76.2 7.3 %collective-permute-start.6 = (bf16[256,128]{1,0:T(8,128)(2,1)S(1)}, bf16[256,128]{1,0:T(8,128)(2,1)S(1)}, u32[]{:S(2)}, u32[]{:S(2)}) collective-permute-start(bf16[256,128]{1,0:T(8,128)(2,1)S(1)} %get-tuple-element.27), channel_id=1, source_target_pairs={{0,8},{4,12},{8,0},{12,4},{16,24},{20,28},{24,16},{28,20},{1,9},{5... | collective-permute-start | bytes 196616 | tf_op jit(solution)/shard_map/ppermute | solution.py:20
  76.3 10.2 %collective-permute-start.8 = (bf16[256,128]{1,0:T(8,128)(2,1)S(1)}, bf16[256,128]{1,0:T(8,128)(2,1)S(1)}, u32[]{:S(2)}, u32[]{:S(2)}) collective-permute-start(bf16[256,128]{1,0:T(8,128)(2,1)S(1)} %get-tuple-element.28), channel_id=1, source_target_pairs={{0,24},{4,28},{8,16},{12,20},{16,8},{20,12},{24,0},{28,4},{1,25},{... | collective-permute-start | bytes 196616 | tf_op jit(solution)/shard_map/ppermute | solution.py:20
  76.4 10.1 %collective-permute-start.7 = (bf16[256,128]{1,0:T(8,128)(2,1)S(1)}, bf16[256,128]{1,0:T(8,128)(2,1)S(1)}, u32[]{:S(2)}, u32[]{:S(2)}) collective-permute-start(bf16[256,128]{1,0:T(8,128)(2,1)S(1)} %get-tuple-element.29), channel_id=1, source_target_pairs={{0,16},{4,20},{8,24},{12,28},{16,0},{20,4},{24,8},{28,12},{1,17},{... | collective-permute-start | bytes 196616 | tf_op jit(solution)/shard_map/ppermute | solution.py:20
  82.9 5.2 %collective-permute-start.10 = (bf16[272,128]{1,0:T(8,128)(2,1)S(1)}, bf16[272,128]{1,0:T(8,128)(2,1)S(1)}, u32[]{:S(2)}, u32[]{:S(2)}) collective-permute-start(bf16[272,128]{1,0:T(8,128)(2,1)S(1)} %get-tuple-element.24), channel_id=1, source_target_pairs={{0,8},{4,12},{8,0},{12,4},{16,24},{20,28},{24,16},{28,20},{1,9},{5... | collective-permute-start | bytes 208904 | tf_op jit(solution)/shard_map/ppermute | solution.py:20
  83.0 6.2 %collective-permute-start.12 = (bf16[272,128]{1,0:T(8,128)(2,1)S(1)}, bf16[272,128]{1,0:T(8,128)(2,1)S(1)}, u32[]{:S(2)}, u32[]{:S(2)}) collective-permute-start(bf16[272,128]{1,0:T(8,128)(2,1)S(1)} %get-tuple-element.25), channel_id=1, source_target_pairs={{0,24},{4,28},{8,16},{12,20},{16,8},{20,12},{24,0},{28,4},{1,25},{... | collective-permute-start | bytes 208904 | tf_op jit(solution)/shard_map/ppermute | solution.py:20
  83.5 8.5 %collective-permute-start.11 = (bf16[272,128]{1,0:T(8,128)(2,1)S(1)}, bf16[272,128]{1,0:T(8,128)(2,1)S(1)}, u32[]{:S(2)}, u32[]{:S(2)}) collective-permute-start(bf16[272,128]{1,0:T(8,128)(2,1)S(1)} %get-tuple-element.26), channel_id=1, source_target_pairs={{0,16},{4,20},{8,24},{12,28},{16,0},{20,4},{24,8},{28,12},{1,17},{... | collective-permute-start | bytes 208904 | tf_op jit(solution)/shard_map/ppermute | solution.py:20

commit v2 on v1

v2 whole, which is shorter than its diff:
```python
import functools
import math

import jax
import jax.numpy as jnp
from jax import lax
from jax.experimental import pallas as pl
from jax.experimental.pallas import tpu as pltpu
from jax.sharding import PartitionSpec as P

BF16, F32 = jnp.bfloat16, jnp.float32
VMEM = pl.BlockSpec(memory_space=pltpu.VMEM)
SMEM = pl.BlockSpec(memory_space=pltpu.SMEM)
CHUNKS = 2
GROUP = 16
K_ROWS = 4


def swap(x, axis, mask):
    return lax.ppermute(x, axis, [(i, i ^ mask) for i in range(lax.axis_size(axis))])


def gathered(x, axis):
    pieces, mask = [x], lax.axis_size(axis) // 2
    masks = [0]
    while mask:
        pieces += [swap(piece, axis, mask) for piece in pieces]
        masks += [m ^ mask for m in masks]
        mask //= 2
    return pieces, masks


def y_and_z_weights(lanes, cells_z):
    q = lax.broadcasted_iota(jnp.int32, (lanes, lanes), 0)
    p = lax.broadcasted_iota(jnp.int32, (lanes, lanes), 1)
    apart = q - p
    around = jnp.where(apart < 0, apart + lanes, apart)
    same = lax.div(q, cells_z) == lax.div(p, cells_z)
    weights_y = jnp.zeros((lanes, lanes), F32)
    weights_z = jnp.zeros((lanes, lanes), F32)
    for step, weight in ((1, 8.0), (-1, -8.0), (2, -1.0), (-2, 1.0)):
        weights_y = weights_y + jnp.where(around == (step * cells_z) % lanes, weight, 0.0)
        weights_z = weights_z + jnp.where(same & (apart == step), weight, 0.0)
    return jnp.concatenate([weights_y, weights_z], 1).astype(BF16)


def prepare_kernel(plan, masks, cells_z, repeat, idx_ref, *refs):
    copies, interior, count_sources = plan
    pieces = len(masks)
    sources = [refs[s * pieces:(s + 1) * pieces] for s in range(count_sources)]
    full_ref, turned_ref, first_ref, grad_ref, visc_ref, slope_ref, every_ref, mine_ref = refs[count_sources * pieces:]
    rows, comps, lanes, width = full_ref.shape
    part = lanes // pieces
    me = idx_ref[0]
    own = width // pieces
    for q, mask in enumerate(masks):
        slot = pl.multiple_of((me ^ mask) * part, part)
        for source, start, stop, at in copies:
            full_ref[at:at + stop - start, :, pl.ds(slot, part), :] = sources[source][q][start:stop]

    def turn(row, carry):
        for comp in range(comps):
            flat = full_ref[row, comp].astype(F32).T
            turned_ref[row, comp] = flat.reshape(width // 8, 8, lanes)
        return carry

    lax.fori_loop(0, rows, turn, 0, unroll=4)
    weights = y_and_z_weights(lanes, cells_z)

    def slopes(at, slot, row):
        mine, every = [], []
        for comp in range(comps):
            def line(step):
                return turned_ref[row + step, comp].reshape(width, lanes)

            along_x = (8.0 * (line(1) - line(-1)) - (line(2) - line(-2))) * (1.0 / 12.0)
            others = jnp.dot(line(0).astype(BF16), weights, preferred_element_type=F32) * (1.0 / 12.0)
            for b, value in enumerate((along_x, others[:, :lanes], others[:, lanes:])):
                slope_ref[b, comp] = value.reshape(width // 8, 8, lanes)
                every.append(value.astype(BF16))
        for b in range(comps):
            for comp in range(comps):
                block = slope_ref[b, comp, pl.ds(me * (own // 8), own // 8)].reshape(own, lanes).astype(BF16)
                mine.append((b, comp, block))
                tiled = jnp.concatenate([block] * repeat, 0)
                if b == 0:
                    first_ref[at, comp] = tiled.astype(F32)
                else:
                    grad_ref[at, b - 1, comp] = tiled
        mine = [m[2] for m in sorted(mine, key=lambda m: (m[1], m[0]))]
        column = pl.ds(pl.multiple_of(slot * (comps * comps * lanes), lanes), comps * comps * lanes)
        every_ref[:, column] = jnp.concatenate(every, 1)
        mine_ref[:, column] = jnp.concatenate(mine, 1)

    batch = mine_ref.shape[1] // (comps * comps * lanes)
    steps = [(row, min(row + batch, stop)) for start, stop in interior for row in range(start, stop, batch)]
    at = 0
    for start, stop in steps:
        def one(step, carry, start=start, at=at):
            slopes(at + step, step, start + step)
            return carry

        lax.fori_loop(0, stop - start, one, 0, unroll=4)
        used = (stop - start) * comps * comps * lanes
        term = lax.dot_general(
            every_ref[:, :used], mine_ref[:, :used], (((1,), (1,)), ((), ())), preferred_element_type=F32
        )
        visc_ref[...] = term if at == 0 else visc_ref[...] + term
        at += stop - start


def main_kernel(plan, own, chunk, idx_ref, full_ref, turned_ref, first_ref, grad_ref, visc_ref,
                send_ref, keep_ref):
    interior = [r for start, stop in plan[1] for r in range(start, stop)]
    _, comps, lanes, width = full_ref.shape
    halves, block_rows = send_ref.shape[:2]
    peers = 2 * halves
    i_block = width // peers
    i_part = i_block // CHUNKS
    tile = grad_ref.shape[3]
    joint = tile // own
    me = idx_ref[1]
    depth = comps * lanes
    dests = max(1, min(halves, GROUP // i_part))

    def group(low, flip):
        def source(i):
            dest = me ^ (flip + 2 * (low + i // i_part))
            row = dest * i_block + chunk * i_part
            if i_part % 8 == 0:
                return row // 8 + (i % i_part) // 8, (i % i_part) % 8
            return row // 8, (chunk * i_part) % 8 + i % i_part

        def pairs(x, i):
            pieces = []
            for lane in range(0, lanes, 128):
                cut = slice(lane, lane + 128)
                wide, narrow = [], []
                for a in range(comps):
                    parts = []
                    for j in range(joint):
                        lead, sub = source(i + j)
                        line = turned_ref[interior[x], a, lead, sub:sub + 1, cut]
                        parts.append(jnp.broadcast_to(line, (own, 128)))
                    wide.append(jnp.concatenate(parts, 0))
                    half = wide[-1][:16].astype(BF16)
                    narrow.append(jnp.concatenate([half] * (tile // 16), 0))
                row = []
                for b in range(comps):
                    phis = wide if b == 0 else narrow
                    slope = [first_ref[x, a, :, cut] if b == 0 else grad_ref[x, b - 1, a, :, cut]
                             for a in range(comps)]
                    pair = phis[0] * slope[0]
                    for a in range(1, comps):
                        pair = pair + phis[a] * slope[a]
                    row.append(pair.astype(BF16))
                pieces.append(row)
            return [pieces[l][b] for b in range(comps) for l in range(lanes // 128)]

        total = None
        for first in range(0, len(interior), K_ROWS):
            count = min(K_ROWS, len(interior) - first)
            left = jnp.concatenate([
                jnp.concatenate([p for x in range(first, first + count) for p in pairs(x, i)], 1)
                for i in range(0, dests * i_part, joint)
            ], 0)
            right = full_ref[interior[first]:interior[first] + count].reshape(count * depth, width)
            term = jnp.dot(left, right, preferred_element_type=F32)
            total = term if total is None else total + term
        return total.reshape(dests, i_part * own, width)

    steps = halves // dests

    def step_of(step, carry):
        sends = step < steps
        low = lax.rem(step, steps) * dests
        value = group(low, jnp.where(sends, 1, 0))

        @pl.when(sends)
        def _():
            send_ref[pl.ds(low, dests), :i_part * own] = value.astype(BF16)

        @pl.when(jnp.logical_not(sends))
        def _():
            keep_ref[pl.ds(low, dests), :i_part * own] = value

        return carry

    lax.fori_loop(0, 2 * steps, step_of, 0)
    if block_rows > i_part * own:
        for low in range(halves):
            for flip, ref in ((1, send_ref), (0, keep_ref)):
                dest = me ^ (flip + 2 * low)
                rows = visc_ref[pl.ds(pl.multiple_of(dest * i_block, i_block), i_block), :]
                rows = jnp.concatenate([rows, jnp.zeros((i_block, width - own), F32)], 1)
                fill = block_rows - i_part * own - i_block
                if fill:
                    rows = jnp.concatenate([rows, jnp.zeros((fill, width), F32)], 0)
                ref[low, i_part * own:] = rows.astype(ref.dtype)


def prepare(plan, masks, cells_z, idx, sources, own):
    copies, interior, _ = plan
    rows = max(at + stop - start for _, start, stop, at in copies)
    count = sum(stop - start for start, stop in interior)
    _, comps, part, width = sources[0].shape
    lanes = part * len(masks)
    tile = max(own, 16)
    batch = max(1, min(max(stop - start for start, stop in interior), 2048 // lanes))
    return pl.pallas_call(
        functools.partial(prepare_kernel, plan, masks, cells_z, tile // own),
        out_shape=(
            jax.ShapeDtypeStruct((rows, comps, lanes, width), BF16),
            jax.ShapeDtypeStruct((rows, comps, width // 8, 8, lanes), F32),
            jax.ShapeDtypeStruct((count, comps, tile, lanes), F32),
            jax.ShapeDtypeStruct((count, comps - 1, comps, tile, lanes), BF16),
            jax.ShapeDtypeStruct((width, own), F32),
        ),
        in_specs=[SMEM] + [VMEM] * len(sources),
        out_specs=(VMEM,) * 5,
        scratch_shapes=[
            pltpu.VMEM((comps, comps, width // 8, 8, lanes), F32),
            pltpu.VMEM((width, batch * comps * comps * lanes), BF16),
            pltpu.VMEM((own, batch * comps * comps * lanes), BF16),
        ],
        compiler_params=pltpu.CompilerParams(vmem_limit_bytes=48 * 2**20),
        name="prepare",
    )(idx, *sources)


def project(plan, chunk, idx, state, own, peers):
    full, turned, first, grad, visc = state
    _, comps, lanes, width = full.shape
    halves, i_block = peers // 2, width // peers
    i_part = i_block // CHUNKS
    rows = i_part * own + (max(16, i_block) if chunk == CHUNKS - 1 else 0)
    flops = 2 * halves * 2 * i_part * own * grad.shape[0] * comps * lanes * width
    return pl.pallas_call(
        functools.partial(main_kernel, plan, own, chunk),
        out_shape=(
            jax.ShapeDtypeStruct((halves, rows, width), BF16),
            jax.ShapeDtypeStruct((halves, rows, width), F32),
        ),
        in_specs=[SMEM] + [VMEM] * 5,
        out_specs=(VMEM,) * 2,
        compiler_params=pltpu.CompilerParams(vmem_limit_bytes=48 * 2**20),
        cost_estimate=pl.CostEstimate(flops=4 * flops, bytes_accessed=4 * 2**20, transcendentals=0),
        name="project",
    )(idx, full, turned, first, grad, visc)


def body(modes):
    cells_x, cells_y, cells_z, comps, width = modes.shape
    peers_x, peers_y = lax.axis_size("gx"), lax.axis_size("gy")
    total_points = cells_x * cells_y * cells_z * peers_x * peers_y
    own = width // peers_y
    i_block = width // peers_x
    i_part = i_block // CHUNKS
    idx = jnp.stack([lax.axis_index("gy"), lax.axis_index("gx")]).astype(jnp.int32)
    block = modes.transpose(0, 3, 1, 2, 4).reshape(cells_x, comps, cells_y * cells_z, width)
    up = [(i, (i + 1) % peers_x) for i in range(peers_x)]
    down = [(j, i) for i, j in up]
    before = lax.ppermute(block[-2:], "gx", up)
    after = lax.ppermute(block[:2], "gx", down)
    padded = jnp.concatenate([before, block, after], 0)
    pieces, masks = gathered(padded, "gy")
    plan = (((0, 0, cells_x + 4, 0),), ((2, cells_x + 2),), 1)
    state = prepare(plan, masks, cells_z, idx, pieces, own)
    finals = []
    for chunk in range(CHUNKS):
        send, keep = project(plan, chunk, idx, state, own, peers_x)
        got = swap(send, "gx", 1)
        sums = keep + got.astype(F32)
        final = sums[0]
        for q in range(1, peers_x // 2):
            final = final + swap(sums[q].astype(BF16), "gx", 2 * q).astype(F32)
        finals.append(final)
    convective = jnp.concatenate(
        [f[:i_part * own].reshape(i_part, own, width) for f in finals], 0
    ) * (-1.0 / math.sqrt(total_points))
    viscous = finals[-1][i_part * own:i_part * own + i_block, :own] * (-1.0 / total_points)
    return (convective, viscous)


def solution(mesh):
    in_specs = (P("gx", "gy", None, None, None),)
    out_specs = (P("gx", "gy", None), P("gx", "gy"))
    return jax.shard_map(body, mesh=mesh, in_specs=in_specs, out_specs=out_specs, check_vma=False)
```

time: 93.7 us -> 73.9 us (0.79)
  Pallas kernels: 45.9 us -> 26.1 us
    pallas_call x2, Pallas kernels: 32.3 us -> 20.7 us  [project(): pl.pallas_call(functools.partial(main_kernel, plan, own, chunk), out_shap...]
    pallas_call x1, Pallas kernels: 13.6 us -> 5.39 us  [prepare(): pl.pallas_call(functools.partial(prepare_kernel, plan, masks, cells_z, ti...]
  transfers between devices with their start and end apart: 13 -> 13, of which waited for: 8 -> 8; matrix products, arithmetic and copies ran while one was open for 2% -> 2% of each run, Pallas kernels for 17% -> 14%
where the time goes in v2:
time: 73.9 us; the launch traced here: 73.6 us
  Pallas kernels  26.1 us (35%)
  waiting for transfers between devices  25.9 us (35%)
  starting transfers between devices  16.9 us (23%)
  local copies, waits for them, and re-layouts  2.28 us (3%)
  other arithmetic  1.68 us (2%)
  between operations  0.76 us (1%)
    pallas_call x2, Pallas kernels, project(): pl.pallas_call(functools.partial(main_kernel, plan, own, chunk), out_shap...  20.7 us
    ppermute x11, waiting for transfers between devices, swap(): lax.ppermute(x, axis, [(i, i ^ mask) for i in range(lax.axis_size(axis))])  20.4 us
    ppermute x11, starting transfers between devices, swap(): lax.ppermute(x, axis, [(i, i ^ mask) for i in range(lax.axis_size(axis))])  10.8 us
    ppermute x1, starting transfers between devices, body(): after = lax.ppermute(block[:2], 'gx', down)  6.06 us
    pallas_call x1, Pallas kernels, prepare(): pl.pallas_call(functools.partial(prepare_kernel, plan, masks, cells_z, ti...  5.39 us
    ppermute x1, waiting for transfers between devices, body(): before = lax.ppermute(block[-2:], 'gx', up)  5.13 us
  transfers between devices with their start and end apart: 13, of which 8 were waited for; matrix products, arithmetic and copies ran while one was open for 2% of the time, Pallas kernels for 14%

profile of v2, /device:TPU:0, one launch (start us, length us, event | category | flops | bytes accessed | tf_op | source)
XLA Modules:
  0.0 73.6 jit_solution(13738444403241663954)
XLA Ops:
  0.6 0.9 %fusion.8 = (bf16[2,3,16,2,128]{4,3,1,2,0:T(2,128)(2,1)S(1)}, bf16[2,3,16,2,128]{4,3,1,2,0:T(2,128)(2,1)S(1)}) fusion(bf16[16,3,16,2,128]{4,3,1,2,0:T(2,128)(2,1)} %bitcast.37), kind=kLoop, calls=%fused_computation.22 | loop fusion | bytes 196608 | tf_op jit(solution)/shard_map/slice | solution.py:263
  1.6 6.1 %collective-permute-start.1 = (bf16[2,3,32,128]{3,2,1,0:T(8,128)(2,1)S(1)}, bf16[2,3,32,128]{3,2,1,0:T(8,128)(2,1)S(1)}, u32[]{:S(2)}, u32[]{:S(2)}) collective-permute-start(bf16[2,3,32,128]{3,2,1,0:T(8,128)(2,1)S(1)} %bitcast.41), channel_id=1, source_target_pairs={{4,0},{8,4},{12,8},{16,12},{20,16},{24,20},{28,24},{0,28},{5,1},{9... | collective-permute-start | bytes 147464 | tf_op jit(solution)/shard_map/ppermute | solution.py:264
  7.7 1.3 %copy.4 = bf16[16,3,16,2,128]{4,3,2,1,0:T(2,128)(2,1)S(1)} copy(bf16[16,3,16,2,128]{4,3,1,2,0:T(2,128)(2,1)} %bitcast.38) | data formatting | bytes 786432 | tf_op jit(solution)/shard_map/transpose | solution.py:260
  9.0 0.4 collective-permute-done.1
  9.4 5.1 %collective-permute-done = bf16[2,3,32,128]{3,2,1,0:T(8,128)(2,1)S(1)} collective-permute-done((bf16[2,3,32,128]{3,2,1,0:T(8,128)(2,1)S(1)}, bf16[2,3,32,128]{3,2,1,0:T(8,128)(2,1)S(1)}, u32[]{:S(2)}, u32[]{:S(2)}) %collective-permute-start) | collective-permute-done | bytes 49184 | tf_op jit(solution)/shard_map/ppermute | solution.py:263
  14.6 1.6 %collective-permute-start.2 = (bf16[20,3,32,128]{3,2,1,0:T(8,128)(2,1)S(1)}, bf16[20,3,32,128]{3,2,1,0:T(8,128)(2,1)S(1)}, u32[]{:S(2)}, u32[]{:S(2)}) collective-permute-start(bf16[20,3,32,128]{3,2,1,0:T(8,128)(2,1)S(1)} %pad_maximum_fusion.refs_0_), channel_id=1, source_target_pairs={{0,2},{1,3},{2,0},{3,1},{4,6},{5,7},{6,4},{7,5},{8,10},{9,11},{10,... | collective-permute-start | bytes 1474568 | tf_op jit(solution)/shard_map/ppermute | solution.py:20
  16.1 10.0 %collective-permute-done.2.refs_1_ = bf16[20,3,32,128]{3,2,1,0:T(8,128)(2,1)S(1)} collective-permute-done((bf16[20,3,32,128]{3,2,1,0:T(8,128)(2,1)S(1)}, bf16[20,3,32,128]{3,2,1,0:T(8,128)(2,1)S(1)}, u32[]{:S(2)}, u32[]{:S(2)}) %collective-permute-start.2) | collective-permute-done | bytes 491552 | tf_op jit(solution)/shard_map/ppermute | solution.py:20
  26.2 0.1 pad_add_fusion.idx_ref
  26.3 1.8 %collective-permute-done.4.refs_3_ = bf16[20,3,32,128]{3,2,1,0:T(8,128)(2,1)S(1)} collective-permute-done((bf16[20,3,32,128]{3,2,1,0:T(8,128)(2,1)S(1)}, bf16[20,3,32,128]{3,2,1,0:T(8,128)(2,1)S(1)}, u32[]{:S(2)}, u32[]{:S(2)}) %collective-permute-start.4) | collective-permute-done | bytes 491552 | tf_op jit(solution)/shard_map/ppermute | solution.py:20
  28.0 5.4 %prepare.1 = (bf16[20,3,128,128]{3,2,1,0:T(8,128)(2,1)S(1)}, f32[20,3,16,8,128]{4,3,2,1,0:T(8,128)}, f32[16,3,32,128]{3,2,1,0:T(8,128)S(1)}, bf16[16,2,3,32,128]{4,3,2,1,0:T(8,128)(2,1)S(1)}, f32[128,32]{1,0:T(8,128)S(1)}) custom-call(s32[2]{0:T(128)S(1)} %pad_add_fusion.idx_ref, bf16[20,3,32,128]{3,2,1,0:T(8,128)(2,1)S(1)} %pad_maximum_fusion.refs_0_, ...), custom_call_target="tpu_custom_call" | custom-call | tf_op jit(solution)/shard_map/prepare/pallas_call | solution.py:210
  33.4 10.2 %project.2 = (bf16[4,256,128]{2,1,0:T(8,128)(2,1)S(1)}, f32[4,256,128]{2,1,0:T(8,128)S(1)}) custom-call(s32[2]{0:T(128)S(1)} %pad_add_fusion.idx_ref, bf16[20,3,128,128]{3,2,1,0:T(8,128)(2,1)S(1)} %get-tuple-element.11.full_ref, f32[20,3,16,8,128]{4,3,2,1,0:T(8,128)} %get-tuple-element.12.turned_ref, f32[16,3,32,128]{3,2,1,0:T(8,128)S(1)} %get-tuple-element.13.first_ref, ...), custom_call_target="tpu_custom_call" | custom-call | flops 12884901888 | bytes 4194304 | tf_op jit(solution)/shard_map/project/pallas_call | solution.py:238
  43.7 10.5 %project.3 = (bf16[4,272,128]{2,1,0:T(8,128)(2,1)S(1)}, f32[4,272,128]{2,1,0:T(8,128)S(1)}) custom-call(s32[2]{0:T(128)S(1)} %pad_add_fusion.idx_ref, bf16[20,3,128,128]{3,2,1,0:T(8,128)(2,1)S(1)} %get-tuple-element.11.full_ref, f32[20,3,16,8,128]{4,3,2,1,0:T(8,128)} %get-tuple-element.12.turned_ref, f32[16,3,32,128]{3,2,1,0:T(8,128)S(1)} %get-tuple-element.13.first_ref, ...), custom_call_target="tpu_custom_call" | custom-call | flops 12884901888 | bytes 4194304 | tf_op jit(solution)/shard_map/project/pallas_call | solution.py:238
  54.2 2.1 %collective-permute-start.9 = (bf16[4,272,128]{2,1,0:T(8,128)(2,1)S(1)}, bf16[4,272,128]{2,1,0:T(8,128)(2,1)S(1)}, u32[]{:S(2)}, u32[]{:S(2)}) collective-permute-start(bf16[4,272,128]{2,1,0:T(8,128)(2,1)S(1)} %get-tuple-element.19), channel_id=1, source_target_pairs={{0,4},{4,0},{8,12},{12,8},{16,20},{20,16},{24,28},{28,24},{1,5},{5... | collective-permute-start | bytes 835592 | tf_op jit(solution)/shard_map/ppermute | solution.py:20
  56.3 0.1 fusion.6
  56.6 3.4 %collective-permute-start.7 = (bf16[256,128]{1,0:T(8,128)(2,1)S(1)}, bf16[256,128]{1,0:T(8,128)(2,1)S(1)}, u32[]{:S(2)}, u32[]{:S(2)}) collective-permute-start(bf16[256,128]{1,0:T(8,128)(2,1)S(1)} %get-tuple-element.31), channel_id=1, source_target_pairs={{0,16},{4,20},{8,24},{12,28},{16,0},{20,4},{24,8},{28,12},{1,17},{... | collective-permute-start | bytes 196616 | tf_op jit(solution)/shard_map/ppermute | solution.py:20
  60.0 3.0 %collective-permute-done.9 = bf16[4,272,128]{2,1,0:T(8,128)(2,1)S(1)} collective-permute-done((bf16[4,272,128]{2,1,0:T(8,128)(2,1)S(1)}, bf16[4,272,128]{2,1,0:T(8,128)(2,1)S(1)}, u32[]{:S(2)}, u32[]{:S(2)}) %collective-permute-start.9) | collective-permute-done | bytes 278560 | tf_op jit(solution)/shard_map/ppermute | solution.py:20
  63.0 0.1 fusion.7
  63.2 0.5 collective-permute-start.12
  63.7 3.0 %collective-permute-start.11 = (bf16[272,128]{1,0:T(8,128)(2,1)S(1)}, bf16[272,128]{1,0:T(8,128)(2,1)S(1)}, u32[]{:S(2)}, u32[]{:S(2)}) collective-permute-start(bf16[272,128]{1,0:T(8,128)(2,1)S(1)} %get-tuple-element.28), channel_id=1, source_target_pairs={{0,16},{4,20},{8,24},{12,28},{16,0},{20,4},{24,8},{28,12},{1,17},{... | collective-permute-start | bytes 208904 | tf_op jit(solution)/shard_map/ppermute | solution.py:20
  66.7 1.6 %collective-permute-done.10 = bf16[272,128]{1,0:T(8,128)(2,1)S(1)} collective-permute-done((bf16[272,128]{1,0:T(8,128)(2,1)S(1)}, bf16[272,128]{1,0:T(8,128)(2,1)S(1)}, u32[]{:S(2)}, u32[]{:S(2)}) %collective-permute-start.10) | collective-permute-done | bytes 69664 | tf_op jit(solution)/shard_map/ppermute | solution.py:20
  68.3 1.1 %collective-permute-done.12 = bf16[272,128]{1,0:T(8,128)(2,1)S(1)} collective-permute-done((bf16[272,128]{1,0:T(8,128)(2,1)S(1)}, bf16[272,128]{1,0:T(8,128)(2,1)S(1)}, u32[]{:S(2)}, u32[]{:S(2)}) %collective-permute-start.12) | collective-permute-done | bytes 69664 | tf_op jit(solution)/shard_map/ppermute | solution.py:20
  69.4 2.9 %collective-permute-done.11 = bf16[272,128]{1,0:T(8,128)(2,1)S(1)} collective-permute-done((bf16[272,128]{1,0:T(8,128)(2,1)S(1)}, bf16[272,128]{1,0:T(8,128)(2,1)S(1)}, u32[]{:S(2)}, u32[]{:S(2)}) %collective-permute-start.11) | collective-permute-done | bytes 69664 | tf_op jit(solution)/shard_map/ppermute | solution.py:20
  72.3 0.6 slice_multiply_fusion
  72.9 0.7 maximum_multiply_fusion
  (20 shorter events, 0.6 us)
Async XLA Ops:
  1.6 7.8 %collective-permute-start.1 = (bf16[2,3,32,128]{3,2,1,0:T(8,128)(2,1)S(1)}, bf16[2,3,32,128]{3,2,1,0:T(8,128)(2,1)S(1)}, u32[]{:S(2)}, u32[]{:S(2)}) collective-permute-start(bf16[2,3,32,128]{3,2,1,0:T(8,128)(2,1)S(1)} %bitcast.41), channel_id=1, source_target_pairs={{4,0},{8,4},{12,8},{16,12},{20,16},{24,20},{28,24},{0,28},{5,1},{9... | collective-permute-start | bytes 147464 | tf_op jit(solution)/shard_map/ppermute | solution.py:264
  7.7 6.8 %collective-permute-start = (bf16[2,3,32,128]{3,2,1,0:T(8,128)(2,1)S(1)}, bf16[2,3,32,128]{3,2,1,0:T(8,128)(2,1)S(1)}, u32[]{:S(2)}, u32[]{:S(2)}) collective-permute-start(bf16[2,3,32,128]{3,2,1,0:T(8,128)(2,1)S(1)} %bitcast.42), channel_id=1, source_target_pairs={{0,4},{4,8},{8,12},{12,16},{16,20},{20,24},{24,28},{28,0},{1,5},{5... | collective-permute-start | bytes 147464 | tf_op jit(solution)/shard_map/ppermute | solution.py:263
  14.6 11.6 %collective-permute-start.2 = (bf16[20,3,32,128]{3,2,1,0:T(8,128)(2,1)S(1)}, bf16[20,3,32,128]{3,2,1,0:T(8,128)(2,1)S(1)}, u32[]{:S(2)}, u32[]{:S(2)}) collective-permute-start(bf16[20,3,32,128]{3,2,1,0:T(8,128)(2,1)S(1)} %pad_maximum_fusion.refs_0_), channel_id=1, source_target_pairs={{0,2},{1,3},{2,0},{3,1},{4,6},{5,7},{6,4},{7,5},{8,10},{9,11},{10,... | collective-permute-start | bytes 1474568 | tf_op jit(solution)/shard_map/ppermute | solution.py:20
  16.1 10.1 %collective-permute-start.3 = (bf16[20,3,32,128]{3,2,1,0:T(8,128)(2,1)S(1)}, bf16[20,3,32,128]{3,2,1,0:T(8,128)(2,1)S(1)}, u32[]{:S(2)}, u32[]{:S(2)}) collective-permute-start(bf16[20,3,32,128]{3,2,1,0:T(8,128)(2,1)S(1)} %pad_maximum_fusion.refs_0_), channel_id=1, source_target_pairs={{0,1},{1,0},{2,3},{3,2},{4,5},{5,4},{6,7},{7,6},{8,9},{9,8},{10,11... | collective-permute-start | bytes 1474568 | tf_op jit(solution)/shard_map/ppermute | solution.py:20
  26.2 1.9 %collective-permute-start.4 = (bf16[20,3,32,128]{3,2,1,0:T(8,128)(2,1)S(1)}, bf16[20,3,32,128]{3,2,1,0:T(8,128)(2,1)S(1)}, u32[]{:S(2)}, u32[]{:S(2)}) collective-permute-start(bf16[20,3,32,128]{3,2,1,0:T(8,128)(2,1)S(1)} %collective-permute-done.2.refs_1_), channel_id=1, source_target_pairs={{0,1},{1,0},{2,3},{3,2},{4,5},{5,4},{6,7},{7,6},{8,9},{9,8},{10,11... | collective-permute-start | bytes 1474568 | tf_op jit(solution)/shard_map/ppermute | solution.py:20
  43.6 12.7 %collective-permute-start.5 = (bf16[4,256,128]{2,1,0:T(8,128)(2,1)S(1)}, bf16[4,256,128]{2,1,0:T(8,128)(2,1)S(1)}, u32[]{:S(2)}, u32[]{:S(2)}) collective-permute-start(bf16[4,256,128]{2,1,0:T(8,128)(2,1)S(1)} %get-tuple-element.17), channel_id=1, source_target_pairs={{0,4},{4,0},{8,12},{12,8},{16,20},{20,16},{24,28},{28,24},{1,5},{5... | collective-permute-start | bytes 786440 | tf_op jit(solution)/shard_map/ppermute | solution.py:20
  54.2 8.8 %collective-permute-start.9 = (bf16[4,272,128]{2,1,0:T(8,128)(2,1)S(1)}, bf16[4,272,128]{2,1,0:T(8,128)(2,1)S(1)}, u32[]{:S(2)}, u32[]{:S(2)}) collective-permute-start(bf16[4,272,128]{2,1,0:T(8,128)(2,1)S(1)} %get-tuple-element.19), channel_id=1, source_target_pairs={{0,4},{4,0},{8,12},{12,8},{16,20},{20,16},{24,28},{28,24},{1,5},{5... | collective-permute-start | bytes 835592 | tf_op jit(solution)/shard_map/ppermute | solution.py:20
  56.4 7.3 %collective-permute-start.6 = (bf16[256,128]{1,0:T(8,128)(2,1)S(1)}, bf16[256,128]{1,0:T(8,128)(2,1)S(1)}, u32[]{:S(2)}, u32[]{:S(2)}) collective-permute-start(bf16[256,128]{1,0:T(8,128)(2,1)S(1)} %get-tuple-element.29), channel_id=1, source_target_pairs={{0,8},{4,12},{8,0},{12,4},{16,24},{20,28},{24,16},{28,20},{1,9},{5... | collective-permute-start | bytes 196616 | tf_op jit(solution)/shard_map/ppermute | solution.py:20
  56.5 10.2 %collective-permute-start.8 = (bf16[256,128]{1,0:T(8,128)(2,1)S(1)}, bf16[256,128]{1,0:T(8,128)(2,1)S(1)}, u32[]{:S(2)}, u32[]{:S(2)}) collective-permute-start(bf16[256,128]{1,0:T(8,128)(2,1)S(1)} %get-tuple-element.30), channel_id=1, source_target_pairs={{0,24},{4,28},{8,16},{12,20},{16,8},{20,12},{24,0},{28,4},{1,25},{... | collective-permute-start | bytes 196616 | tf_op jit(solution)/shard_map/ppermute | solution.py:20
  56.6 10.1 %collective-permute-start.7 = (bf16[256,128]{1,0:T(8,128)(2,1)S(1)}, bf16[256,128]{1,0:T(8,128)(2,1)S(1)}, u32[]{:S(2)}, u32[]{:S(2)}) collective-permute-start(bf16[256,128]{1,0:T(8,128)(2,1)S(1)} %get-tuple-element.31), channel_id=1, source_target_pairs={{0,16},{4,20},{8,24},{12,28},{16,0},{20,4},{24,8},{28,12},{1,17},{... | collective-permute-start | bytes 196616 | tf_op jit(solution)/shard_map/ppermute | solution.py:20
  63.1 5.2 %collective-permute-start.10 = (bf16[272,128]{1,0:T(8,128)(2,1)S(1)}, bf16[272,128]{1,0:T(8,128)(2,1)S(1)}, u32[]{:S(2)}, u32[]{:S(2)}) collective-permute-start(bf16[272,128]{1,0:T(8,128)(2,1)S(1)} %get-tuple-element.26), channel_id=1, source_target_pairs={{0,8},{4,12},{8,0},{12,4},{16,24},{20,28},{24,16},{28,20},{1,9},{5... | collective-permute-start | bytes 208904 | tf_op jit(solution)/shard_map/ppermute | solution.py:20
  63.2 6.2 %collective-permute-start.12 = (bf16[272,128]{1,0:T(8,128)(2,1)S(1)}, bf16[272,128]{1,0:T(8,128)(2,1)S(1)}, u32[]{:S(2)}, u32[]{:S(2)}) collective-permute-start(bf16[272,128]{1,0:T(8,128)(2,1)S(1)} %get-tuple-element.27), channel_id=1, source_target_pairs={{0,24},{4,28},{8,16},{12,20},{16,8},{20,12},{24,0},{28,4},{1,25},{... | collective-permute-start | bytes 208904 | tf_op jit(solution)/shard_map/ppermute | solution.py:20
  63.7 8.5 %collective-permute-start.11 = (bf16[272,128]{1,0:T(8,128)(2,1)S(1)}, bf16[272,128]{1,0:T(8,128)(2,1)S(1)}, u32[]{:S(2)}, u32[]{:S(2)}) collective-permute-start(bf16[272,128]{1,0:T(8,128)(2,1)S(1)} %get-tuple-element.28), channel_id=1, source_target_pairs={{0,16},{4,20},{8,24},{12,28},{16,0},{20,4},{24,8},{28,12},{1,17},{... | collective-permute-start | bytes 208904 | tf_op jit(solution)/shard_map/ppermute | solution.py:20

commit v3 on v2

--- a/solution.py
+++ b/solution.py
@@ -12,8 +12,15 @@
 VMEM = pl.BlockSpec(memory_space=pltpu.VMEM)
 SMEM = pl.BlockSpec(memory_space=pltpu.SMEM)
 CHUNKS = 2
-GROUP = 16
 K_ROWS = 4
+
+
+def group_rows(lanes):
+    return 32 if lanes <= 128 else 16
+
+
+def vmem_limit(lanes):
+    return min(52, 16 * -(-lanes // 128)) * 2**20
 
 
 def swap(x, axis, mask):
@@ -28,6 +35,14 @@
         masks += [m ^ mask for m in masks]
         mask //= 2
     return pieces, masks
+
+
+def gathered_stack(x, axis):
+    stack, mask = x[None], lax.axis_size(axis) // 2
+    while mask:
+        stack = jnp.concatenate([stack, swap(stack, axis, mask)], 0)
+        mask //= 2
+    return stack
 
 
 def y_and_z_weights(lanes, cells_z):
@@ -45,10 +60,11 @@
 
 
 def prepare_kernel(plan, masks, cells_z, repeat, idx_ref, *refs):
-    copies, interior, count_sources = plan
+    copies, interior = plan
     pieces = len(masks)
-    sources = [refs[s * pieces:(s + 1) * pieces] for s in range(count_sources)]
-    full_ref, turned_ref, first_ref, grad_ref, visc_ref, slope_ref, every_ref, mine_ref = refs[count_sources * pieces:]
+    edges_ref = refs[pieces]
+    sources = (refs[:pieces], [edges_ref.at[q] for q in range(pieces)])
+    full_ref, turned_ref, first_ref, grad_ref, visc_ref, slope_ref, every_ref, mine_ref = refs[pieces + 1:]
     rows, comps, lanes, width = full_ref.shape
     part = lanes // pieces
     me = idx_ref[0]
@@ -121,7 +137,7 @@
     joint = tile // own
     me = idx_ref[1]
     depth = comps * lanes
-    dests = max(1, min(halves, GROUP // i_part))
+    dests = max(1, min(halves, group_rows(lanes) // i_part))
 
     def group(low, flip):
         def source(i):
@@ -199,8 +215,8 @@
                 ref[low, i_part * own:] = rows.astype(ref.dtype)
 
 
-def prepare(plan, masks, cells_z, idx, sources, own):
-    copies, interior, _ = plan
+def prepare(plan, masks, cells_z, idx, sources, edges, own):
+    copies, interior = plan
     rows = max(at + stop - start for _, start, stop, at in copies)
     count = sum(stop - start for start, stop in interior)
     _, comps, part, width = sources[0].shape
@@ -216,16 +232,16 @@
             jax.ShapeDtypeStruct((count, comps - 1, comps, tile, lanes), BF16),
             jax.ShapeDtypeStruct((width, own), F32),
         ),
-        in_specs=[SMEM] + [VMEM] * len(sources),
+        in_specs=[SMEM] + [VMEM] * (len(sources) + 1),
         out_specs=(VMEM,) * 5,
         scratch_shapes=[
             pltpu.VMEM((comps, comps, width // 8, 8, lanes), F32),
             pltpu.VMEM((width, batch * comps * comps * lanes), BF16),
             pltpu.VMEM((own, batch * comps * comps * lanes), BF16),
         ],
-        compiler_params=pltpu.CompilerParams(vmem_limit_bytes=48 * 2**20),
+        compiler_params=pltpu.CompilerParams(vmem_limit_bytes=vmem_limit(lanes)),
         name="prepare",
-    )(idx, *sources)
+    )(idx, *sources, edges)
 
 
 def project(plan, chunk, idx, state, own, peers):
@@ -243,7 +259,7 @@
         ),
         in_specs=[SMEM] + [VMEM] * 5,
         out_specs=(VMEM,) * 2,
-        compiler_params=pltpu.CompilerParams(vmem_limit_bytes=48 * 2**20),
+        compiler_params=pltpu.CompilerParams(vmem_limit_bytes=vmem_limit(lanes)),
         cost_estimate=pl.CostEstimate(flops=4 * flops, bytes_accessed=4 * 2**20, transcendentals=0),
         name="project",
     )(idx, full, turned, first, grad, visc)
@@ -260,12 +276,15 @@
     block = modes.transpose(0, 3, 1, 2, 4).reshape(cells_x, comps, cells_y * cells_z, width)
     up = [(i, (i + 1) % peers_x) for i in range(peers_x)]
     down = [(j, i) for i, j in up]
+    pieces, masks = gathered(block, "gy")
     before = lax.ppermute(block[-2:], "gx", up)
     after = lax.ppermute(block[:2], "gx", down)
-    padded = jnp.concatenate([before, block, after], 0)
-    pieces, masks = gathered(padded, "gy")
-    plan = (((0, 0, cells_x + 4, 0),), ((2, cells_x + 2),), 1)
-    state = prepare(plan, masks, cells_z, idx, pieces, own)
+    edges = gathered_stack(jnp.concatenate([before, after], 0), "gy")
+    plan = (
+        ((0, 0, cells_x, 2), (1, 0, 2, 0), (1, 2, 4, cells_x + 2)),
+        ((2, cells_x + 2),),
+    )
+    state = prepare(plan, masks, cells_z, idx, pieces, edges, own)
     finals = []
     for chunk in range(CHUNKS):
         send, keep = project(plan, chunk, idx, state, own, peers_x)

time: 73.9 us -> 65.8 us (0.89)
  waiting for transfers between devices: 25.9 us -> 20.2 us
  Pallas kernels: 26.1 us -> 22.5 us
  starting transfers between devices: 16.9 us -> 18.1 us
    ppermute x11 -> x13, waiting for transfers between devices: 20.4 us -> 13.5 us  [swap(): lax.ppermute(x, axis, [(i, i ^ mask) for i in range(lax.axis_size(axis))])]
    pallas_call x2, Pallas kernels: 20.7 us -> 17 us  [project(): pl.pallas_call(functools.partial(main_kernel, plan, own, chunk), out_shap...]
    ppermute x11 -> x13, starting transfers between devices: 10.8 us -> 13.4 us  [swap(): lax.ppermute(x, axis, [(i, i ^ mask) for i in range(lax.axis_size(axis))])]
    ppermute x1, starting transfers between devices: 6.06 us -> 4.61 us  [body(): after = lax.ppermute(block[:2], 'gx', down)]
    ppermute x1, waiting for transfers between devices: 0.37 us -> 1.65 us  [body(): after = lax.ppermute(block[:2], 'gx', down)]
  transfers between devices with their start and end apart: 13 -> 15, of which waited for: 8 -> 8; matrix products, arithmetic and copies ran while one was open for 2% -> 2% of each run, Pallas kernels for 14% -> 13%
where the time goes in v3:
time: 65.8 us; the launch traced here: 65.6 us
  Pallas kernels  22.5 us (34%)
  waiting for transfers between devices  20.2 us (31%)
  starting transfers between devices  18.1 us (28%)
  local copies, waits for them, and re-layouts  2.27 us (3%)
  other arithmetic  1.69 us (3%)
  between operations  0.8 us (1%)
    pallas_call x2, Pallas kernels, project(): pl.pallas_call(functools.partial(main_kernel, plan, own, chunk), out_shap...  17 us
    ppermute x13, waiting for transfers between devices, swap(): lax.ppermute(x, axis, [(i, i ^ mask) for i in range(lax.axis_size(axis))])  13.5 us
    ppermute x13, starting transfers between devices, swap(): lax.ppermute(x, axis, [(i, i ^ mask) for i in range(lax.axis_size(axis))])  13.4 us
    pallas_call x1, Pallas kernels, prepare(): pl.pallas_call(functools.partial(prepare_kernel, plan, masks, cells_z, ti...  5.5 us
    ppermute x1, waiting for transfers between devices, body(): before = lax.ppermute(block[-2:], 'gx', up)  5.13 us
    ppermute x1, starting transfers between devices, body(): after = lax.ppermute(block[:2], 'gx', down)  4.61 us
    ppermute x1, waiting for transfers between devices, body(): after = lax.ppermute(block[:2], 'gx', down)  1.65 us
  transfers between devices with their start and end apart: 15, of which 8 were waited for; matrix products, arithmetic and copies ran while one was open for 2% of the time, Pallas kernels for 13%

profile of v3, /device:TPU:0, one launch (start us, length us, event | category | flops | bytes accessed | tf_op | source)
XLA Modules:
  0.0 65.6 jit_solution(8415650137297091825)
XLA Ops:
  0.6 1.3 %copy.3 = bf16[16,3,16,2,128]{4,3,2,1,0:T(2,128)(2,1)S(1)} copy(bf16[16,3,16,2,128]{4,3,1,2,0:T(2,128)(2,1)} %bitcast.41) | data formatting | bytes 786432 | tf_op jit(solution)/shard_map/transpose | solution.py:276
  1.9 3.0 %collective-permute-start = (bf16[16,3,32,128]{3,2,1,0:T(8,128)(2,1)S(1)}, bf16[16,3,32,128]{3,2,1,0:T(8,128)(2,1)S(1)}, u32[]{:S(2)}, u32[]{:S(2)}) collective-permute-start(bf16[16,3,32,128]{3,2,1,0:T(8,128)(2,1)S(1)} %bitcast.38), channel_id=1, source_target_pairs={{0,2},{1,3},{2,0},{3,1},{4,6},{5,7},{6,4},{7,5},{8,10},{9,11},{10,... | collective-permute-start | bytes 1179656 | tf_op jit(solution)/shard_map/ppermute | solution.py:27
  4.9 0.9 %fusion.8 = (bf16[2,3,16,2,128]{4,3,1,2,0:T(2,128)(2,1)S(1)}, bf16[2,3,16,2,128]{4,3,1,2,0:T(2,128)(2,1)S(1)}) fusion(bf16[16,3,16,2,128]{4,3,1,2,0:T(2,128)(2,1)} %bitcast.42), kind=kLoop, calls=%fused_computation.24 | loop fusion | bytes 196608 | tf_op jit(solution)/shard_map/slice | solution.py:280
  5.8 4.6 %collective-permute-start.4 = (bf16[2,3,32,128]{3,2,1,0:T(8,128)(2,1)S(1)}, bf16[2,3,32,128]{3,2,1,0:T(8,128)(2,1)S(1)}, u32[]{:S(2)}, u32[]{:S(2)}) collective-permute-start(bf16[2,3,32,128]{3,2,1,0:T(8,128)(2,1)S(1)} %bitcast.45), channel_id=1, source_target_pairs={{4,0},{8,4},{12,8},{16,12},{20,16},{24,20},{28,24},{0,28},{5,1},{9... | collective-permute-start | bytes 147464 | tf_op jit(solution)/shard_map/ppermute | solution.py:281
  10.6 1.6 %collective-permute-done.4 = bf16[2,3,32,128]{3,2,1,0:T(8,128)(2,1)S(1)} collective-permute-done((bf16[2,3,32,128]{3,2,1,0:T(8,128)(2,1)S(1)}, bf16[2,3,32,128]{3,2,1,0:T(8,128)(2,1)S(1)}, u32[]{:S(2)}, u32[]{:S(2)}) %collective-permute-start.4) | collective-permute-done | bytes 49184 | tf_op jit(solution)/shard_map/ppermute | solution.py:281
  12.2 5.1 %collective-permute-done.3 = bf16[2,3,32,128]{3,2,1,0:T(8,128)(2,1)S(1)} collective-permute-done((bf16[2,3,32,128]{3,2,1,0:T(8,128)(2,1)S(1)}, bf16[2,3,32,128]{3,2,1,0:T(8,128)(2,1)S(1)}, u32[]{:S(2)}, u32[]{:S(2)}) %collective-permute-start.3) | collective-permute-done | bytes 49184 | tf_op jit(solution)/shard_map/ppermute | solution.py:280
  17.3 0.6 collective-permute-start.5
  18.0 0.5 collective-permute-start.2
  18.5 3.6 %collective-permute-done.5 = bf16[1,4,3,32,128]{4,3,2,1,0:T(8,128)(2,1)S(1)} collective-permute-done((bf16[1,4,3,32,128]{4,3,2,1,0:T(8,128)(2,1)S(1)}, bf16[1,4,3,32,128]{4,3,2,1,0:T(8,128)(2,1)S(1)}, u32[]{:S(2)}, u32[]{:S(2)}) %collective-permute-start.5) | collective-permute-done | bytes 98336 | tf_op jit(solution)/shard_map/ppermute | solution.py:27
  22.2 1.3 %collective-permute-done.6 = bf16[2,4,3,32,128]{4,3,2,1,0:T(8,128)(2,1)S(1)} collective-permute-done((bf16[2,4,3,32,128]{4,3,2,1,0:T(8,128)(2,1)S(1)}, bf16[2,4,3,32,128]{4,3,2,1,0:T(8,128)(2,1)S(1)}, u32[]{:S(2)}, u32[]{:S(2)}) %collective-permute-start.6) | collective-permute-done | bytes 196640 | tf_op jit(solution)/shard_map/ppermute | solution.py:27
  23.6 5.5 %prepare.1 = (bf16[20,3,128,128]{3,2,1,0:T(8,128)(2,1)S(1)}, f32[20,3,16,8,128]{4,3,2,1,0:T(8,128)S(1)}, f32[16,3,32,128]{3,2,1,0:T(8,128)S(1)}, bf16[16,2,3,32,128]{4,3,2,1,0:T(8,128)(2,1)S(1)}, f32[128,32]{1,0:T(8,128)S(1)}) custom-call(s32[2]{0:T(128)S(1)} %pad_add_fusion.idx_ref, bf16[16,3,32,128]{3,2,1,0:T(8,128)(2,1)S(1)} %bitcast.40, ...), custom_call_target="tpu_custom_call" | custom-call | tf_op jit(solution)/shard_map/prepare/pallas_call | solution.py:226
  29.1 8.4 %project.2 = (bf16[4,256,128]{2,1,0:T(8,128)(2,1)S(1)}, f32[4,256,128]{2,1,0:T(8,128)S(1)}) custom-call(s32[2]{0:T(128)S(1)} %pad_add_fusion.idx_ref, bf16[20,3,128,128]{3,2,1,0:T(8,128)(2,1)S(1)} %get-tuple-element.11.full_ref, f32[20,3,16,8,128]{4,3,2,1,0:T(8,128)S(1)} %get-tuple-element.12.turned_ref, f32[16,3,32,128]{3,2,1,0:T(8,128)S(1)} %get-tuple-element.13.first_ref, ...), custom_call_target="tpu_custom_call" | custom-call | flops 12884901888 | bytes 4194304 | tf_op jit(solution)/shard_map/project/pallas_call | solution.py:254
  37.7 8.5 %project.3 = (bf16[4,272,128]{2,1,0:T(8,128)(2,1)S(1)}, f32[4,272,128]{2,1,0:T(8,128)S(1)}) custom-call(s32[2]{0:T(128)S(1)} %pad_add_fusion.idx_ref, bf16[20,3,128,128]{3,2,1,0:T(8,128)(2,1)S(1)} %get-tuple-element.11.full_ref, f32[20,3,16,8,128]{4,3,2,1,0:T(8,128)S(1)} %get-tuple-element.12.turned_ref, f32[16,3,32,128]{3,2,1,0:T(8,128)S(1)} %get-tuple-element.13.first_ref, ...), custom_call_target="tpu_custom_call" | custom-call | flops 12884901888 | bytes 4194304 | tf_op jit(solution)/shard_map/project/pallas_call | solution.py:254
  46.2 2.1 %collective-permute-start.11 = (bf16[4,272,128]{2,1,0:T(8,128)(2,1)S(1)}, bf16[4,272,128]{2,1,0:T(8,128)(2,1)S(1)}, u32[]{:S(2)}, u32[]{:S(2)}) collective-permute-start(bf16[4,272,128]{2,1,0:T(8,128)(2,1)S(1)} %get-tuple-element.19), channel_id=1, source_target_pairs={{0,4},{4,0},{8,12},{12,8},{16,20},{20,16},{24,28},{28,24},{1,5},{5... | collective-permute-start | bytes 835592 | tf_op jit(solution)/shard_map/ppermute | solution.py:27
  48.5 3.4 %collective-permute-start.9 = (bf16[256,128]{1,0:T(8,128)(2,1)S(1)}, bf16[256,128]{1,0:T(8,128)(2,1)S(1)}, u32[]{:S(2)}, u32[]{:S(2)}) collective-permute-start(bf16[256,128]{1,0:T(8,128)(2,1)S(1)} %get-tuple-element.31), channel_id=1, source_target_pairs={{0,16},{4,20},{8,24},{12,28},{16,0},{20,4},{24,8},{28,12},{1,17},{... | collective-permute-start | bytes 196616 | tf_op jit(solution)/shard_map/ppermute | solution.py:27
  51.9 3.0 %collective-permute-done.11 = bf16[4,272,128]{2,1,0:T(8,128)(2,1)S(1)} collective-permute-done((bf16[4,272,128]{2,1,0:T(8,128)(2,1)S(1)}, bf16[4,272,128]{2,1,0:T(8,128)(2,1)S(1)}, u32[]{:S(2)}, u32[]{:S(2)}) %collective-permute-start.11) | collective-permute-done | bytes 278560 | tf_op jit(solution)/shard_map/ppermute | solution.py:27
  55.0 0.1 fusion.7
  55.1 0.2 collective-permute-start.14
  55.4 3.2 %collective-permute-start.13 = (bf16[272,128]{1,0:T(8,128)(2,1)S(1)}, bf16[272,128]{1,0:T(8,128)(2,1)S(1)}, u32[]{:S(2)}, u32[]{:S(2)}) collective-permute-start(bf16[272,128]{1,0:T(8,128)(2,1)S(1)} %get-tuple-element.28), channel_id=1, source_target_pairs={{0,16},{4,20},{8,24},{12,28},{16,0},{20,4},{24,8},{28,12},{1,17},{... | collective-permute-start | bytes 208904 | tf_op jit(solution)/shard_map/ppermute | solution.py:27
  58.7 1.6 %collective-permute-done.12 = bf16[272,128]{1,0:T(8,128)(2,1)S(1)} collective-permute-done((bf16[272,128]{1,0:T(8,128)(2,1)S(1)}, bf16[272,128]{1,0:T(8,128)(2,1)S(1)}, u32[]{:S(2)}, u32[]{:S(2)}) %collective-permute-start.12) | collective-permute-done | bytes 69664 | tf_op jit(solution)/shard_map/ppermute | solution.py:27
  60.2 1.1 %collective-permute-done.14 = bf16[272,128]{1,0:T(8,128)(2,1)S(1)} collective-permute-done((bf16[272,128]{1,0:T(8,128)(2,1)S(1)}, bf16[272,128]{1,0:T(8,128)(2,1)S(1)}, u32[]{:S(2)}, u32[]{:S(2)}) %collective-permute-start.14) | collective-permute-done | bytes 69664 | tf_op jit(solution)/shard_map/ppermute | solution.py:27
  61.3 2.9 %collective-permute-done.13 = bf16[272,128]{1,0:T(8,128)(2,1)S(1)} collective-permute-done((bf16[272,128]{1,0:T(8,128)(2,1)S(1)}, bf16[272,128]{1,0:T(8,128)(2,1)S(1)}, u32[]{:S(2)}, u32[]{:S(2)}) %collective-permute-start.13) | collective-permute-done | bytes 69664 | tf_op jit(solution)/shard_map/ppermute | solution.py:27
  64.2 0.6 slice_multiply_fusion
  64.8 0.7 %maximum_multiply_fusion = f32[16,32,128]{2,1,0:T(8,128)} fusion(f32[8,32,128]{2,1,0:T(8,128)S(1)} %bitcast.44, f32[8,32,128]{2,1,0:T(8,128)S(1)} %bitcast.43), kind=kLoop, calls=%fused_computation.3 | loop fusion | flops 131072 | bytes 524288 | tf_op jit(solution)/shard_map/mul | solution.py:297
  (26 shorter events, 0.8 us)
Async XLA Ops:
  1.9 16.1 %collective-permute-start = (bf16[16,3,32,128]{3,2,1,0:T(8,128)(2,1)S(1)}, bf16[16,3,32,128]{3,2,1,0:T(8,128)(2,1)S(1)}, u32[]{:S(2)}, u32[]{:S(2)}) collective-permute-start(bf16[16,3,32,128]{3,2,1,0:T(8,128)(2,1)S(1)} %bitcast.38), channel_id=1, source_target_pairs={{0,2},{1,3},{2,0},{3,1},{4,6},{5,7},{6,4},{7,5},{8,10},{9,11},{10,... | collective-permute-start | bytes 1179656 | tf_op jit(solution)/shard_map/ppermute | solution.py:27
  5.8 6.4 %collective-permute-start.4 = (bf16[2,3,32,128]{3,2,1,0:T(8,128)(2,1)S(1)}, bf16[2,3,32,128]{3,2,1,0:T(8,128)(2,1)S(1)}, u32[]{:S(2)}, u32[]{:S(2)}) collective-permute-start(bf16[2,3,32,128]{3,2,1,0:T(8,128)(2,1)S(1)} %bitcast.45), channel_id=1, source_target_pairs={{4,0},{8,4},{12,8},{16,12},{20,16},{24,20},{28,24},{0,28},{5,1},{9... | collective-permute-start | bytes 147464 | tf_op jit(solution)/shard_map/ppermute | solution.py:281
  10.5 6.8 %collective-permute-start.3 = (bf16[2,3,32,128]{3,2,1,0:T(8,128)(2,1)S(1)}, bf16[2,3,32,128]{3,2,1,0:T(8,128)(2,1)S(1)}, u32[]{:S(2)}, u32[]{:S(2)}) collective-permute-start(bf16[2,3,32,128]{3,2,1,0:T(8,128)(2,1)S(1)} %bitcast.46), channel_id=1, source_target_pairs={{0,4},{4,8},{8,12},{12,16},{16,20},{20,24},{24,28},{28,0},{1,5},{5... | collective-permute-start | bytes 147464 | tf_op jit(solution)/shard_map/ppermute | solution.py:280
  17.3 4.7 %collective-permute-start.5 = (bf16[1,4,3,32,128]{4,3,2,1,0:T(8,128)(2,1)S(1)}, bf16[1,4,3,32,128]{4,3,2,1,0:T(8,128)(2,1)S(1)}, u32[]{:S(2)}, u32[]{:S(2)}) collective-permute-start(bf16[1,4,3,32,128]{4,3,2,1,0:T(8,128)(2,1)S(1)} %maximum_bitcast_fusion), channel_id=1, source_target_pairs={{0,2},{1,3},{2,0},{3,1},{4,6},{5,7},{6,4},{7,5},{8,10},{9,11},{10,... | collective-permute-start | bytes 294920 | tf_op jit(solution)/shard_map/ppermute | solution.py:27
  17.9 5.7 %collective-permute-start.1 = (bf16[16,3,32,128]{3,2,1,0:T(8,128)(2,1)S(1)}, bf16[16,3,32,128]{3,2,1,0:T(8,128)(2,1)S(1)}, u32[]{:S(2)}, u32[]{:S(2)}) collective-permute-start(bf16[16,3,32,128]{3,2,1,0:T(8,128)(2,1)S(1)} %bitcast.39), channel_id=1, source_target_pairs={{0,1},{1,0},{2,3},{3,2},{4,5},{5,4},{6,7},{7,6},{8,9},{9,8},{10,11... | collective-permute-start | bytes 1179656 | tf_op jit(solution)/shard_map/ppermute | solution.py:27
  18.0 5.7 %collective-permute-start.2 = (bf16[16,3,32,128]{3,2,1,0:T(8,128)(2,1)S(1)}, bf16[16,3,32,128]{3,2,1,0:T(8,128)(2,1)S(1)}, u32[]{:S(2)}, u32[]{:S(2)}) collective-permute-start(bf16[16,3,32,128]{3,2,1,0:T(8,128)(2,1)S(1)} %collective-permute-done.refs_1_), channel_id=1, source_target_pairs={{0,1},{1,0},{2,3},{3,2},{4,5},{5,4},{6,7},{7,6},{8,9},{9,8},{10,11... | collective-permute-start | bytes 1179656 | tf_op jit(solution)/shard_map/ppermute | solution.py:27
  22.1 1.5 %collective-permute-start.6 = (bf16[2,4,3,32,128]{4,3,2,1,0:T(8,128)(2,1)S(1)}, bf16[2,4,3,32,128]{4,3,2,1,0:T(8,128)(2,1)S(1)}, u32[]{:S(2)}, u32[]{:S(2)}) collective-permute-start(bf16[2,4,3,32,128]{4,3,2,1,0:T(8,128)(2,1)S(1)} %pad_maximum_fusion.1), channel_id=1, source_target_pairs={{0,1},{1,0},{2,3},{3,2},{4,5},{5,4},{6,7},{7,6},{8,9},{9,8},{10,11... | collective-permute-start | bytes 589832 | tf_op jit(solution)/shard_map/ppermute | solution.py:27
  37.6 10.7 %collective-permute-start.7 = (bf16[4,256,128]{2,1,0:T(8,128)(2,1)S(1)}, bf16[4,256,128]{2,1,0:T(8,128)(2,1)S(1)}, u32[]{:S(2)}, u32[]{:S(2)}) collective-permute-start(bf16[4,256,128]{2,1,0:T(8,128)(2,1)S(1)} %get-tuple-element.17), channel_id=1, source_target_pairs={{0,4},{4,0},{8,12},{12,8},{16,20},{20,16},{24,28},{28,24},{1,5},{5... | collective-permute-start | bytes 786440 | tf_op jit(solution)/shard_map/ppermute | solution.py:27
  46.2 8.8 %collective-permute-start.11 = (bf16[4,272,128]{2,1,0:T(8,128)(2,1)S(1)}, bf16[4,272,128]{2,1,0:T(8,128)(2,1)S(1)}, u32[]{:S(2)}, u32[]{:S(2)}) collective-permute-start(bf16[4,272,128]{2,1,0:T(8,128)(2,1)S(1)} %get-tuple-element.19), channel_id=1, source_target_pairs={{0,4},{4,0},{8,12},{12,8},{16,20},{20,16},{24,28},{28,24},{1,5},{5... | collective-permute-start | bytes 835592 | tf_op jit(solution)/shard_map/ppermute | solution.py:27
  48.4 7.0 %collective-permute-start.8 = (bf16[256,128]{1,0:T(8,128)(2,1)S(1)}, bf16[256,128]{1,0:T(8,128)(2,1)S(1)}, u32[]{:S(2)}, u32[]{:S(2)}) collective-permute-start(bf16[256,128]{1,0:T(8,128)(2,1)S(1)} %get-tuple-element.29), channel_id=1, source_target_pairs={{0,8},{4,12},{8,0},{12,4},{16,24},{20,28},{24,16},{28,20},{1,9},{5... | collective-permute-start | bytes 196616 | tf_op jit(solution)/shard_map/ppermute | solution.py:27
  48.5 10.2 %collective-permute-start.10 = (bf16[256,128]{1,0:T(8,128)(2,1)S(1)}, bf16[256,128]{1,0:T(8,128)(2,1)S(1)}, u32[]{:S(2)}, u32[]{:S(2)}) collective-permute-start(bf16[256,128]{1,0:T(8,128)(2,1)S(1)} %get-tuple-element.30), channel_id=1, source_target_pairs={{0,24},{4,28},{8,16},{12,20},{16,8},{20,12},{24,0},{28,4},{1,25},{... | collective-permute-start | bytes 196616 | tf_op jit(solution)/shard_map/ppermute | solution.py:27
  48.5 10.1 %collective-permute-start.9 = (bf16[256,128]{1,0:T(8,128)(2,1)S(1)}, bf16[256,128]{1,0:T(8,128)(2,1)S(1)}, u32[]{:S(2)}, u32[]{:S(2)}) collective-permute-start(bf16[256,128]{1,0:T(8,128)(2,1)S(1)} %get-tuple-element.31), channel_id=1, source_target_pairs={{0,16},{4,20},{8,24},{12,28},{16,0},{20,4},{24,8},{28,12},{1,17},{... | collective-permute-start | bytes 196616 | tf_op jit(solution)/shard_map/ppermute | solution.py:27
  55.1 5.2 %collective-permute-start.12 = (bf16[272,128]{1,0:T(8,128)(2,1)S(1)}, bf16[272,128]{1,0:T(8,128)(2,1)S(1)}, u32[]{:S(2)}, u32[]{:S(2)}) collective-permute-start(bf16[272,128]{1,0:T(8,128)(2,1)S(1)} %get-tuple-element.26), channel_id=1, source_target_pairs={{0,8},{4,12},{8,0},{12,4},{16,24},{20,28},{24,16},{28,20},{1,9},{5... | collective-permute-start | bytes 208904 | tf_op jit(solution)/shard_map/ppermute | solution.py:27
  55.1 6.2 %collective-permute-start.14 = (bf16[272,128]{1,0:T(8,128)(2,1)S(1)}, bf16[272,128]{1,0:T(8,128)(2,1)S(1)}, u32[]{:S(2)}, u32[]{:S(2)}) collective-permute-start(bf16[272,128]{1,0:T(8,128)(2,1)S(1)} %get-tuple-element.27), channel_id=1, source_target_pairs={{0,24},{4,28},{8,16},{12,20},{16,8},{20,12},{24,0},{28,4},{1,25},{... | collective-permute-start | bytes 208904 | tf_op jit(solution)/shard_map/ppermute | solution.py:27
  55.4 8.8 %collective-permute-start.13 = (bf16[272,128]{1,0:T(8,128)(2,1)S(1)}, bf16[272,128]{1,0:T(8,128)(2,1)S(1)}, u32[]{:S(2)}, u32[]{:S(2)}) collective-permute-start(bf16[272,128]{1,0:T(8,128)(2,1)S(1)} %get-tuple-element.28), channel_id=1, source_target_pairs={{0,16},{4,20},{8,24},{12,28},{16,0},{20,4},{24,8},{28,12},{1,17},{... | collective-permute-start | bytes 208904 | tf_op jit(solution)/shard_map/ppermute | solution.py:27

commit v4 on v3

--- a/solution.py
+++ b/solution.py
@@ -11,12 +11,12 @@
 BF16, F32 = jnp.bfloat16, jnp.float32
 VMEM = pl.BlockSpec(memory_space=pltpu.VMEM)
 SMEM = pl.BlockSpec(memory_space=pltpu.SMEM)
-CHUNKS = 2
+PARTS = 2
 K_ROWS = 4
 
 
 def group_rows(lanes):
-    return 32 if lanes <= 128 else 16
+    return 32 if lanes <= 128 else 8
 
 
 def vmem_limit(lanes):
@@ -125,27 +125,37 @@
         at += stop - start
 
 
-def main_kernel(plan, own, chunk, idx_ref, full_ref, turned_ref, first_ref, grad_ref, visc_ref,
-                send_ref, keep_ref):
+def code_of(part, stage, j):
+    if part == 0 or stage >= 2:
+        return (2 * j + 1) << stage
+    if stage == 0:
+        return (j & 1) | 2 | ((j >> 1) << 2)
+    return 1 | (j << 2)
+
+
+def bit_of(part, stage):
+    return 1 - stage if part == 1 and stage < 2 else stage
+
+
+def main_kernel(plan, own, stage, parts, idx_ref, full_ref, turned_ref, first_ref, grad_ref, visc_ref, *out_refs):
     interior = [r for start, stop in plan[1] for r in range(start, stop)]
     _, comps, lanes, width = full_ref.shape
-    halves, block_rows = send_ref.shape[:2]
-    peers = 2 * halves
-    i_block = width // peers
-    i_part = i_block // CHUNKS
+    i_block, i_part = parts[0][2], parts[0][3]
     tile = grad_ref.shape[3]
     joint = tile // own
     me = idx_ref[1]
     depth = comps * lanes
-    dests = max(1, min(halves, group_rows(lanes) // i_part))
-
-    def group(low, flip):
+
+    def code(part, j):
+        return 0 if stage is None else code_of(part, stage, j)
+
+    def group(jobs):
         def source(i):
-            dest = me ^ (flip + 2 * (low + i // i_part))
-            row = dest * i_block + chunk * i_part
+            part, j = jobs[i // i_part]
+            row = (me ^ code(part, j)) * i_block + part * i_part
             if i_part % 8 == 0:
-                return row // 8 + (i % i_part) // 8, (i % i_part) % 8
-            return row // 8, (chunk * i_part) % 8 + i % i_part
+                return row // 8 + (i % i_part) // 8, i % 8
+            return row // 8, (part * i_part) % 8 + i % i_part
 
         def pairs(x, i):
             pieces = []
@@ -153,12 +163,12 @@
                 cut = slice(lane, lane + 128)
                 wide, narrow = [], []
                 for a in range(comps):
-                    parts = []
+                    lines = []
                     for j in range(joint):
                         lead, sub = source(i + j)
                         line = turned_ref[interior[x], a, lead, sub:sub + 1, cut]
-                        parts.append(jnp.broadcast_to(line, (own, 128)))
-                    wide.append(jnp.concatenate(parts, 0))
+                        lines.append(jnp.broadcast_to(line, (own, 128)))
+                    wide.append(jnp.concatenate(lines, 0))
                     half = wide[-1][:16].astype(BF16)
                     narrow.append(jnp.concatenate([half] * (tile // 16), 0))
                 row = []
@@ -178,41 +188,41 @@
             count = min(K_ROWS, len(interior) - first)
             left = jnp.concatenate([
                 jnp.concatenate([p for x in range(first, first + count) for p in pairs(x, i)], 1)
-                for i in range(0, dests * i_part, joint)
+                for i in range(0, len(jobs) * i_part, joint)
             ], 0)
             right = full_ref[interior[first]:interior[first] + count].reshape(count * depth, width)
             term = jnp.dot(left, right, preferred_element_type=F32)
             total = term if total is None else total + term
-        return total.reshape(dests, i_part * own, width)
-
-    steps = halves // dests
-
-    def step_of(step, carry):
-        sends = step < steps
-        low = lax.rem(step, steps) * dests
-        value = group(low, jnp.where(sends, 1, 0))
-
-        @pl.when(sends)
-        def _():
-            send_ref[pl.ds(low, dests), :i_part * own] = value.astype(BF16)
-
-        @pl.when(jnp.logical_not(sends))
-        def _():
-            keep_ref[pl.ds(low, dests), :i_part * own] = value
-
-        return carry
-
-    lax.fori_loop(0, 2 * steps, step_of, 0)
-    if block_rows > i_part * own:
-        for low in range(halves):
-            for flip, ref in ((1, send_ref), (0, keep_ref)):
-                dest = me ^ (flip + 2 * low)
+        return total.reshape(len(jobs), i_part * own, width)
+
+    jobs = [(part, j) for part, count, _, _ in parts for j in range(count)]
+    at_once = group_rows(lanes) // i_part
+    if len(jobs) <= at_once:
+        value, at = group(jobs), 0
+        for (part, count, _, _), ref in zip(parts, out_refs):
+            ref[:, :i_part * own] = value[at:at + count].astype(ref.dtype)
+            at += count
+    else:
+        for (part, count, _, _), ref in zip(parts, out_refs):
+            size = min(at_once, count)
+
+            def one(step, carry, part=part, ref=ref, size=size):
+                low = step * size
+                value = group([(part, low + j) for j in range(size)])
+                ref[pl.ds(low, size), :i_part * own] = value.astype(ref.dtype)
+                return carry
+
+            lax.fori_loop(0, count // size, one, 0)
+    for (part, count, _, _), ref in zip(parts, out_refs):
+        if part == 0:
+            for j in range(count):
+                dest = me ^ code(part, j)
                 rows = visc_ref[pl.ds(pl.multiple_of(dest * i_block, i_block), i_block), :]
                 rows = jnp.concatenate([rows, jnp.zeros((i_block, width - own), F32)], 1)
-                fill = block_rows - i_part * own - i_block
+                fill = ref.shape[1] - i_part * own - i_block
                 if fill:
                     rows = jnp.concatenate([rows, jnp.zeros((fill, width), F32)], 0)
-                ref[low, i_part * own:] = rows.astype(ref.dtype)
+                ref[j, i_part * own:] = rows.astype(ref.dtype)
 
 
 def prepare(plan, masks, cells_z, idx, sources, edges, own):
@@ -244,25 +254,32 @@
     )(idx, *sources, edges)
 
 
-def project(plan, chunk, idx, state, own, peers):
+def project(plan, stage, parts, idx, state, own, peers, dtype):
     full, turned, first, grad, visc = state
     _, comps, lanes, width = full.shape
-    halves, i_block = peers // 2, width // peers
-    i_part = i_block // CHUNKS
-    rows = i_part * own + (max(16, i_block) if chunk == CHUNKS - 1 else 0)
-    flops = 2 * halves * 2 * i_part * own * grad.shape[0] * comps * lanes * width
+    i_block = width // peers
+    i_part = i_block // PARTS
+    count = 1 if stage is None else peers >> (stage + 1)
+    sizes = [i_part * own + (max(16, i_block) if part == 0 else 0) for part in parts]
+    flops = 2 * len(parts) * count * i_part * own * grad.shape[0] * comps * lanes * width
     return pl.pallas_call(
-        functools.partial(main_kernel, plan, own, chunk),
-        out_shape=(
-            jax.ShapeDtypeStruct((halves, rows, width), BF16),
-            jax.ShapeDtypeStruct((halves, rows, width), F32),
-        ),
+        functools.partial(main_kernel, plan, own, stage, [(part, count, i_block, i_part) for part in parts]),
+        out_shape=[jax.ShapeDtypeStruct((count, rows, width), dtype) for rows in sizes],
         in_specs=[SMEM] + [VMEM] * 5,
-        out_specs=(VMEM,) * 2,
+        out_specs=[VMEM] * len(parts),
         compiler_params=pltpu.CompilerParams(vmem_limit_bytes=vmem_limit(lanes)),
-        cost_estimate=pl.CostEstimate(flops=4 * flops, bytes_accessed=4 * 2**20, transcendentals=0),
+        cost_estimate=pl.CostEstimate(flops=4 * flops, bytes_accessed=2**20, transcendentals=0),
         name="project",
     )(idx, full, turned, first, grad, visc)
+
+
+def arrived(results, part, code):
+    found = []
+    for stage, blocks in enumerate(results):
+        for j in range(blocks.shape[0]):
+            if code_of(part, stage, j) ^ (1 << bit_of(part, stage)) == code:
+                found.append(blocks[j].astype(F32))
+    return sum(found)
 
 
 def body(modes):
@@ -271,7 +288,7 @@
     total_points = cells_x * cells_y * cells_z * peers_x * peers_y
     own = width // peers_y
     i_block = width // peers_x
-    i_part = i_block // CHUNKS
+    i_part = i_block // PARTS
     idx = jnp.stack([lax.axis_index("gy"), lax.axis_index("gx")]).astype(jnp.int32)
     block = modes.transpose(0, 3, 1, 2, 4).reshape(cells_x, comps, cells_y * cells_z, width)
     up = [(i, (i + 1) % peers_x) for i in range(peers_x)]
@@ -285,19 +302,35 @@
         ((2, cells_x + 2),),
     )
     state = prepare(plan, masks, cells_z, idx, pieces, edges, own)
-    finals = []
-    for chunk in range(CHUNKS):
-        send, keep = project(plan, chunk, idx, state, own, peers_x)
-        got = swap(send, "gx", 1)
-        sums = keep + got.astype(F32)
-        final = sums[0]
-        for q in range(1, peers_x // 2):
-            final = final + swap(sums[q].astype(BF16), "gx", 2 * q).astype(F32)
-        finals.append(final)
+    stages = peers_x.bit_length() - 1
+    both = tuple(range(PARTS))
+    results = [[], []]
+    for part in both:
+        (send,) = project(plan, 0, (part,), idx, state, own, peers_x, BF16)
+        results[part].append(swap(send, "gx", 1 << bit_of(part, 0)))
+        idx, send = lax.optimization_barrier((idx, send))
+    for stage in range(1, stages):
+        kept = project(plan, stage, both, idx, state, own, peers_x, F32)
+        sums = [
+            jnp.stack([kept[part][j] + arrived(results[part], part, code_of(part, stage, j))
+                       for j in range(kept[part].shape[0])]).astype(BF16)
+            for part in both
+        ]
+        if bit_of(0, stage) == bit_of(1, stage):
+            rows = sums[0].shape[1]
+            joined = swap(jnp.concatenate(sums, 1), "gx", 1 << stage)
+            got = [joined[:, :rows], joined[:, rows:]]
+        else:
+            got = [swap(sums[part], "gx", 1 << bit_of(part, stage)) for part in both]
+        for part in both:
+            results[part].append(got[part])
+        idx, sums = lax.optimization_barrier((idx, sums))
+    kept = project(plan, None, both, idx, state, own, peers_x, F32)
+    finals = [kept[part][0] + arrived(results[part], part, 0) for part in both]
     convective = jnp.concatenate(
         [f[:i_part * own].reshape(i_part, own, width) for f in finals], 0
     ) * (-1.0 / math.sqrt(total_points))
-    viscous = finals[-1][i_part * own:i_part * own + i_block, :own] * (-1.0 / total_points)
+    viscous = finals[0][i_part * own:i_part * own + i_block, :own] * (-1.0 / total_points)
     return (convective, viscous)
 
 

time: 65.8 us -> 61.6 us (0.936)
  starting transfers between devices: 18.1 us -> 10.9 us
  Pallas kernels: 22.5 us -> 24.4 us
  waiting for transfers between devices: 20.2 us -> 21.3 us
    ppermute x13 -> x10, starting transfers between devices: 13.4 us -> 6.2 us  [swap(): lax.ppermute(x, axis, [(i, i ^ mask) for i in range(lax.axis_size(axis))])]
    pallas_call x2 -> x5, Pallas kernels: 17 us -> 18.9 us  [project(): pl.pallas_call(functools.partial(main_kernel, plan, own, stage, [(part, c...]
    ppermute x13 -> x10, waiting for transfers between devices: 13.5 us -> 14.6 us  [swap(): lax.ppermute(x, axis, [(i, i ^ mask) for i in range(lax.axis_size(axis))])]
  transfers between devices with their start and end apart: 15 -> 12, of which waited for: 8 -> 9; matrix products, arithmetic and copies ran while one was open for 2% -> 2% of each run, Pallas kernels for 13% -> 16%
where the time goes in v4:
time: 61.6 us; the launch traced here: 61.3 us
  Pallas kernels  24.4 us (40%)
  waiting for transfers between devices  21.3 us (35%)
  starting transfers between devices  10.9 us (18%)
  local copies, waits for them, and re-layouts  2.24 us (4%)
  other arithmetic  1.7 us (3%)
  between operations  0.83 us (1%)
    pallas_call x5, Pallas kernels, project(): pl.pallas_call(functools.partial(main_kernel, plan, own, stage, [(part, c...  18.9 us
    ppermute x10, waiting for transfers between devices, swap(): lax.ppermute(x, axis, [(i, i ^ mask) for i in range(lax.axis_size(axis))])  14.6 us
    ppermute x10, starting transfers between devices, swap(): lax.ppermute(x, axis, [(i, i ^ mask) for i in range(lax.axis_size(axis))])  6.2 us
    pallas_call x1, Pallas kernels, prepare(): pl.pallas_call(functools.partial(prepare_kernel, plan, masks, cells_z, ti...  5.5 us
    ppermute x1, waiting for transfers between devices, body(): before = lax.ppermute(block[-2:], 'gx', up)  5.13 us
    ppermute x1, starting transfers between devices, body(): after = lax.ppermute(block[:2], 'gx', down)  4.61 us
    ppermute x1, waiting for transfers between devices, body(): after = lax.ppermute(block[:2], 'gx', down)  1.65 us
    transpose x1, local copies, waits for them, and re-layouts, body(): modes.transpose(0, 3, 1, 2, 4)  1.27 us
  transfers between devices with their start and end apart: 12, of which 9 were waited for; matrix products, arithmetic and copies ran while one was open for 2% of the time, Pallas kernels for 16%

profile of v4, /device:TPU:0, one launch (start us, length us, event | category | flops | bytes accessed | tf_op | source)
XLA Modules:
  0.0 61.3 jit_solution(17028624692720624227)
XLA Ops:
  0.6 1.3 %copy.3 = bf16[16,3,16,2,128]{4,3,2,1,0:T(2,128)(2,1)S(1)} copy(bf16[16,3,16,2,128]{4,3,1,2,0:T(2,128)(2,1)} %bitcast.14) | data formatting | bytes 786432 | tf_op jit(solution)/shard_map/transpose | solution.py:293
  1.9 3.0 %collective-permute-start = (bf16[16,3,32,128]{3,2,1,0:T(8,128)(2,1)S(1)}, bf16[16,3,32,128]{3,2,1,0:T(8,128)(2,1)S(1)}, u32[]{:S(2)}, u32[]{:S(2)}) collective-permute-start(bf16[16,3,32,128]{3,2,1,0:T(8,128)(2,1)S(1)} %bitcast.11), channel_id=1, source_target_pairs={{0,2},{1,3},{2,0},{3,1},{4,6},{5,7},{6,4},{7,5},{8,10},{9,11},{10,... | collective-permute-start | bytes 1179656 | tf_op jit(solution)/shard_map/ppermute | solution.py:27
  4.9 0.9 %fusion = (bf16[2,3,16,2,128]{4,3,1,2,0:T(2,128)(2,1)S(1)}, bf16[2,3,16,2,128]{4,3,1,2,0:T(2,128)(2,1)S(1)}) fusion(bf16[16,3,16,2,128]{4,3,1,2,0:T(2,128)(2,1)} %bitcast.15), kind=kLoop, calls=%fused_computation.17 | loop fusion | bytes 196608 | tf_op jit(solution)/shard_map/slice | solution.py:297
  5.8 4.6 %collective-permute-start.4 = (bf16[2,3,32,128]{3,2,1,0:T(8,128)(2,1)S(1)}, bf16[2,3,32,128]{3,2,1,0:T(8,128)(2,1)S(1)}, u32[]{:S(2)}, u32[]{:S(2)}) collective-permute-start(bf16[2,3,32,128]{3,2,1,0:T(8,128)(2,1)S(1)} %bitcast.19), channel_id=1, source_target_pairs={{4,0},{8,4},{12,8},{16,12},{20,16},{24,20},{28,24},{0,28},{5,1},{9... | collective-permute-start | bytes 147464 | tf_op jit(solution)/shard_map/ppermute | solution.py:298
  10.6 1.6 %collective-permute-done.4 = bf16[2,3,32,128]{3,2,1,0:T(8,128)(2,1)S(1)} collective-permute-done((bf16[2,3,32,128]{3,2,1,0:T(8,128)(2,1)S(1)}, bf16[2,3,32,128]{3,2,1,0:T(8,128)(2,1)S(1)}, u32[]{:S(2)}, u32[]{:S(2)}) %collective-permute-start.4) | collective-permute-done | bytes 49184 | tf_op jit(solution)/shard_map/ppermute | solution.py:298
  12.2 5.1 %collective-permute-done.3 = bf16[2,3,32,128]{3,2,1,0:T(8,128)(2,1)S(1)} collective-permute-done((bf16[2,3,32,128]{3,2,1,0:T(8,128)(2,1)S(1)}, bf16[2,3,32,128]{3,2,1,0:T(8,128)(2,1)S(1)}, u32[]{:S(2)}, u32[]{:S(2)}) %collective-permute-start.3) | collective-permute-done | bytes 49184 | tf_op jit(solution)/shard_map/ppermute | solution.py:297
  17.3 0.6 collective-permute-start.5
  18.0 0.5 collective-permute-start.2
  18.5 3.6 %collective-permute-done.5 = bf16[1,4,3,32,128]{4,3,2,1,0:T(8,128)(2,1)S(1)} collective-permute-done((bf16[1,4,3,32,128]{4,3,2,1,0:T(8,128)(2,1)S(1)}, bf16[1,4,3,32,128]{4,3,2,1,0:T(8,128)(2,1)S(1)}, u32[]{:S(2)}, u32[]{:S(2)}) %collective-permute-start.5) | collective-permute-done | bytes 98336 | tf_op jit(solution)/shard_map/ppermute | solution.py:27
  22.2 1.3 %collective-permute-done.6 = bf16[2,4,3,32,128]{4,3,2,1,0:T(8,128)(2,1)S(1)} collective-permute-done((bf16[2,4,3,32,128]{4,3,2,1,0:T(8,128)(2,1)S(1)}, bf16[2,4,3,32,128]{4,3,2,1,0:T(8,128)(2,1)S(1)}, u32[]{:S(2)}, u32[]{:S(2)}) %collective-permute-start.6) | collective-permute-done | bytes 196640 | tf_op jit(solution)/shard_map/ppermute | solution.py:27
  23.6 5.5 %prepare.1 = (bf16[20,3,128,128]{3,2,1,0:T(8,128)(2,1)S(1)}, f32[20,3,16,8,128]{4,3,2,1,0:T(8,128)S(1)}, f32[16,3,32,128]{3,2,1,0:T(8,128)S(1)}, bf16[16,2,3,32,128]{4,3,2,1,0:T(8,128)(2,1)S(1)}, f32[128,32]{1,0:T(8,128)S(1)}) custom-call(s32[2]{0:T(128)S(1)} %pad_add_fusion.idx_ref, bf16[16,3,32,128]{3,2,1,0:T(8,128)(2,1)S(1)} %bitcast.13, ...), custom_call_target="tpu_custom_call" | custom-call | tf_op jit(solution)/shard_map/prepare/pallas_call | solution.py:236
  29.1 4.4 %project.5 = bf16[4,272,128]{2,1,0:T(8,128)(2,1)S(1)} custom-call(s32[2]{0:T(128)S(1)} %pad_add_fusion.idx_ref, bf16[20,3,128,128]{3,2,1,0:T(8,128)(2,1)S(1)} %get-tuple-element.17.full_ref, f32[20,3,16,8,128]{4,3,2,1,0:T(8,128)S(1)} %get-tuple-element.18.turned_ref, f32[16,3,32,128]{3,2,1,0:T(8,128)S(1)} %get-tuple-element.19.first_ref, ...), custom_call_target="tpu_custom_call" | custom-call | flops 6442450944 | bytes 1048576 | tf_op jit(solution)/shard_map/project/pallas_call | solution.py:265
  33.5 4.5 %project.6 = bf16[4,256,128]{2,1,0:T(8,128)(2,1)S(1)} custom-call(s32[2]{0:T(128)S(1)} %pad_add_fusion.idx_ref, bf16[20,3,128,128]{3,2,1,0:T(8,128)(2,1)S(1)} %get-tuple-element.17.full_ref, f32[20,3,16,8,128]{4,3,2,1,0:T(8,128)S(1)} %get-tuple-element.18.turned_ref, f32[16,3,32,128]{3,2,1,0:T(8,128)S(1)} %get-tuple-element.19.first_ref, ...), custom_call_target="tpu_custom_call" | custom-call | flops 6442450944 | bytes 1048576 | tf_op jit(solution)/shard_map/project/pallas_call | solution.py:265
  38.2 4.7 %project.7 = (f32[2,272,128]{2,1,0:T(8,128)S(1)}, f32[2,256,128]{2,1,0:T(8,128)S(1)}) custom-call(s32[2]{0:T(128)S(1)} %pad_add_fusion.idx_ref, bf16[20,3,128,128]{3,2,1,0:T(8,128)(2,1)S(1)} %get-tuple-element.17.full_ref, f32[20,3,16,8,128]{4,3,2,1,0:T(8,128)S(1)} %get-tuple-element.18.turned_ref, f32[16,3,32,128]{3,2,1,0:T(8,128)S(1)} %get-tuple-element.19.first_ref, ...), custom_call_target="tpu_custom_call" | custom-call | flops 6442450944 | bytes 1048576 | tf_op jit(solution)/shard_map/project/pallas_call | solution.py:265
  42.9 3.5 %collective-permute-done.8 = bf16[4,256,128]{2,1,0:T(8,128)(2,1)S(1)} collective-permute-done((bf16[4,256,128]{2,1,0:T(8,128)(2,1)S(1)}, bf16[4,256,128]{2,1,0:T(8,128)(2,1)S(1)}, u32[]{:S(2)}, u32[]{:S(2)}) %collective-permute-start.8) | collective-permute-done | bytes 262176 | tf_op jit(solution)/shard_map/ppermute | solution.py:27
  46.6 0.3 collective-permute-done.7
  46.9 1.7 %collective-permute-start.9 = (bf16[2,272,128]{2,1,0:T(8,128)(2,1)S(1)}, bf16[2,272,128]{2,1,0:T(8,128)(2,1)S(1)}, u32[]{:S(2)}, u32[]{:S(2)}) collective-permute-start(bf16[2,272,128]{2,1,0:T(8,128)(2,1)S(1)} %pad_maximum_fusion.2), channel_id=1, source_target_pairs={{0,8},{4,12},{8,0},{12,4},{16,24},{20,28},{24,16},{28,20},{1,9},{5... | collective-permute-start | bytes 417800 | tf_op jit(solution)/shard_map/ppermute | solution.py:27
  48.7 2.6 %project.8 = (f32[1,272,128]{2,1,0:T(8,128)S(1)}, f32[1,256,128]{2,1,0:T(8,128)S(1)}) custom-call(s32[2]{0:T(128)S(1)} %pad_add_fusion.idx_ref, bf16[20,3,128,128]{3,2,1,0:T(8,128)(2,1)S(1)} %get-tuple-element.17.full_ref, f32[20,3,16,8,128]{4,3,2,1,0:T(8,128)S(1)} %get-tuple-element.18.turned_ref, f32[16,3,32,128]{3,2,1,0:T(8,128)S(1)} %get-tuple-element.19.first_ref, ...), custom_call_target="tpu_custom_call" | custom-call | flops 3221225472 | bytes 1048576 | tf_op jit(solution)/shard_map/project/pallas_call | solution.py:265
  51.3 0.2 collective-permute-done.10
  51.6 0.5 collective-permute-done.9
  52.2 2.6 %project.9 = (f32[1,272,128]{2,1,0:T(8,128)S(1)}, f32[1,256,128]{2,1,0:T(8,128)S(1)}) custom-call(s32[2]{0:T(128)S(1)} %pad_add_fusion.idx_ref, bf16[20,3,128,128]{3,2,1,0:T(8,128)(2,1)S(1)} %get-tuple-element.17.full_ref, f32[20,3,16,8,128]{4,3,2,1,0:T(8,128)S(1)} %get-tuple-element.18.turned_ref, f32[16,3,32,128]{3,2,1,0:T(8,128)S(1)} %get-tuple-element.19.first_ref, ...), custom_call_target="tpu_custom_call" | custom-call | flops 3221225472 | bytes 1048576 | tf_op jit(solution)/shard_map/project/pallas_call | solution.py:265
  54.8 5.1 %collective-permute-done.11 = bf16[1,528,128]{2,1,0:T(8,128)(2,1)S(1)} collective-permute-done((bf16[1,528,128]{2,1,0:T(8,128)(2,1)S(1)}, bf16[1,528,128]{2,1,0:T(8,128)(2,1)S(1)}, u32[]{:S(2)}, u32[]{:S(2)}) %collective-permute-start.11) | collective-permute-done | bytes 135200 | tf_op jit(solution)/shard_map/ppermute | solution.py:27
  60.0 0.6 slice_multiply_fusion
  60.6 0.7 %maximum_multiply_fusion = f32[16,32,128]{2,1,0:T(8,128)} fusion(f32[8,32,128]{2,1,0:T(8,128)S(1)} %bitcast.17, f32[8,32,128]{2,1,0:T(8,128)S(1)} %bitcast.18), kind=kLoop, calls=%fused_computation.1 | loop fusion | flops 131072 | bytes 524288 | tf_op jit(solution)/shard_map/mul | solution.py:330
  (26 shorter events, 0.9 us)
Async XLA Ops:
  1.9 16.1 %collective-permute-start = (bf16[16,3,32,128]{3,2,1,0:T(8,128)(2,1)S(1)}, bf16[16,3,32,128]{3,2,1,0:T(8,128)(2,1)S(1)}, u32[]{:S(2)}, u32[]{:S(2)}) collective-permute-start(bf16[16,3,32,128]{3,2,1,0:T(8,128)(2,1)S(1)} %bitcast.11), channel_id=1, source_target_pairs={{0,2},{1,3},{2,0},{3,1},{4,6},{5,7},{6,4},{7,5},{8,10},{9,11},{10,... | collective-permute-start | bytes 1179656 | tf_op jit(solution)/shard_map/ppermute | solution.py:27
  5.8 6.4 %collective-permute-start.4 = (bf16[2,3,32,128]{3,2,1,0:T(8,128)(2,1)S(1)}, bf16[2,3,32,128]{3,2,1,0:T(8,128)(2,1)S(1)}, u32[]{:S(2)}, u32[]{:S(2)}) collective-permute-start(bf16[2,3,32,128]{3,2,1,0:T(8,128)(2,1)S(1)} %bitcast.19), channel_id=1, source_target_pairs={{4,0},{8,4},{12,8},{16,12},{20,16},{24,20},{28,24},{0,28},{5,1},{9... | collective-permute-start | bytes 147464 | tf_op jit(solution)/shard_map/ppermute | solution.py:298
  10.5 6.8 %collective-permute-start.3 = (bf16[2,3,32,128]{3,2,1,0:T(8,128)(2,1)S(1)}, bf16[2,3,32,128]{3,2,1,0:T(8,128)(2,1)S(1)}, u32[]{:S(2)}, u32[]{:S(2)}) collective-permute-start(bf16[2,3,32,128]{3,2,1,0:T(8,128)(2,1)S(1)} %bitcast.20), channel_id=1, source_target_pairs={{0,4},{4,8},{8,12},{12,16},{16,20},{20,24},{24,28},{28,0},{1,5},{5... | collective-permute-start | bytes 147464 | tf_op jit(solution)/shard_map/ppermute | solution.py:297
  17.3 4.7 %collective-permute-start.5 = (bf16[1,4,3,32,128]{4,3,2,1,0:T(8,128)(2,1)S(1)}, bf16[1,4,3,32,128]{4,3,2,1,0:T(8,128)(2,1)S(1)}, u32[]{:S(2)}, u32[]{:S(2)}) collective-permute-start(bf16[1,4,3,32,128]{4,3,2,1,0:T(8,128)(2,1)S(1)} %maximum_bitcast_fusion), channel_id=1, source_target_pairs={{0,2},{1,3},{2,0},{3,1},{4,6},{5,7},{6,4},{7,5},{8,10},{9,11},{10,... | collective-permute-start | bytes 294920 | tf_op jit(solution)/shard_map/ppermute | solution.py:27
  17.9 5.7 %collective-permute-start.1 = (bf16[16,3,32,128]{3,2,1,0:T(8,128)(2,1)S(1)}, bf16[16,3,32,128]{3,2,1,0:T(8,128)(2,1)S(1)}, u32[]{:S(2)}, u32[]{:S(2)}) collective-permute-start(bf16[16,3,32,128]{3,2,1,0:T(8,128)(2,1)S(1)} %bitcast.12), channel_id=1, source_target_pairs={{0,1},{1,0},{2,3},{3,2},{4,5},{5,4},{6,7},{7,6},{8,9},{9,8},{10,11... | collective-permute-start | bytes 1179656 | tf_op jit(solution)/shard_map/ppermute | solution.py:27
  18.0 5.7 %collective-permute-start.2 = (bf16[16,3,32,128]{3,2,1,0:T(8,128)(2,1)S(1)}, bf16[16,3,32,128]{3,2,1,0:T(8,128)(2,1)S(1)}, u32[]{:S(2)}, u32[]{:S(2)}) collective-permute-start(bf16[16,3,32,128]{3,2,1,0:T(8,128)(2,1)S(1)} %collective-permute-done.refs_1_), channel_id=1, source_target_pairs={{0,1},{1,0},{2,3},{3,2},{4,5},{5,4},{6,7},{7,6},{8,9},{9,8},{10,11... | collective-permute-start | bytes 1179656 | tf_op jit(solution)/shard_map/ppermute | solution.py:27
  22.1 1.5 %collective-permute-start.6 = (bf16[2,4,3,32,128]{4,3,2,1,0:T(8,128)(2,1)S(1)}, bf16[2,4,3,32,128]{4,3,2,1,0:T(8,128)(2,1)S(1)}, u32[]{:S(2)}, u32[]{:S(2)}) collective-permute-start(bf16[2,4,3,32,128]{4,3,2,1,0:T(8,128)(2,1)S(1)} %pad_maximum_fusion.1), channel_id=1, source_target_pairs={{0,1},{1,0},{2,3},{3,2},{4,5},{5,4},{6,7},{7,6},{8,9},{9,8},{10,11... | collective-permute-start | bytes 589832 | tf_op jit(solution)/shard_map/ppermute | solution.py:27
  38.0 8.4 %collective-permute-start.8 = (bf16[4,256,128]{2,1,0:T(8,128)(2,1)S(1)}, bf16[4,256,128]{2,1,0:T(8,128)(2,1)S(1)}, u32[]{:S(2)}, u32[]{:S(2)}) collective-permute-start(bf16[4,256,128]{2,1,0:T(8,128)(2,1)S(1)} %project.6), channel_id=1, source_target_pairs={{0,8},{4,12},{8,0},{12,4},{16,24},{20,28},{24,16},{28,20},{1,9},{5... | collective-permute-start | bytes 786440 | tf_op jit(solution)/shard_map/ppermute | solution.py:27
  38.1 8.8 %collective-permute-start.7 = (bf16[4,272,128]{2,1,0:T(8,128)(2,1)S(1)}, bf16[4,272,128]{2,1,0:T(8,128)(2,1)S(1)}, u32[]{:S(2)}, u32[]{:S(2)}) collective-permute-start(bf16[4,272,128]{2,1,0:T(8,128)(2,1)S(1)} %project.5), channel_id=1, source_target_pairs={{0,4},{4,0},{8,12},{12,8},{16,20},{20,16},{24,28},{28,24},{1,5},{5... | collective-permute-start | bytes 835592 | tf_op jit(solution)/shard_map/ppermute | solution.py:27
  46.5 5.0 %collective-permute-start.10 = (bf16[2,256,128]{2,1,0:T(8,128)(2,1)S(1)}, bf16[2,256,128]{2,1,0:T(8,128)(2,1)S(1)}, u32[]{:S(2)}, u32[]{:S(2)}) collective-permute-start(bf16[2,256,128]{2,1,0:T(8,128)(2,1)S(1)} %pad_maximum_fusion.4), channel_id=1, source_target_pairs={{0,4},{4,0},{8,12},{12,8},{16,20},{20,16},{24,28},{28,24},{1,5},{5... | collective-permute-start | bytes 393224 | tf_op jit(solution)/shard_map/ppermute | solution.py:27
  46.9 5.1 %collective-permute-start.9 = (bf16[2,272,128]{2,1,0:T(8,128)(2,1)S(1)}, bf16[2,272,128]{2,1,0:T(8,128)(2,1)S(1)}, u32[]{:S(2)}, u32[]{:S(2)}) collective-permute-start(bf16[2,272,128]{2,1,0:T(8,128)(2,1)S(1)} %pad_maximum_fusion.2), channel_id=1, source_target_pairs={{0,8},{4,12},{8,0},{12,4},{16,24},{20,28},{24,16},{28,20},{1,9},{5... | collective-permute-start | bytes 417800 | tf_op jit(solution)/shard_map/ppermute | solution.py:27
  52.1 7.8 %collective-permute-start.11 = (bf16[1,528,128]{2,1,0:T(8,128)(2,1)S(1)}, bf16[1,528,128]{2,1,0:T(8,128)(2,1)S(1)}, u32[]{:S(2)}, u32[]{:S(2)}) collective-permute-start(bf16[1,528,128]{2,1,0:T(8,128)(2,1)S(1)} %pad_maximum_fusion.3), channel_id=1, source_target_pairs={{0,16},{4,20},{8,24},{12,28},{16,0},{20,4},{24,8},{28,12},{1,17},{... | collective-permute-start | bytes 405512 | tf_op jit(solution)/shard_map/ppermute | solution.py:27

commit v5 on v4

--- a/solution.py
+++ b/solution.py
@@ -37,10 +37,13 @@
     return pieces, masks
 
 
-def gathered_stack(x, axis):
+def gathered_stack(x, axis, behind):
     stack, mask = x[None], lax.axis_size(axis) // 2
     while mask:
-        stack = jnp.concatenate([stack, swap(stack, axis, mask)], 0)
+        got = swap(stack, axis, mask)
+        if behind is not None:
+            stack, got, behind = *lax.optimization_barrier((stack, got, behind))[:2], None
+        stack = jnp.concatenate([stack, got], 0)
         mask //= 2
     return stack
 
@@ -62,9 +65,11 @@
 def prepare_kernel(plan, masks, cells_z, repeat, idx_ref, *refs):
     copies, interior = plan
     pieces = len(masks)
-    edges_ref = refs[pieces]
-    sources = (refs[:pieces], [edges_ref.at[q] for q in range(pieces)])
-    full_ref, turned_ref, first_ref, grad_ref, visc_ref, slope_ref, every_ref, mine_ref = refs[pieces + 1:]
+    extra = 1 if any(source for source, *_ in copies) else 0
+    sources = [refs[:pieces]]
+    if extra:
+        sources.append([refs[pieces].at[q] for q in range(pieces)])
+    full_ref, turned_ref, first_ref, grad_ref, visc_ref, slope_ref, every_ref, mine_ref = refs[pieces + extra:]
     rows, comps, lanes, width = full_ref.shape
     part = lanes // pieces
     me = idx_ref[0]
@@ -137,11 +142,15 @@
     return 1 - stage if part == 1 and stage < 2 else stage
 
 
-def main_kernel(plan, own, stage, parts, idx_ref, full_ref, turned_ref, first_ref, grad_ref, visc_ref, *out_refs):
-    interior = [r for start, stop in plan[1] for r in range(start, stop)]
-    _, comps, lanes, width = full_ref.shape
+def main_kernel(plans, own, stage, parts, prior, viscous, earlier, idx_ref, *refs):
+    states = [refs[5 * n:5 * n + 5] for n in range(len(plans))]
+    prior_refs = refs[5 * len(plans):5 * len(plans) + (len(parts) if prior else 0)]
+    out_refs = refs[len(refs) - len(parts):]
+    visc_refs = [state[4] for state in states] + list(refs[len(refs) - len(parts) - earlier:len(refs) - len(parts)])
+    rows_of = [[r for start, stop in plan[1] for r in range(start, stop)] for plan in plans]
+    _, comps, lanes, width = states[0][0].shape
     i_block, i_part = parts[0][2], parts[0][3]
-    tile = grad_ref.shape[3]
+    tile = states[0][3].shape[3]
     joint = tile // own
     me = idx_ref[1]
     depth = comps * lanes
@@ -157,7 +166,8 @@
                 return row // 8 + (i % i_part) // 8, i % 8
             return row // 8, (part * i_part) % 8 + i % i_part
 
-        def pairs(x, i):
+        def pairs(state, interior, x, i):
+            _, turned_ref, first_ref, grad_ref, _ = state
             pieces = []
             for lane in range(0, lanes, 128):
                 cut = slice(lane, lane + 128)
@@ -184,48 +194,58 @@
             return [pieces[l][b] for b in range(comps) for l in range(lanes // 128)]
 
         total = None
-        for first in range(0, len(interior), K_ROWS):
-            count = min(K_ROWS, len(interior) - first)
-            left = jnp.concatenate([
-                jnp.concatenate([p for x in range(first, first + count) for p in pairs(x, i)], 1)
-                for i in range(0, len(jobs) * i_part, joint)
-            ], 0)
-            right = full_ref[interior[first]:interior[first] + count].reshape(count * depth, width)
-            term = jnp.dot(left, right, preferred_element_type=F32)
-            total = term if total is None else total + term
+        for state, interior in zip(states, rows_of):
+            for first in range(0, len(interior), K_ROWS):
+                count = min(K_ROWS, len(interior) - first)
+                left = jnp.concatenate([
+                    jnp.concatenate(
+                        [p for x in range(first, first + count) for p in pairs(state, interior, x, i)], 1
+                    )
+                    for i in range(0, len(jobs) * i_part, joint)
+                ], 0)
+                right = state[0][interior[first]:interior[first] + count].reshape(count * depth, width)
+                term = jnp.dot(left, right, preferred_element_type=F32)
+                total = term if total is None else total + term
         return total.reshape(len(jobs), i_part * own, width)
 
     jobs = [(part, j) for part, count, _, _ in parts for j in range(count)]
     at_once = group_rows(lanes) // i_part
+
+    def put(n, low, value):
+        if prior:
+            value = value + prior_refs[n][pl.ds(low, value.shape[0])]
+        out_refs[n][pl.ds(low, value.shape[0]), :i_part * own] = value.astype(out_refs[n].dtype)
+
     if len(jobs) <= at_once:
         value, at = group(jobs), 0
-        for (part, count, _, _), ref in zip(parts, out_refs):
-            ref[:, :i_part * own] = value[at:at + count].astype(ref.dtype)
+        for n, (_, count, _, _) in enumerate(parts):
+            put(n, 0, value[at:at + count])
             at += count
     else:
-        for (part, count, _, _), ref in zip(parts, out_refs):
+        for n, (part, count, _, _) in enumerate(parts):
             size = min(at_once, count)
 
-            def one(step, carry, part=part, ref=ref, size=size):
+            def one(step, carry, n=n, part=part, size=size):
                 low = step * size
-                value = group([(part, low + j) for j in range(size)])
-                ref[pl.ds(low, size), :i_part * own] = value.astype(ref.dtype)
+                put(n, low, group([(part, low + j) for j in range(size)]))
                 return carry
 
             lax.fori_loop(0, count // size, one, 0)
-    for (part, count, _, _), ref in zip(parts, out_refs):
-        if part == 0:
+    for (part, count, _, _), out_ref in zip(parts, out_refs):
+        if part == 0 and viscous:
             for j in range(count):
                 dest = me ^ code(part, j)
-                rows = visc_ref[pl.ds(pl.multiple_of(dest * i_block, i_block), i_block), :]
+                block = pl.ds(pl.multiple_of(dest * i_block, i_block), i_block)
+                rows = sum(ref[block, :] for ref in visc_refs)
                 rows = jnp.concatenate([rows, jnp.zeros((i_block, width - own), F32)], 1)
-                fill = ref.shape[1] - i_part * own - i_block
+                fill = out_ref.shape[1] - i_part * own - i_block
                 if fill:
                     rows = jnp.concatenate([rows, jnp.zeros((fill, width), F32)], 0)
-                ref[j, i_part * own:] = rows.astype(ref.dtype)
+                out_ref[j, i_part * own:] = rows.astype(out_ref.dtype)
 
 
 def prepare(plan, masks, cells_z, idx, sources, edges, own):
+    operands = list(sources) + ([] if edges is None else [edges])
     copies, interior = plan
     rows = max(at + stop - start for _, start, stop, at in copies)
     count = sum(stop - start for start, stop in interior)
@@ -242,7 +262,7 @@
             jax.ShapeDtypeStruct((count, comps - 1, comps, tile, lanes), BF16),
             jax.ShapeDtypeStruct((width, own), F32),
         ),
-        in_specs=[SMEM] + [VMEM] * (len(sources) + 1),
+        in_specs=[SMEM] + [VMEM] * len(operands),
         out_specs=(VMEM,) * 5,
         scratch_shapes=[
             pltpu.VMEM((comps, comps, width // 8, 8, lanes), F32),
@@ -251,26 +271,29 @@
         ],
         compiler_params=pltpu.CompilerParams(vmem_limit_bytes=vmem_limit(lanes)),
         name="prepare",
-    )(idx, *sources, edges)
-
-
-def project(plan, stage, parts, idx, state, own, peers, dtype):
-    full, turned, first, grad, visc = state
-    _, comps, lanes, width = full.shape
+    )(idx, *operands)
+
+
+def project(plans, stage, parts, idx, states, own, peers, dtype, prior=(), viscous=True, earlier=()):
+    _, comps, lanes, width = states[0][0].shape
     i_block = width // peers
     i_part = i_block // PARTS
     count = 1 if stage is None else peers >> (stage + 1)
-    sizes = [i_part * own + (max(16, i_block) if part == 0 else 0) for part in parts]
-    flops = 2 * len(parts) * count * i_part * own * grad.shape[0] * comps * lanes * width
+    sizes = [i_part * own + (max(16, i_block) if part == 0 and viscous else 0) for part in parts]
+    depth = sum(state[3].shape[0] for state in states) * comps * lanes
+    flops = 2 * len(parts) * count * i_part * own * depth * width
+    layout = [(part, count, i_block, i_part) for part in parts]
+    operands = [array for state in states for array in state] + list(prior)
+    operands += [state[4] for state in earlier]
     return pl.pallas_call(
-        functools.partial(main_kernel, plan, own, stage, [(part, count, i_block, i_part) for part in parts]),
+        functools.partial(main_kernel, plans, own, stage, layout, bool(prior), viscous, len(earlier)),
         out_shape=[jax.ShapeDtypeStruct((count, rows, width), dtype) for rows in sizes],
-        in_specs=[SMEM] + [VMEM] * 5,
+        in_specs=[SMEM] + [VMEM] * len(operands),
         out_specs=[VMEM] * len(parts),
         compiler_params=pltpu.CompilerParams(vmem_limit_bytes=vmem_limit(lanes)),
         cost_estimate=pl.CostEstimate(flops=4 * flops, bytes_accessed=2**20, transcendentals=0),
         name="project",
-    )(idx, full, turned, first, grad, visc)
+    )(idx, *operands)
 
 
 def arrived(results, part, code):
@@ -293,24 +316,36 @@
     block = modes.transpose(0, 3, 1, 2, 4).reshape(cells_x, comps, cells_y * cells_z, width)
     up = [(i, (i + 1) % peers_x) for i in range(peers_x)]
     down = [(j, i) for i, j in up]
-    pieces, masks = gathered(block, "gy")
+    quarter = cells_x // 4
+    middle = block[quarter - 2:cells_x - quarter + 2]
+    pieces, masks = gathered(middle, "gy")
     before = lax.ppermute(block[-2:], "gx", up)
     after = lax.ppermute(block[:2], "gx", down)
-    edges = gathered_stack(jnp.concatenate([before, after], 0), "gy")
-    plan = (
-        ((0, 0, cells_x, 2), (1, 0, 2, 0), (1, 2, 4, cells_x + 2)),
-        ((2, cells_x + 2),),
+    length = middle.shape[0]
+    plans = (
+        (((0, 0, length, 0),), ((2, length - 2),)),
+        (
+            ((1, 0, quarter, 0), (0, 0, 4, quarter), (0, length - 4, length, quarter + 4),
+             (1, quarter, 2 * quarter, quarter + 8)),
+            ((2, quarter + 2), (quarter + 6, 2 * quarter + 6)),
+        ),
     )
-    state = prepare(plan, masks, cells_z, idx, pieces, edges, own)
     stages = peers_x.bit_length() - 1
     both = tuple(range(PARTS))
     results = [[], []]
+    states = [prepare(plans[0], masks, cells_z, idx, pieces, None, own)]
+    rim = gathered_stack(
+        jnp.concatenate([before, block[:quarter - 2], block[cells_x - quarter + 2:], after], 0),
+        "gy", states[0][4],
+    )
+    begun = project(plans[:1], 0, both, idx, states, own, peers_x, F32, viscous=False)
+    states.append(prepare(plans[1], masks, cells_z, idx, pieces, rim, own))
+    sends = project(plans[1:], 0, both, idx, states[1:], own, peers_x, BF16, prior=begun, earlier=states[:1])
     for part in both:
-        (send,) = project(plan, 0, (part,), idx, state, own, peers_x, BF16)
-        results[part].append(swap(send, "gx", 1 << bit_of(part, 0)))
-        idx, send = lax.optimization_barrier((idx, send))
+        results[part].append(swap(sends[part], "gx", 1 << bit_of(part, 0)))
+    idx, sends = lax.optimization_barrier((idx, sends))
     for stage in range(1, stages):
-        kept = project(plan, stage, both, idx, state, own, peers_x, F32)
+        kept = project(plans, stage, both, idx, states, own, peers_x, F32)
         sums = [
             jnp.stack([kept[part][j] + arrived(results[part], part, code_of(part, stage, j))
                        for j in range(kept[part].shape[0])]).astype(BF16)
@@ -325,7 +360,7 @@
         for part in both:
             results[part].append(got[part])
         idx, sums = lax.optimization_barrier((idx, sums))
-    kept = project(plan, None, both, idx, state, own, peers_x, F32)
+    kept = project(plans, None, both, idx, states, own, peers_x, F32)
     finals = [kept[part][0] + arrived(results[part], part, 0) for part in both]
     convective = jnp.concatenate(
         [f[:i_part * own].reshape(i_part, own, width) for f in finals], 0

time: 61.6 us -> 60.7 us (0.985)
  waiting for transfers between devices: 21.3 us -> 19.7 us
  Pallas kernels: 24.4 us -> 25.1 us
    slice x1 -> x3, local copies, waits for them, and re-layouts: 0.04 us -> 1.41 us  [the longest x2 1.37 us: body(): middle = block[quarter - 2:cells_x - quarter + 2]]
    ppermute x1, waiting for transfers between devices: 1.65 us -> 0.29 us  [body(): after = lax.ppermute(block[:2], 'gx', down)]
    transpose x1 -> x0, local copies, waits for them, and re-layouts: 1.27 us -> none  [body(): modes.transpose(0, 3, 1, 2, 4)]
    pallas_call x1 -> x2, Pallas kernels: 5.5 us -> 6.39 us  [prepare(): pl.pallas_call(functools.partial(prepare_kernel, plan, masks, cells_z, ti...]
  transfers between devices with their start and end apart: 12 -> 12, of which waited for: 9 -> 8; matrix products, arithmetic and copies ran while one was open for 2% -> 2% of each run, Pallas kernels for 16% -> 28%
where the time goes in v5:
time: 60.7 us; the launch traced here: 60.5 us
  Pallas kernels  25.1 us (41%)
  waiting for transfers between devices  19.7 us (32%)
  starting transfers between devices  10.7 us (18%)
  local copies, waits for them, and re-layouts  2.35 us (4%)
  other arithmetic  1.78 us (3%)
  between operations  0.83 us (1%)
    pallas_call x5, Pallas kernels, project(): pl.pallas_call(functools.partial(main_kernel, plans, own, stage, layout,...  18.7 us
    ppermute x10, waiting for transfers between devices, swap(): lax.ppermute(x, axis, [(i, i ^ mask) for i in range(lax.axis_size(axis))])  14.3 us
    pallas_call x2, Pallas kernels, prepare(): pl.pallas_call(functools.partial(prepare_kernel, plan, masks, cells_z, ti...  6.39 us
    ppermute x10, starting transfers between devices, swap(): lax.ppermute(x, axis, [(i, i ^ mask) for i in range(lax.axis_size(axis))])  6.04 us
    ppermute x1, waiting for transfers between devices, body(): before = lax.ppermute(block[-2:], 'gx', up)  5.13 us
    ppermute x1, starting transfers between devices, body(): after = lax.ppermute(block[:2], 'gx', down)  4.61 us
    slice x2, local copies, waits for them, and re-layouts, body(): middle = block[quarter - 2:cells_x - quarter + 2]  1.37 us
  transfers between devices with their start and end apart: 12, of which 8 were waited for; matrix products, arithmetic and copies ran while one was open for 2% of the time, Pallas kernels for 28%

profile of v5, /device:TPU:0, one launch (start us, length us, event | category | flops | bytes accessed | tf_op | source)
XLA Modules:
  0.0 60.5 jit_solution(15886679821672992424)
XLA Ops:
  0.6 1.2 %slice.107 = bf16[12,3,16,2,128]{4,3,1,2,0:T(2,128)(2,1)S(1)} slice(bf16[16,3,16,2,128]{4,3,1,2,0:T(2,128)(2,1)} %bitcast.18), slice={[2:14], [0:3], [0:16], [0:2], [0:128]} | slice | bytes 589824 | tf_op jit(solution)/shard_map/slice | solution.py:320
  2.0 3.0 %collective-permute-start = (bf16[12,3,32,128]{3,2,1,0:T(8,128)(2,1)S(1)}, bf16[12,3,32,128]{3,2,1,0:T(8,128)(2,1)S(1)}, u32[]{:S(2)}, u32[]{:S(2)}) collective-permute-start(bf16[12,3,32,128]{3,2,1,0:T(8,128)(2,1)S(1)} %bitcast.11), channel_id=1, source_target_pairs={{0,2},{1,3},{2,0},{3,1},{4,6},{5,7},{6,4},{7,5},{8,10},{9,11},{10,... | collective-permute-start | bytes 884744 | tf_op jit(solution)/shard_map/ppermute | solution.py:27
  5.0 0.9 %fusion = (bf16[2,3,16,2,128]{4,3,1,2,0:T(2,128)(2,1)S(1)}, bf16[2,3,16,2,128]{4,3,1,2,0:T(2,128)(2,1)S(1)}) fusion(bf16[16,3,16,2,128]{4,3,1,2,0:T(2,128)(2,1)} %bitcast.19), kind=kLoop, calls=%fused_computation.17 | loop fusion | bytes 196608 | tf_op jit(solution)/shard_map/slice | solution.py:322
  6.0 4.6 %collective-permute-start.4 = (bf16[2,3,32,128]{3,2,1,0:T(8,128)(2,1)S(1)}, bf16[2,3,32,128]{3,2,1,0:T(8,128)(2,1)S(1)}, u32[]{:S(2)}, u32[]{:S(2)}) collective-permute-start(bf16[2,3,32,128]{3,2,1,0:T(8,128)(2,1)S(1)} %bitcast.20), channel_id=1, source_target_pairs={{4,0},{8,4},{12,8},{16,12},{20,16},{24,20},{28,24},{0,28},{5,1},{9... | collective-permute-start | bytes 147464 | tf_op jit(solution)/shard_map/ppermute | solution.py:323
  10.8 1.3 %collective-permute-done.refs_1_ = bf16[12,3,32,128]{3,2,1,0:T(8,128)(2,1)S(1)} collective-permute-done((bf16[12,3,32,128]{3,2,1,0:T(8,128)(2,1)S(1)}, bf16[12,3,32,128]{3,2,1,0:T(8,128)(2,1)S(1)}, u32[]{:S(2)}, u32[]{:S(2)}) %collective-permute-start) | collective-permute-done | bytes 294944 | tf_op jit(solution)/shard_map/ppermute | solution.py:27
  12.0 0.3 collective-permute-done.4
  12.3 5.1 %collective-permute-done.3 = bf16[2,3,32,128]{3,2,1,0:T(8,128)(2,1)S(1)} collective-permute-done((bf16[2,3,32,128]{3,2,1,0:T(8,128)(2,1)S(1)}, bf16[2,3,32,128]{3,2,1,0:T(8,128)(2,1)S(1)}, u32[]{:S(2)}, u32[]{:S(2)}) %collective-permute-start.3) | collective-permute-done | bytes 49184 | tf_op jit(solution)/shard_map/ppermute | solution.py:322
  17.5 0.6 collective-permute-start.5
  18.2 3.2 %prepare.2 = (bf16[12,3,128,128]{3,2,1,0:T(8,128)(2,1)S(1)}, f32[12,3,16,8,128]{4,3,2,1,0:T(8,128)S(1)}, f32[8,3,32,128]{3,2,1,0:T(8,128)S(1)}, bf16[8,2,3,32,128]{4,3,2,1,0:T(8,128)(2,1)S(1)}, f32[128,32]{1,0:T(8,128)S(1)}) custom-call(s32[2]{0:T(128)S(1)} %pad_add_fusion.idx_ref, bf16[12,3,32,128]{3,2,1,0:T(8,128)(2,1)S(1)} %bitcast.13, ...), custom_call_target="tpu_custom_call" | custom-call | tf_op jit(solution)/shard_map/prepare/pallas_call | solution.py:256
  21.4 1.8 %collective-permute-done.5 = bf16[1,8,3,32,128]{4,3,2,1,0:T(8,128)(2,1)S(1)} collective-permute-done((bf16[1,8,3,32,128]{4,3,2,1,0:T(8,128)(2,1)S(1)}, bf16[1,8,3,32,128]{4,3,2,1,0:T(8,128)(2,1)S(1)}, u32[]{:S(2)}, u32[]{:S(2)}) %collective-permute-start.5) | collective-permute-done | bytes 196640 | tf_op jit(solution)/shard_map/ppermute | solution.py:27
  23.3 4.2 %project.5 = (f32[4,256,128]{2,1,0:T(8,128)S(1)}, f32[4,256,128]{2,1,0:T(8,128)S(1)}) custom-call(s32[2]{0:T(128)S(1)} %pad_add_fusion.idx_ref, bf16[12,3,128,128]{3,2,1,0:T(8,128)(2,1)S(1)} %get-tuple-element.35.refs_0_, f32[12,3,16,8,128]{4,3,2,1,0:T(8,128)S(1)} %get-tuple-element.36.refs_1_, f32[8,3,32,128]{3,2,1,0:T(8,128)S(1)} %get-tuple-element.37.refs_2_, ...), custom_call_target="tpu_custom_call" | custom-call | flops 6442450944 | bytes 1048576 | tf_op jit(solution)/shard_map/project/pallas_call | solution.py:288
  27.6 3.2 %prepare.3 = (bf16[16,3,128,128]{3,2,1,0:T(8,128)(2,1)S(1)}, f32[16,3,16,8,128]{4,3,2,1,0:T(8,128)S(1)}, f32[8,3,32,128]{3,2,1,0:T(8,128)S(1)}, bf16[8,2,3,32,128]{4,3,2,1,0:T(8,128)(2,1)S(1)}, f32[128,32]{1,0:T(8,128)S(1)}) custom-call(s32[2]{0:T(128)S(1)} %pad_add_fusion.idx_ref, bf16[12,3,32,128]{3,2,1,0:T(8,128)(2,1)S(1)} %bitcast.14, ...), custom_call_target="tpu_custom_call" | custom-call | tf_op jit(solution)/shard_map/prepare/pallas_call | solution.py:256
  30.8 4.8 %project.6 = (bf16[4,272,128]{2,1,0:T(8,128)(2,1)S(1)}, bf16[4,256,128]{2,1,0:T(8,128)(2,1)S(1)}) custom-call(s32[2]{0:T(128)S(1)} %pad_add_fusion.idx_ref, bf16[16,3,128,128]{3,2,1,0:T(8,128)(2,1)S(1)} %get-tuple-element.30.refs_0_.refs_5_, f32[16,3,16,8,128]{4,3,2,1,0:T(8,128)S(1)} %get-tuple-element.31.refs_1_.refs_6_, ...), custom_call_target="tpu_custom_call" | custom-call | flops 6442450944 | bytes 1048576 | tf_op jit(solution)/shard_map/project/pallas_call | solution.py:288
  35.7 4.5 %project.7 = (f32[2,272,128]{2,1,0:T(8,128)S(1)}, f32[2,256,128]{2,1,0:T(8,128)S(1)}) custom-call(s32[2]{0:T(128)S(1)} %pad_add_fusion.idx_ref, bf16[12,3,128,128]{3,2,1,0:T(8,128)(2,1)S(1)} %get-tuple-element.35.refs_0_, f32[12,3,16,8,128]{4,3,2,1,0:T(8,128)S(1)} %get-tuple-element.36.refs_1_, f32[8,3,32,128]{3,2,1,0:T(8,128)S(1)} %get-tuple-element.37.refs_2_, ...), custom_call_target="tpu_custom_call" | custom-call | flops 6442450944 | bytes 1048576 | tf_op jit(solution)/shard_map/project/pallas_call | solution.py:288
  40.2 4.2 %collective-permute-done.8 = bf16[4,256,128]{2,1,0:T(8,128)(2,1)S(1)} collective-permute-done((bf16[4,256,128]{2,1,0:T(8,128)(2,1)S(1)}, bf16[4,256,128]{2,1,0:T(8,128)(2,1)S(1)}, u32[]{:S(2)}, u32[]{:S(2)}) %collective-permute-start.8) | collective-permute-done | bytes 262176 | tf_op jit(solution)/shard_map/ppermute | solution.py:27
  44.5 1.7 %collective-permute-start.10 = (bf16[2,256,128]{2,1,0:T(8,128)(2,1)S(1)}, bf16[2,256,128]{2,1,0:T(8,128)(2,1)S(1)}, u32[]{:S(2)}, u32[]{:S(2)}) collective-permute-start(bf16[2,256,128]{2,1,0:T(8,128)(2,1)S(1)} %pad_maximum_fusion.4), channel_id=1, source_target_pairs={{0,4},{4,0},{8,12},{12,8},{16,20},{20,16},{24,28},{28,24},{1,5},{5... | collective-permute-start | bytes 393224 | tf_op jit(solution)/shard_map/ppermute | solution.py:27
  46.3 0.3 collective-permute-start.9
  46.6 2.6 %project.8 = (f32[1,272,128]{2,1,0:T(8,128)S(1)}, f32[1,256,128]{2,1,0:T(8,128)S(1)}) custom-call(s32[2]{0:T(128)S(1)} %pad_add_fusion.idx_ref, bf16[12,3,128,128]{3,2,1,0:T(8,128)(2,1)S(1)} %get-tuple-element.35.refs_0_, f32[12,3,16,8,128]{4,3,2,1,0:T(8,128)S(1)} %get-tuple-element.36.refs_1_, f32[8,3,32,128]{3,2,1,0:T(8,128)S(1)} %get-tuple-element.37.refs_2_, ...), custom_call_target="tpu_custom_call" | custom-call | flops 3221225472 | bytes 1048576 | tf_op jit(solution)/shard_map/project/pallas_call | solution.py:288
  49.3 0.4 collective-permute-done.10
  49.7 1.7 %collective-permute-done.9 = bf16[2,272,128]{2,1,0:T(8,128)(2,1)S(1)} collective-permute-done((bf16[2,272,128]{2,1,0:T(8,128)(2,1)S(1)}, bf16[2,272,128]{2,1,0:T(8,128)(2,1)S(1)}, u32[]{:S(2)}, u32[]{:S(2)}) %collective-permute-start.9) | collective-permute-done | bytes 139296 | tf_op jit(solution)/shard_map/ppermute | solution.py:27
  51.5 2.6 %project.9 = (f32[1,272,128]{2,1,0:T(8,128)S(1)}, f32[1,256,128]{2,1,0:T(8,128)S(1)}) custom-call(s32[2]{0:T(128)S(1)} %pad_add_fusion.idx_ref, bf16[12,3,128,128]{3,2,1,0:T(8,128)(2,1)S(1)} %get-tuple-element.35.refs_0_, f32[12,3,16,8,128]{4,3,2,1,0:T(8,128)S(1)} %get-tuple-element.36.refs_1_, f32[8,3,32,128]{3,2,1,0:T(8,128)S(1)} %get-tuple-element.37.refs_2_, ...), custom_call_target="tpu_custom_call" | custom-call | flops 3221225472 | bytes 1048576 | tf_op jit(solution)/shard_map/project/pallas_call | solution.py:288
  54.2 4.9 %collective-permute-done.11 = bf16[1,528,128]{2,1,0:T(8,128)(2,1)S(1)} collective-permute-done((bf16[1,528,128]{2,1,0:T(8,128)(2,1)S(1)}, bf16[1,528,128]{2,1,0:T(8,128)(2,1)S(1)}, u32[]{:S(2)}, u32[]{:S(2)}) %collective-permute-start.11) | collective-permute-done | bytes 135200 | tf_op jit(solution)/shard_map/ppermute | solution.py:27
  59.1 0.6 slice_multiply_fusion
  59.8 0.7 %maximum_multiply_fusion = f32[16,32,128]{2,1,0:T(8,128)} fusion(f32[8,32,128]{2,1,0:T(8,128)S(1)} %bitcast.16, f32[8,32,128]{2,1,0:T(8,128)S(1)} %bitcast.17), kind=kLoop, calls=%fused_computation.2 | loop fusion | flops 131072 | bytes 524288 | tf_op jit(solution)/shard_map/mul | solution.py:365
  (28 shorter events, 1.2 us)
Async XLA Ops:
  2.0 10.0 %collective-permute-start = (bf16[12,3,32,128]{3,2,1,0:T(8,128)(2,1)S(1)}, bf16[12,3,32,128]{3,2,1,0:T(8,128)(2,1)S(1)}, u32[]{:S(2)}, u32[]{:S(2)}) collective-permute-start(bf16[12,3,32,128]{3,2,1,0:T(8,128)(2,1)S(1)} %bitcast.11), channel_id=1, source_target_pairs={{0,2},{1,3},{2,0},{3,1},{4,6},{5,7},{6,4},{7,5},{8,10},{9,11},{10,... | collective-permute-start | bytes 884744 | tf_op jit(solution)/shard_map/ppermute | solution.py:27
  6.0 6.4 %collective-permute-start.4 = (bf16[2,3,32,128]{3,2,1,0:T(8,128)(2,1)S(1)}, bf16[2,3,32,128]{3,2,1,0:T(8,128)(2,1)S(1)}, u32[]{:S(2)}, u32[]{:S(2)}) collective-permute-start(bf16[2,3,32,128]{3,2,1,0:T(8,128)(2,1)S(1)} %bitcast.20), channel_id=1, source_target_pairs={{4,0},{8,4},{12,8},{16,12},{20,16},{24,20},{28,24},{0,28},{5,1},{9... | collective-permute-start | bytes 147464 | tf_op jit(solution)/shard_map/ppermute | solution.py:323
  10.6 6.8 %collective-permute-start.3 = (bf16[2,3,32,128]{3,2,1,0:T(8,128)(2,1)S(1)}, bf16[2,3,32,128]{3,2,1,0:T(8,128)(2,1)S(1)}, u32[]{:S(2)}, u32[]{:S(2)}) collective-permute-start(bf16[2,3,32,128]{3,2,1,0:T(8,128)(2,1)S(1)} %bitcast.22), channel_id=1, source_target_pairs={{0,4},{4,8},{8,12},{12,16},{16,20},{20,24},{24,28},{28,0},{1,5},{5... | collective-permute-start | bytes 147464 | tf_op jit(solution)/shard_map/ppermute | solution.py:322
  10.7 7.5 %collective-permute-start.1 = (bf16[12,3,32,128]{3,2,1,0:T(8,128)(2,1)S(1)}, bf16[12,3,32,128]{3,2,1,0:T(8,128)(2,1)S(1)}, u32[]{:S(2)}, u32[]{:S(2)}) collective-permute-start(bf16[12,3,32,128]{3,2,1,0:T(8,128)(2,1)S(1)} %bitcast.12), channel_id=1, source_target_pairs={{0,1},{1,0},{2,3},{3,2},{4,5},{5,4},{6,7},{7,6},{8,9},{9,8},{10,11... | collective-permute-start | bytes 884744 | tf_op jit(solution)/shard_map/ppermute | solution.py:27
  12.0 6.1 %collective-permute-start.2 = (bf16[12,3,32,128]{3,2,1,0:T(8,128)(2,1)S(1)}, bf16[12,3,32,128]{3,2,1,0:T(8,128)(2,1)S(1)}, u32[]{:S(2)}, u32[]{:S(2)}) collective-permute-start(bf16[12,3,32,128]{3,2,1,0:T(8,128)(2,1)S(1)} %collective-permute-done.refs_1_), channel_id=1, source_target_pairs={{0,1},{1,0},{2,3},{3,2},{4,5},{5,4},{6,7},{7,6},{8,9},{9,8},{10,11... | collective-permute-start | bytes 884744 | tf_op jit(solution)/shard_map/ppermute | solution.py:27
  17.5 5.7 %collective-permute-start.5 = (bf16[1,8,3,32,128]{4,3,2,1,0:T(8,128)(2,1)S(1)}, bf16[1,8,3,32,128]{4,3,2,1,0:T(8,128)(2,1)S(1)}, u32[]{:S(2)}, u32[]{:S(2)}) collective-permute-start(bf16[1,8,3,32,128]{4,3,2,1,0:T(8,128)(2,1)S(1)} %maximum_bitcast_fusion), channel_id=1, source_target_pairs={{0,2},{1,3},{2,0},{3,1},{4,6},{5,7},{6,4},{7,5},{8,10},{9,11},{10,... | collective-permute-start | bytes 589832 | tf_op jit(solution)/shard_map/ppermute | solution.py:27
  23.3 4.3 %collective-permute-start.6 = (bf16[2,8,3,32,128]{4,3,2,1,0:T(8,128)(2,1)S(1)}, bf16[2,8,3,32,128]{4,3,2,1,0:T(8,128)(2,1)S(1)}, u32[]{:S(2)}, u32[]{:S(2)}) collective-permute-start(bf16[2,8,3,32,128]{4,3,2,1,0:T(8,128)(2,1)S(1)} %pad_maximum_fusion.1), channel_id=1, source_target_pairs={{0,1},{1,0},{2,3},{3,2},{4,5},{5,4},{6,7},{7,6},{8,9},{9,8},{10,11... | collective-permute-start | bytes 1179656 | tf_op jit(solution)/shard_map/ppermute | solution.py:27
  35.6 10.6 %collective-permute-start.7 = (bf16[4,272,128]{2,1,0:T(8,128)(2,1)S(1)}, bf16[4,272,128]{2,1,0:T(8,128)(2,1)S(1)}, u32[]{:S(2)}, u32[]{:S(2)}) collective-permute-start(bf16[4,272,128]{2,1,0:T(8,128)(2,1)S(1)} %get-tuple-element.41), channel_id=1, source_target_pairs={{0,4},{4,0},{8,12},{12,8},{16,20},{20,16},{24,28},{28,24},{1,5},{5... | collective-permute-start | bytes 835592 | tf_op jit(solution)/shard_map/ppermute | solution.py:27
  35.6 8.8 %collective-permute-start.8 = (bf16[4,256,128]{2,1,0:T(8,128)(2,1)S(1)}, bf16[4,256,128]{2,1,0:T(8,128)(2,1)S(1)}, u32[]{:S(2)}, u32[]{:S(2)}) collective-permute-start(bf16[4,256,128]{2,1,0:T(8,128)(2,1)S(1)} %get-tuple-element.42), channel_id=1, source_target_pairs={{0,8},{4,12},{8,0},{12,4},{16,24},{20,28},{24,16},{28,20},{1,9},{5... | collective-permute-start | bytes 786440 | tf_op jit(solution)/shard_map/ppermute | solution.py:27
  44.5 5.2 %collective-permute-start.10 = (bf16[2,256,128]{2,1,0:T(8,128)(2,1)S(1)}, bf16[2,256,128]{2,1,0:T(8,128)(2,1)S(1)}, u32[]{:S(2)}, u32[]{:S(2)}) collective-permute-start(bf16[2,256,128]{2,1,0:T(8,128)(2,1)S(1)} %pad_maximum_fusion.4), channel_id=1, source_target_pairs={{0,4},{4,0},{8,12},{12,8},{16,20},{20,16},{24,28},{28,24},{1,5},{5... | collective-permute-start | bytes 393224 | tf_op jit(solution)/shard_map/ppermute | solution.py:27
  46.3 5.1 %collective-permute-start.9 = (bf16[2,272,128]{2,1,0:T(8,128)(2,1)S(1)}, bf16[2,272,128]{2,1,0:T(8,128)(2,1)S(1)}, u32[]{:S(2)}, u32[]{:S(2)}) collective-permute-start(bf16[2,272,128]{2,1,0:T(8,128)(2,1)S(1)} %pad_maximum_fusion.2), channel_id=1, source_target_pairs={{0,8},{4,12},{8,0},{12,4},{16,24},{20,28},{24,16},{28,20},{1,9},{5... | collective-permute-start | bytes 417800 | tf_op jit(solution)/shard_map/ppermute | solution.py:27
  51.4 7.6 %collective-permute-start.11 = (bf16[1,528,128]{2,1,0:T(8,128)(2,1)S(1)}, bf16[1,528,128]{2,1,0:T(8,128)(2,1)S(1)}, u32[]{:S(2)}, u32[]{:S(2)}) collective-permute-start(bf16[1,528,128]{2,1,0:T(8,128)(2,1)S(1)} %pad_maximum_fusion.3), channel_id=1, source_target_pairs={{0,16},{4,20},{8,24},{12,28},{16,0},{20,4},{24,8},{28,12},{1,17},{... | collective-permute-start | bytes 405512 | tf_op jit(solution)/shard_map/ppermute | solution.py:27

commit v6 on v5

--- a/solution.py
+++ b/solution.py
@@ -65,7 +65,7 @@
 def prepare_kernel(plan, masks, cells_z, repeat, idx_ref, *refs):
     copies, interior = plan
     pieces = len(masks)
-    extra = 1 if any(source for source, *_ in copies) else 0
+    extra = 2 if any(source for source, *_ in copies) else 0
     sources = [refs[:pieces]]
     if extra:
         sources.append([refs[pieces].at[q] for q in range(pieces)])
@@ -85,7 +85,12 @@
             turned_ref[row, comp] = flat.reshape(width // 8, 8, lanes)
         return carry
 
-    lax.fori_loop(0, rows, turn, 0, unroll=4)
+    for source, start, stop, at in copies:
+        count = stop - start
+        if extra and source == 0:
+            turned_ref[at:at + count] = refs[pieces + 1][start:stop]
+        else:
+            lax.fori_loop(at, at + count, turn, 0, unroll=count if count % 4 else 4)
     weights = y_and_z_weights(lanes, cells_z)
 
     def slopes(at, slot, row):
@@ -121,7 +126,7 @@
             slopes(at + step, step, start + step)
             return carry
 
-        lax.fori_loop(0, stop - start, one, 0, unroll=4)
+        lax.fori_loop(0, stop - start, one, 0, unroll=5 if (stop - start) % 5 == 0 else min(4, stop - start))
         used = (stop - start) * comps * comps * lanes
         term = lax.dot_general(
             every_ref[:, :used], mine_ref[:, :used], (((1,), (1,)), ((), ())), preferred_element_type=F32
@@ -195,15 +200,18 @@
 
         total = None
         for state, interior in zip(states, rows_of):
-            for first in range(0, len(interior), K_ROWS):
-                count = min(K_ROWS, len(interior) - first)
+            k_rows = K_ROWS if len(interior) % K_ROWS == 0 else 6
+            for first in range(0, len(interior), k_rows):
+                count = min(k_rows, len(interior) - first)
                 left = jnp.concatenate([
                     jnp.concatenate(
                         [p for x in range(first, first + count) for p in pairs(state, interior, x, i)], 1
                     )
                     for i in range(0, len(jobs) * i_part, joint)
                 ], 0)
-                right = state[0][interior[first]:interior[first] + count].reshape(count * depth, width)
+                right = jnp.concatenate(
+                    [state[0][row].reshape(depth, width) for row in interior[first:first + count]], 0
+                )
                 term = jnp.dot(left, right, preferred_element_type=F32)
                 total = term if total is None else total + term
         return total.reshape(len(jobs), i_part * own, width)
@@ -244,8 +252,8 @@
                 out_ref[j, i_part * own:] = rows.astype(out_ref.dtype)
 
 
-def prepare(plan, masks, cells_z, idx, sources, edges, own):
-    operands = list(sources) + ([] if edges is None else [edges])
+def prepare(plan, masks, cells_z, idx, sources, extra, own):
+    operands = list(sources) + list(extra)
     copies, interior = plan
     rows = max(at + stop - start for _, start, stop, at in copies)
     count = sum(stop - start for start, stop in interior)
@@ -305,6 +313,21 @@
     return sum(found)
 
 
+def finish_kernel(scales, parts, *refs):
+    convective_ref, viscous_ref = refs[-2:]
+    i_block, own, width = convective_ref.shape
+    i_part = i_block // parts
+    each = (len(refs) - 2) // parts
+    for part in range(parts):
+        total = refs[part * each][0]
+        for ref in refs[part * each + 1:(part + 1) * each]:
+            total = total + ref[0].astype(F32)
+        rows = total[:i_part * own] * scales[0]
+        convective_ref[part * i_part:(part + 1) * i_part] = rows.reshape(i_part, own, width)
+        if part == 0:
+            viscous_ref[...] = total[i_part * own:i_part * own + i_block, :own] * scales[1]
+
+
 def body(modes):
     cells_x, cells_y, cells_z, comps, width = modes.shape
     peers_x, peers_y = lax.axis_size("gx"), lax.axis_size("gy")
@@ -316,7 +339,7 @@
     block = modes.transpose(0, 3, 1, 2, 4).reshape(cells_x, comps, cells_y * cells_z, width)
     up = [(i, (i + 1) % peers_x) for i in range(peers_x)]
     down = [(j, i) for i, j in up]
-    quarter = cells_x // 4
+    quarter = max(2, cells_x // 5)
     middle = block[quarter - 2:cells_x - quarter + 2]
     pieces, masks = gathered(middle, "gy")
     before = lax.ppermute(block[-2:], "gx", up)
@@ -333,13 +356,13 @@
     stages = peers_x.bit_length() - 1
     both = tuple(range(PARTS))
     results = [[], []]
-    states = [prepare(plans[0], masks, cells_z, idx, pieces, None, own)]
+    states = [prepare(plans[0], masks, cells_z, idx, pieces, (), own)]
     rim = gathered_stack(
         jnp.concatenate([before, block[:quarter - 2], block[cells_x - quarter + 2:], after], 0),
         "gy", states[0][4],
     )
     begun = project(plans[:1], 0, both, idx, states, own, peers_x, F32, viscous=False)
-    states.append(prepare(plans[1], masks, cells_z, idx, pieces, rim, own))
+    states.append(prepare(plans[1], masks, cells_z, idx, pieces, (rim, states[0][1]), own))
     sends = project(plans[1:], 0, both, idx, states[1:], own, peers_x, BF16, prior=begun, earlier=states[:1])
     for part in both:
         results[part].append(swap(sends[part], "gx", 1 << bit_of(part, 0)))
@@ -361,11 +384,18 @@
             results[part].append(got[part])
         idx, sums = lax.optimization_barrier((idx, sums))
     kept = project(plans, None, both, idx, states, own, peers_x, F32)
-    finals = [kept[part][0] + arrived(results[part], part, 0) for part in both]
-    convective = jnp.concatenate(
-        [f[:i_part * own].reshape(i_part, own, width) for f in finals], 0
-    ) * (-1.0 / math.sqrt(total_points))
-    viscous = finals[0][i_part * own:i_part * own + i_block, :own] * (-1.0 / total_points)
+    scales = (-1.0 / math.sqrt(total_points), -1.0 / total_points)
+    blocks = [blocks for part in both for blocks in (kept[part], *results[part])]
+    convective, viscous = pl.pallas_call(
+        functools.partial(finish_kernel, scales, len(both)),
+        out_shape=(
+            jax.ShapeDtypeStruct((i_block, own, width), F32),
+            jax.ShapeDtypeStruct((i_block, own), F32),
+        ),
+        in_specs=[VMEM] * len(blocks),
+        out_specs=(VMEM,) * 2,
+        name="finish",
+    )(*blocks)
     return (convective, viscous)
 
 

time: 60.7 us -> 61.1 us (level)
  waiting for transfers between devices: 19.7 us -> 15.1 us
  local copies, waits for them, and re-layouts: 2.35 us -> 5.81 us
  Pallas kernels: 25.1 us -> 26.6 us
  other arithmetic: 1.78 us -> 0.37 us
  starting transfers between devices: 10.7 us -> 12 us
    ppermute x10, waiting for transfers between devices: 14.3 us -> 11.6 us  [swap(): lax.ppermute(x, axis, [(i, i ^ mask) for i in range(lax.axis_size(axis))])]
    pallas_call x0 -> x1, Pallas kernels: none -> 2 us  [body(): pl.pallas_call(functools.partial(finish_kernel, scales, len(both)), out_s...]
    ppermute x1, waiting for transfers between devices: 5.13 us -> 3.51 us  [body(): before = lax.ppermute(block[-2:], 'gx', up)]
    mul x2 -> x0, other arithmetic: 1.33 us -> none  [the longest x1 0.72 us: body(): jnp.concatenate([f[:i_part * own].reshape(i_part, own, width) for f in fi...]
    unnamed x0 -> x12, local copies, waits for them, and re-layouts: none -> 1.31 us
    slice x1 -> x4, local copies, waits for them, and re-layouts: 0.01 us -> 1.31 us  [the longest x2 1.25 us: body(): got = [joined[:, :rows], joined[:, rows:]]]
    ppermute x10, starting transfers between devices: 6.04 us -> 7.32 us  [swap(): lax.ppermute(x, axis, [(i, i ^ mask) for i in range(lax.axis_size(axis))])]
    slice x1 -> x2, local copies, waits for them, and re-layouts: 0.04 us -> 0.81 us  [body(): block[:quarter - 2]]
  transfers between devices with their start and end apart: 12 -> 12, of which waited for: 8 -> 7; matrix products, arithmetic and copies ran while one was open for 2% -> 3% of each run, Pallas kernels for 28% -> 31%
where the time goes in v6:
time: 61.1 us; the launch traced here: 60.8 us
  Pallas kernels  26.6 us (44%)
  waiting for transfers between devices  15.1 us (25%)
  starting transfers between devices  12 us (20%)
  local copies, waits for them, and re-layouts  5.81 us (10%)
  between operations  0.86 us (1%)
    pallas_call x5, Pallas kernels, project(): pl.pallas_call(functools.partial(main_kernel, plans, own, stage, layout,...  18.7 us
    ppermute x10, waiting for transfers between devices, swap(): lax.ppermute(x, axis, [(i, i ^ mask) for i in range(lax.axis_size(axis))])  11.6 us
    ppermute x10, starting transfers between devices, swap(): lax.ppermute(x, axis, [(i, i ^ mask) for i in range(lax.axis_size(axis))])  7.32 us
    pallas_call x2, Pallas kernels, prepare(): pl.pallas_call(functools.partial(prepare_kernel, plan, masks, cells_z, ti...  5.93 us
    ppermute x1, starting transfers between devices, body(): after = lax.ppermute(block[:2], 'gx', down)  4.61 us
    ppermute x1, waiting for transfers between devices, body(): before = lax.ppermute(block[-2:], 'gx', up)  3.51 us
    pallas_call x1, Pallas kernels, body(): pl.pallas_call(functools.partial(finish_kernel, scales, len(both)), out_s...  2 us
    slice x2, local copies, waits for them, and re-layouts, body(): middle = block[quarter - 2:cells_x - quarter + 2]  1.46 us
  transfers between devices with their start and end apart: 12, of which 7 were waited for; matrix products, arithmetic and copies ran while one was open for 3% of the time, Pallas kernels for 31%

profile of v6, /device:TPU:0, one launch (start us, length us, event | category | flops | bytes accessed | tf_op | source)
XLA Modules:
  0.0 60.8 jit_solution(7757756721640974148)
XLA Ops:
  0.6 1.2 %slice.96 = bf16[14,3,16,2,128]{4,3,1,2,0:T(2,128)(2,1)S(1)} slice(bf16[16,3,16,2,128]{4,3,1,2,0:T(2,128)(2,1)} %bitcast.14), slice={[1:15], [0:3], [0:16], [0:2], [0:128]} | slice | bytes 688128 | tf_op jit(solution)/shard_map/slice | solution.py:343
  2.1 3.0 %collective-permute-start = (bf16[14,3,32,128]{3,2,1,0:T(8,128)(2,1)S(1)}, bf16[14,3,32,128]{3,2,1,0:T(8,128)(2,1)S(1)}, u32[]{:S(2)}, u32[]{:S(2)}) collective-permute-start(bf16[14,3,32,128]{3,2,1,0:T(8,128)(2,1)S(1)} %bitcast.10), channel_id=1, source_target_pairs={{0,2},{1,3},{2,0},{3,1},{4,6},{5,7},{6,4},{7,5},{8,10},{9,11},{10,... | collective-permute-start | bytes 1032200 | tf_op jit(solution)/shard_map/ppermute | solution.py:27
  5.1 0.9 %fusion = (bf16[2,3,16,2,128]{4,3,1,2,0:T(2,128)(2,1)S(1)}, bf16[2,3,16,2,128]{4,3,1,2,0:T(2,128)(2,1)S(1)}) fusion(bf16[16,3,16,2,128]{4,3,1,2,0:T(2,128)(2,1)} %bitcast.15), kind=kLoop, calls=%fused_computation.13 | loop fusion | bytes 196608 | tf_op jit(solution)/shard_map/slice | solution.py:345
  6.0 4.6 %collective-permute-start.4 = (bf16[2,3,32,128]{3,2,1,0:T(8,128)(2,1)S(1)}, bf16[2,3,32,128]{3,2,1,0:T(8,128)(2,1)S(1)}, u32[]{:S(2)}, u32[]{:S(2)}) collective-permute-start(bf16[2,3,32,128]{3,2,1,0:T(8,128)(2,1)S(1)} %bitcast.19), channel_id=1, source_target_pairs={{4,0},{8,4},{12,8},{16,12},{20,16},{24,20},{28,24},{0,28},{5,1},{9... | collective-permute-start | bytes 147464 | tf_op jit(solution)/shard_map/ppermute | solution.py:346
  10.8 2.4 %collective-permute-done.refs_1_ = bf16[14,3,32,128]{3,2,1,0:T(8,128)(2,1)S(1)} collective-permute-done((bf16[14,3,32,128]{3,2,1,0:T(8,128)(2,1)S(1)}, bf16[14,3,32,128]{3,2,1,0:T(8,128)(2,1)S(1)}, u32[]{:S(2)}, u32[]{:S(2)}) %collective-permute-start) | collective-permute-done | bytes 344096 | tf_op jit(solution)/shard_map/ppermute | solution.py:27
  13.2 0.8 %fusion.1 = (bf16[1,3,16,2,128]{4,3,1,2,0:T(2,128)(2,1)S(1)}, bf16[1,3,16,2,128]{4,3,1,2,0:T(2,128)(2,1)S(1)}) fusion(bf16[16,3,16,2,128]{4,3,1,2,0:T(2,128)(2,1)} %bitcast.16), kind=kLoop, calls=%fused_computation.14 | loop fusion | bytes 98304 | tf_op jit(solution)/shard_map/slice | solution.py:361
  14.0 3.5 %collective-permute-done.3 = bf16[2,3,32,128]{3,2,1,0:T(8,128)(2,1)S(1)} collective-permute-done((bf16[2,3,32,128]{3,2,1,0:T(8,128)(2,1)S(1)}, bf16[2,3,32,128]{3,2,1,0:T(8,128)(2,1)S(1)}, u32[]{:S(2)}, u32[]{:S(2)}) %collective-permute-start.3) | collective-permute-done | bytes 49184 | tf_op jit(solution)/shard_map/ppermute | solution.py:345
  18.2 3.7 %prepare.2 = (bf16[14,3,128,128]{3,2,1,0:T(8,128)(2,1)S(1)}, f32[14,3,16,8,128]{4,3,2,1,0:T(8,128)S(1)}, f32[10,3,32,128]{3,2,1,0:T(8,128)S(1)}, bf16[10,2,3,32,128]{4,3,2,1,0:T(8,128)(2,1)S(1)}, f32[128,32]{1,0:T(8,128)S(1)}) custom-call(s32[2]{0:T(128)S(1)} %pad_add_fusion.idx_ref, bf16[14,3,32,128]{3,2,1,0:T(8,128)(2,1)S(1)} %bitcast.12, ...), custom_call_target="tpu_custom_call" | custom-call | tf_op jit(solution)/shard_map/prepare/pallas_call | solution.py:264
  21.9 0.8 %collective-permute-done.5 = bf16[1,6,3,32,128]{4,3,2,1,0:T(8,128)(2,1)S(1)} collective-permute-done((bf16[1,6,3,32,128]{4,3,2,1,0:T(8,128)(2,1)S(1)}, bf16[1,6,3,32,128]{4,3,2,1,0:T(8,128)(2,1)S(1)}, u32[]{:S(2)}, u32[]{:S(2)}) %collective-permute-start.5) | collective-permute-done | bytes 147488 | tf_op jit(solution)/shard_map/ppermute | solution.py:27
  22.9 5.1 %project.5 = (f32[4,256,128]{2,1,0:T(8,128)S(1)}, f32[4,256,128]{2,1,0:T(8,128)S(1)}) custom-call(s32[2]{0:T(128)S(1)} %pad_add_fusion.idx_ref, bf16[14,3,128,128]{3,2,1,0:T(8,128)(2,1)S(1)} %get-tuple-element.36.refs_0_, f32[14,3,16,8,128]{4,3,2,1,0:T(8,128)S(1)} %get-tuple-element.30.refs_5_.refs_1_, f32[10,3,32,128]{3,2,1,0:T(8,128)S(1)} %get-tuple-element.37.refs_2_, ...), custom_call_target="tpu_custom_call" | custom-call | flops 8053063680 | bytes 1048576 | tf_op jit(solution)/shard_map/project/pallas_call | solution.py:296
  28.0 2.2 %prepare.3 = (bf16[14,3,128,128]{3,2,1,0:T(8,128)(2,1)S(1)}, f32[14,3,16,8,128]{4,3,2,1,0:T(8,128)S(1)}, f32[6,3,32,128]{3,2,1,0:T(8,128)S(1)}, bf16[6,2,3,32,128]{4,3,2,1,0:T(8,128)(2,1)S(1)}, f32[128,32]{1,0:T(8,128)S(1)}) custom-call(s32[2]{0:T(128)S(1)} %pad_add_fusion.idx_ref, bf16[14,3,32,128]{3,2,1,0:T(8,128)(2,1)S(1)} %bitcast.13, ...), custom_call_target="tpu_custom_call" | custom-call | tf_op jit(solution)/shard_map/prepare/pallas_call | solution.py:264
  30.3 3.8 %project.6 = (bf16[4,272,128]{2,1,0:T(8,128)(2,1)S(1)}, bf16[4,256,128]{2,1,0:T(8,128)(2,1)S(1)}) custom-call(s32[2]{0:T(128)S(1)} %pad_add_fusion.idx_ref, bf16[14,3,128,128]{3,2,1,0:T(8,128)(2,1)S(1)} %get-tuple-element.31.refs_0_.refs_5_, f32[14,3,16,8,128]{4,3,2,1,0:T(8,128)S(1)} %get-tuple-element.32.refs_1_.refs_6_, ...), custom_call_target="tpu_custom_call" | custom-call | flops 4831838208 | bytes 1048576 | tf_op jit(solution)/shard_map/project/pallas_call | solution.py:296
  34.1 1.0 %collective-permute-start.8 = (bf16[4,256,128]{2,1,0:T(8,128)(2,1)S(1)}, bf16[4,256,128]{2,1,0:T(8,128)(2,1)S(1)}, u32[]{:S(2)}, u32[]{:S(2)}) collective-permute-start(bf16[4,256,128]{2,1,0:T(8,128)(2,1)S(1)} %get-tuple-element.42), channel_id=1, source_target_pairs={{0,8},{4,12},{8,0},{12,4},{16,24},{20,28},{24,16},{28,20},{1,9},{5... | collective-permute-start | bytes 786440 | tf_op jit(solution)/shard_map/ppermute | solution.py:27
  35.1 4.7 %project.7 = (f32[2,272,128]{2,1,0:T(8,128)S(1)}, f32[2,256,128]{2,1,0:T(8,128)S(1)}) custom-call(s32[2]{0:T(128)S(1)} %pad_add_fusion.idx_ref, bf16[14,3,128,128]{3,2,1,0:T(8,128)(2,1)S(1)} %get-tuple-element.36.refs_0_, f32[14,3,16,8,128]{4,3,2,1,0:T(8,128)S(1)} %get-tuple-element.30.refs_5_.refs_1_, f32[10,3,32,128]{3,2,1,0:T(8,128)S(1)} %get-tuple-element.37.refs_2_, ...), custom_call_target="tpu_custom_call" | custom-call | flops 6442450944 | bytes 1048576 | tf_op jit(solution)/shard_map/project/pallas_call | solution.py:296
  39.8 3.1 %collective-permute-done.8.refs_5_ = bf16[4,256,128]{2,1,0:T(8,128)(2,1)S(1)} collective-permute-done((bf16[4,256,128]{2,1,0:T(8,128)(2,1)S(1)}, bf16[4,256,128]{2,1,0:T(8,128)(2,1)S(1)}, u32[]{:S(2)}, u32[]{:S(2)}) %collective-permute-start.8) | collective-permute-done | bytes 262176 | tf_op jit(solution)/shard_map/ppermute | solution.py:27
  42.9 1.7 %collective-permute-start.10 = (bf16[2,256,128]{2,1,0:T(8,128)(2,1)S(1)}, bf16[2,256,128]{2,1,0:T(8,128)(2,1)S(1)}, u32[]{:S(2)}, u32[]{:S(2)}) collective-permute-start(bf16[2,256,128]{2,1,0:T(8,128)(2,1)S(1)} %pad_maximum_fusion.4), channel_id=1, source_target_pairs={{0,4},{4,0},{8,12},{12,8},{16,20},{20,16},{24,28},{28,24},{1,5},{5... | collective-permute-start | bytes 393224 | tf_op jit(solution)/shard_map/ppermute | solution.py:27
  45.1 2.6 %project.8 = (f32[1,272,128]{2,1,0:T(8,128)S(1)}, f32[1,256,128]{2,1,0:T(8,128)S(1)}) custom-call(s32[2]{0:T(128)S(1)} %pad_add_fusion.idx_ref, bf16[14,3,128,128]{3,2,1,0:T(8,128)(2,1)S(1)} %get-tuple-element.36.refs_0_, f32[14,3,16,8,128]{4,3,2,1,0:T(8,128)S(1)} %get-tuple-element.30.refs_5_.refs_1_, f32[10,3,32,128]{3,2,1,0:T(8,128)S(1)} %get-tuple-element.37.refs_2_, ...), custom_call_target="tpu_custom_call" | custom-call | flops 3221225472 | bytes 1048576 | tf_op jit(solution)/shard_map/project/pallas_call | solution.py:296
  48.2 1.7 %collective-permute-done.9.refs_2_ = bf16[2,272,128]{2,1,0:T(8,128)(2,1)S(1)} collective-permute-done((bf16[2,272,128]{2,1,0:T(8,128)(2,1)S(1)}, bf16[2,272,128]{2,1,0:T(8,128)(2,1)S(1)}, u32[]{:S(2)}, u32[]{:S(2)}) %collective-permute-start.9) | collective-permute-done | bytes 139296 | tf_op jit(solution)/shard_map/ppermute | solution.py:27
  50.5 2.6 %project.9 = (f32[1,272,128]{2,1,0:T(8,128)S(1)}, f32[1,256,128]{2,1,0:T(8,128)S(1)}) custom-call(s32[2]{0:T(128)S(1)} %pad_add_fusion.idx_ref, bf16[14,3,128,128]{3,2,1,0:T(8,128)(2,1)S(1)} %get-tuple-element.36.refs_0_, f32[14,3,16,8,128]{4,3,2,1,0:T(8,128)S(1)} %get-tuple-element.30.refs_5_.refs_1_, f32[10,3,32,128]{3,2,1,0:T(8,128)S(1)} %get-tuple-element.37.refs_2_, ...), custom_call_target="tpu_custom_call" | custom-call | flops 3221225472 | bytes 1048576 | tf_op jit(solution)/shard_map/project/pallas_call | solution.py:296
  53.1 0.6 %copy-done = f32[1,272,128]{2,1,0:T(8,128)} copy-done((f32[1,272,128]{2,1,0:T(8,128)}, f32[1,272,128]{2,1,0:T(8,128)S(1)}, u32[]{:S(2)}) %copy-start) | copy-done | bytes 139288
  53.8 0.6 %copy-done.1 = f32[1,256,128]{2,1,0:T(8,128)} copy-done((f32[1,256,128]{2,1,0:T(8,128)}, f32[1,256,128]{2,1,0:T(8,128)S(1)}, u32[]{:S(2)}) %copy-start.1) | copy-done | bytes 131096
  54.4 3.1 %collective-permute-done.11 = bf16[1,528,128]{2,1,0:T(8,128)(2,1)S(1)} collective-permute-done((bf16[1,528,128]{2,1,0:T(8,128)(2,1)S(1)}, bf16[1,528,128]{2,1,0:T(8,128)(2,1)S(1)}, u32[]{:S(2)}, u32[]{:S(2)}) %collective-permute-start.11) | collective-permute-done | bytes 135200 | tf_op jit(solution)/shard_map/ppermute | solution.py:27
  57.5 0.6 %slice.109.refs_3_ = bf16[1,272,128]{2,1,0:T(8,128)(2,1)} slice(bf16[1,528,128]{2,1,0:T(8,128)(2,1)S(1)} %collective-permute-done.11), slice={[0:1], [0:272], [0:128]} | slice | bytes 139264 | tf_op jit(solution)/shard_map/slice | solution.py:380
  58.8 2.0 %finish.1 = (f32[16,32,128]{2,1,0:T(8,128)}, f32[16,32]{1,0:T(8,128)}) custom-call(f32[1,272,128]{2,1,0:T(8,128)} %copy-done, bf16[4,272,128]{2,1,0:T(8,128)(2,1)} %copy-done.2, bf16[2,272,128]{2,1,0:T(8,128)(2,1)} %copy-done.4, bf16[1,272,128]{2,1,0:T(8,128)(2,1)} %slice.109.refs_3_, f32[1,256,128]{2,1,0:T(8,128)} %copy-done.1, ...), custom_call_target="tpu_custom_call" | custom-call | tf_op jit(solution)/shard_map/finish/pallas_call | solution.py:389
  (41 shorter events, 3.5 us)
Async XLA Ops:
  2.1 11.1 %collective-permute-start = (bf16[14,3,32,128]{3,2,1,0:T(8,128)(2,1)S(1)}, bf16[14,3,32,128]{3,2,1,0:T(8,128)(2,1)S(1)}, u32[]{:S(2)}, u32[]{:S(2)}) collective-permute-start(bf16[14,3,32,128]{3,2,1,0:T(8,128)(2,1)S(1)} %bitcast.10), channel_id=1, source_target_pairs={{0,2},{1,3},{2,0},{3,1},{4,6},{5,7},{6,4},{7,5},{8,10},{9,11},{10,... | collective-permute-start | bytes 1032200 | tf_op jit(solution)/shard_map/ppermute | solution.py:27
  5.1 13.1 %collective-permute-start.1 = (bf16[14,3,32,128]{3,2,1,0:T(8,128)(2,1)S(1)}, bf16[14,3,32,128]{3,2,1,0:T(8,128)(2,1)S(1)}, u32[]{:S(2)}, u32[]{:S(2)}) collective-permute-start(bf16[14,3,32,128]{3,2,1,0:T(8,128)(2,1)S(1)} %bitcast.11), channel_id=1, source_target_pairs={{0,1},{1,0},{2,3},{3,2},{4,5},{5,4},{6,7},{7,6},{8,9},{9,8},{10,11... | collective-permute-start | bytes 1032200 | tf_op jit(solution)/shard_map/ppermute | solution.py:27
  6.0 8.0 %collective-permute-start.4 = (bf16[2,3,32,128]{3,2,1,0:T(8,128)(2,1)S(1)}, bf16[2,3,32,128]{3,2,1,0:T(8,128)(2,1)S(1)}, u32[]{:S(2)}, u32[]{:S(2)}) collective-permute-start(bf16[2,3,32,128]{3,2,1,0:T(8,128)(2,1)S(1)} %bitcast.19), channel_id=1, source_target_pairs={{4,0},{8,4},{12,8},{16,12},{20,16},{24,20},{28,24},{0,28},{5,1},{9... | collective-permute-start | bytes 147464 | tf_op jit(solution)/shard_map/ppermute | solution.py:346
  10.7 6.8 %collective-permute-start.3 = (bf16[2,3,32,128]{3,2,1,0:T(8,128)(2,1)S(1)}, bf16[2,3,32,128]{3,2,1,0:T(8,128)(2,1)S(1)}, u32[]{:S(2)}, u32[]{:S(2)}) collective-permute-start(bf16[2,3,32,128]{3,2,1,0:T(8,128)(2,1)S(1)} %bitcast.20), channel_id=1, source_target_pairs={{0,4},{4,8},{8,12},{12,16},{16,20},{20,24},{24,28},{28,0},{1,5},{5... | collective-permute-start | bytes 147464 | tf_op jit(solution)/shard_map/ppermute | solution.py:345
  13.2 5.1 %collective-permute-start.2 = (bf16[14,3,32,128]{3,2,1,0:T(8,128)(2,1)S(1)}, bf16[14,3,32,128]{3,2,1,0:T(8,128)(2,1)S(1)}, u32[]{:S(2)}, u32[]{:S(2)}) collective-permute-start(bf16[14,3,32,128]{3,2,1,0:T(8,128)(2,1)S(1)} %collective-permute-done.refs_1_), channel_id=1, source_target_pairs={{0,1},{1,0},{2,3},{3,2},{4,5},{5,4},{6,7},{7,6},{8,9},{9,8},{10,11... | collective-permute-start | bytes 1032200 | tf_op jit(solution)/shard_map/ppermute | solution.py:27
  17.6 5.2 %collective-permute-start.5 = (bf16[1,6,3,32,128]{4,3,2,1,0:T(8,128)(2,1)S(1)}, bf16[1,6,3,32,128]{4,3,2,1,0:T(8,128)(2,1)S(1)}, u32[]{:S(2)}, u32[]{:S(2)}) collective-permute-start(bf16[1,6,3,32,128]{4,3,2,1,0:T(8,128)(2,1)S(1)} %maximum_bitcast_fusion), channel_id=1, source_target_pairs={{0,2},{1,3},{2,0},{3,1},{4,6},{5,7},{6,4},{7,5},{8,10},{9,11},{10,... | collective-permute-start | bytes 442376 | tf_op jit(solution)/shard_map/ppermute | solution.py:27
  22.8 5.2 %collective-permute-start.6 = (bf16[2,6,3,32,128]{4,3,2,1,0:T(8,128)(2,1)S(1)}, bf16[2,6,3,32,128]{4,3,2,1,0:T(8,128)(2,1)S(1)}, u32[]{:S(2)}, u32[]{:S(2)}) collective-permute-start(bf16[2,6,3,32,128]{4,3,2,1,0:T(8,128)(2,1)S(1)} %pad_maximum_fusion.1), channel_id=1, source_target_pairs={{0,1},{1,0},{2,3},{3,2},{4,5},{5,4},{6,7},{7,6},{8,9},{9,8},{10,11... | collective-permute-start | bytes 884744 | tf_op jit(solution)/shard_map/ppermute | solution.py:27
  34.0 10.6 %collective-permute-start.7 = (bf16[4,272,128]{2,1,0:T(8,128)(2,1)S(1)}, bf16[4,272,128]{2,1,0:T(8,128)(2,1)S(1)}, u32[]{:S(2)}, u32[]{:S(2)}) collective-permute-start(bf16[4,272,128]{2,1,0:T(8,128)(2,1)S(1)} %get-tuple-element.41), channel_id=1, source_target_pairs={{0,4},{4,0},{8,12},{12,8},{16,20},{20,16},{24,28},{28,24},{1,5},{5... | collective-permute-start | bytes 835592 | tf_op jit(solution)/shard_map/ppermute | solution.py:27
  34.1 8.8 %collective-permute-start.8 = (bf16[4,256,128]{2,1,0:T(8,128)(2,1)S(1)}, bf16[4,256,128]{2,1,0:T(8,128)(2,1)S(1)}, u32[]{:S(2)}, u32[]{:S(2)}) collective-permute-start(bf16[4,256,128]{2,1,0:T(8,128)(2,1)S(1)} %get-tuple-element.42), channel_id=1, source_target_pairs={{0,8},{4,12},{8,0},{12,4},{16,24},{20,28},{24,16},{28,20},{1,9},{5... | collective-permute-start | bytes 786440 | tf_op jit(solution)/shard_map/ppermute | solution.py:27
  42.9 5.2 %copy-start.3 = (bf16[4,256,128]{2,1,0:T(8,128)(2,1)}, bf16[4,256,128]{2,1,0:T(8,128)(2,1)S(1)}, u32[]{:S(2)}) copy-start(bf16[4,256,128]{2,1,0:T(8,128)(2,1)S(1)} %collective-permute-done.8.refs_5_) | copy-start | bytes 786436
  42.9 5.2 %collective-permute-start.10 = (bf16[2,256,128]{2,1,0:T(8,128)(2,1)S(1)}, bf16[2,256,128]{2,1,0:T(8,128)(2,1)S(1)}, u32[]{:S(2)}, u32[]{:S(2)}) collective-permute-start(bf16[2,256,128]{2,1,0:T(8,128)(2,1)S(1)} %pad_maximum_fusion.4), channel_id=1, source_target_pairs={{0,4},{4,0},{8,12},{12,8},{16,20},{20,16},{24,28},{28,24},{1,5},{5... | collective-permute-start | bytes 393224 | tf_op jit(solution)/shard_map/ppermute | solution.py:27
  44.7 5.2 %copy-start.2 = (bf16[4,272,128]{2,1,0:T(8,128)(2,1)}, bf16[4,272,128]{2,1,0:T(8,128)(2,1)S(1)}, u32[]{:S(2)}) copy-start(bf16[4,272,128]{2,1,0:T(8,128)(2,1)S(1)} %collective-permute-done.7.refs_1_) | copy-start | bytes 835588
  44.7 5.1 %collective-permute-start.9 = (bf16[2,272,128]{2,1,0:T(8,128)(2,1)S(1)}, bf16[2,272,128]{2,1,0:T(8,128)(2,1)S(1)}, u32[]{:S(2)}, u32[]{:S(2)}) collective-permute-start(bf16[2,272,128]{2,1,0:T(8,128)(2,1)S(1)} %pad_maximum_fusion.2), channel_id=1, source_target_pairs={{0,8},{4,12},{8,0},{12,4},{16,24},{20,28},{24,16},{28,20},{1,9},{5... | collective-permute-start | bytes 417800 | tf_op jit(solution)/shard_map/ppermute | solution.py:27
  48.1 5.0 %copy-start.5 = (bf16[2,256,128]{2,1,0:T(8,128)(2,1)}, bf16[2,256,128]{2,1,0:T(8,128)(2,1)S(1)}, u32[]{:S(2)}) copy-start(bf16[2,256,128]{2,1,0:T(8,128)(2,1)S(1)} %collective-permute-done.10.refs_6_) | copy-start | bytes 393220
  49.9 3.2 %copy-start.4 = (bf16[2,272,128]{2,1,0:T(8,128)(2,1)}, bf16[2,272,128]{2,1,0:T(8,128)(2,1)S(1)}, u32[]{:S(2)}) copy-start(bf16[2,272,128]{2,1,0:T(8,128)(2,1)S(1)} %collective-permute-done.9.refs_2_) | copy-start | bytes 417796
  49.9 7.6 %collective-permute-start.11 = (bf16[1,528,128]{2,1,0:T(8,128)(2,1)S(1)}, bf16[1,528,128]{2,1,0:T(8,128)(2,1)S(1)}, u32[]{:S(2)}, u32[]{:S(2)}) collective-permute-start(bf16[1,528,128]{2,1,0:T(8,128)(2,1)S(1)} %pad_maximum_fusion.3), channel_id=1, source_target_pairs={{0,16},{4,20},{8,24},{12,28},{16,0},{20,4},{24,8},{28,12},{1,17},{... | collective-permute-start | bytes 405512 | tf_op jit(solution)/shard_map/ppermute | solution.py:27
  53.1 0.7 %copy-start = (f32[1,272,128]{2,1,0:T(8,128)}, f32[1,272,128]{2,1,0:T(8,128)S(1)}, u32[]{:S(2)}) copy-start(f32[1,272,128]{2,1,0:T(8,128)S(1)} %get-tuple-element.50.refs_0_) | copy-start | bytes 417796
  53.7 0.6 %copy-start.1 = (f32[1,256,128]{2,1,0:T(8,128)}, f32[1,256,128]{2,1,0:T(8,128)S(1)}, u32[]{:S(2)}) copy-start(f32[1,256,128]{2,1,0:T(8,128)S(1)} %get-tuple-element.51.refs_4_) | copy-start | bytes 393220

commit v7 on v6

--- a/solution.py
+++ b/solution.py
@@ -69,7 +69,7 @@
     sources = [refs[:pieces]]
     if extra:
         sources.append([refs[pieces].at[q] for q in range(pieces)])
-    full_ref, turned_ref, first_ref, grad_ref, visc_ref, slope_ref, every_ref, mine_ref = refs[pieces + extra:]
+    full_ref, turned_ref, first_ref, grad_ref, visc_ref, every_ref, mine_ref = refs[pieces + extra:]
     rows, comps, lanes, width = full_ref.shape
     part = lanes // pieces
     me = idx_ref[0]
@@ -93,27 +93,28 @@
             lax.fori_loop(at, at + count, turn, 0, unroll=count if count % 4 else 4)
     weights = y_and_z_weights(lanes, cells_z)
 
+    def derivatives(line):
+        along_x = (8.0 * (line(1) - line(-1)) - (line(2) - line(-2))) * (1.0 / 12.0)
+        others = jnp.dot(line(0).astype(BF16), weights, preferred_element_type=F32) * (1.0 / 12.0)
+        return [value.astype(BF16) for value in (along_x, others[:, :lanes], others[:, lanes:])]
+
     def slopes(at, slot, row):
         mine, every = [], []
         for comp in range(comps):
-            def line(step):
+            def all_rows(step):
                 return turned_ref[row + step, comp].reshape(width, lanes)
 
-            along_x = (8.0 * (line(1) - line(-1)) - (line(2) - line(-2))) * (1.0 / 12.0)
-            others = jnp.dot(line(0).astype(BF16), weights, preferred_element_type=F32) * (1.0 / 12.0)
-            for b, value in enumerate((along_x, others[:, :lanes], others[:, lanes:])):
-                slope_ref[b, comp] = value.reshape(width // 8, 8, lanes)
-                every.append(value.astype(BF16))
-        for b in range(comps):
-            for comp in range(comps):
-                block = slope_ref[b, comp, pl.ds(me * (own // 8), own // 8)].reshape(own, lanes).astype(BF16)
-                mine.append((b, comp, block))
+            def own_rows(step):
+                return turned_ref[row + step, comp, pl.ds(me * (own // 8), own // 8)].reshape(own, lanes)
+
+            every += derivatives(all_rows)
+            for b, block in enumerate(derivatives(own_rows)):
+                mine.append(block)
                 tiled = jnp.concatenate([block] * repeat, 0)
                 if b == 0:
                     first_ref[at, comp] = tiled.astype(F32)
                 else:
                     grad_ref[at, b - 1, comp] = tiled
-        mine = [m[2] for m in sorted(mine, key=lambda m: (m[1], m[0]))]
         column = pl.ds(pl.multiple_of(slot * (comps * comps * lanes), lanes), comps * comps * lanes)
         every_ref[:, column] = jnp.concatenate(every, 1)
         mine_ref[:, column] = jnp.concatenate(mine, 1)
@@ -273,7 +274,6 @@
         in_specs=[SMEM] + [VMEM] * len(operands),
         out_specs=(VMEM,) * 5,
         scratch_shapes=[
-            pltpu.VMEM((comps, comps, width // 8, 8, lanes), F32),
             pltpu.VMEM((width, batch * comps * comps * lanes), BF16),
             pltpu.VMEM((own, batch * comps * comps * lanes), BF16),
         ],
@@ -313,15 +313,12 @@
     return sum(found)
 
 
-def finish_kernel(scales, parts, *refs):
+def finish_kernel(scales, terms, *refs):
     convective_ref, viscous_ref = refs[-2:]
     i_block, own, width = convective_ref.shape
-    i_part = i_block // parts
-    each = (len(refs) - 2) // parts
-    for part in range(parts):
-        total = refs[part * each][0]
-        for ref in refs[part * each + 1:(part + 1) * each]:
-            total = total + ref[0].astype(F32)
+    i_part = i_block // len(terms)
+    for part, found in enumerate(terms):
+        total = sum(refs[n][0, start:stop].astype(F32) for n, start, stop in found)
         rows = total[:i_part * own] * scales[0]
         convective_ref[part * i_part:(part + 1) * i_part] = rows.reshape(i_part, own, width)
         if part == 0:
@@ -385,17 +382,23 @@
         idx, sums = lax.optimization_barrier((idx, sums))
     kept = project(plans, None, both, idx, states, own, peers_x, F32)
     scales = (-1.0 / math.sqrt(total_points), -1.0 / total_points)
-    blocks = [blocks for part in both for blocks in (kept[part], *results[part])]
+    blocks, terms = [], []
+    for part in both:
+        rows = kept[part].shape[1]
+        blocks += [kept[part]] + results[part][:-1]
+        terms.append([(n, 0, rows) for n in range(len(blocks) - stages, len(blocks))])
+        terms[part].append((stages * len(both), sum(k.shape[1] for k in kept[:part]), sum(k.shape[1] for k in kept[:part + 1])))
     convective, viscous = pl.pallas_call(
-        functools.partial(finish_kernel, scales, len(both)),
+        functools.partial(finish_kernel, scales, terms),
         out_shape=(
             jax.ShapeDtypeStruct((i_block, own, width), F32),
             jax.ShapeDtypeStruct((i_block, own), F32),
         ),
-        in_specs=[VMEM] * len(blocks),
+        in_specs=[VMEM] * (len(blocks) + 1),
         out_specs=(VMEM,) * 2,
+        compiler_params=pltpu.CompilerParams(vmem_limit_bytes=4 * 2**20),
         name="finish",
-    )(*blocks)
+    )(*blocks, joined)
     return (convective, viscous)
 
 

time: 61.1 us -> 58.8 us (0.962)
  local copies, waits for them, and re-layouts: 5.81 us -> 3.25 us
  waiting for transfers between devices: 15.1 us -> 16.5 us
  Pallas kernels: 26.6 us -> 25.6 us
    ppermute x10, waiting for transfers between devices: 11.6 us -> 12.9 us  [swap(): lax.ppermute(x, axis, [(i, i ^ mask) for i in range(lax.axis_size(axis))])]
    unnamed x12 -> x0, local copies, waits for them, and re-layouts: 1.31 us -> none
    slice x2 -> x0, local copies, waits for them, and re-layouts: 1.25 us -> none  [body(): got = [joined[:, :rows], joined[:, rows:]]]
    pallas_call x1, Pallas kernels: 2 us -> 0.78 us  [body(): pl.pallas_call(functools.partial(finish_kernel, scales, terms), out_shape...]
  transfers between devices with their start and end apart: 12 -> 12, of which waited for: 7 -> 7; matrix products, arithmetic and copies ran while one was open for 3% -> 3% of each run, Pallas kernels for 31% -> 32%
where the time goes in v7:
time: 58.8 us; the launch traced here: 58.5 us
  Pallas kernels  25.6 us (44%)
  waiting for transfers between devices  16.5 us (28%)
  starting transfers between devices  12 us (20%)
  local copies, waits for them, and re-layouts  3.25 us (6%)
  between operations  0.83 us (1%)
    pallas_call x5, Pallas kernels, project(): pl.pallas_call(functools.partial(main_kernel, plans, own, stage, layout,...  18.8 us
    ppermute x10, waiting for transfers between devices, swap(): lax.ppermute(x, axis, [(i, i ^ mask) for i in range(lax.axis_size(axis))])  12.9 us
    ppermute x10, starting transfers between devices, swap(): lax.ppermute(x, axis, [(i, i ^ mask) for i in range(lax.axis_size(axis))])  7.33 us
    pallas_call x2, Pallas kernels, prepare(): pl.pallas_call(functools.partial(prepare_kernel, plan, masks, cells_z, ti...  6.07 us
    ppermute x1, starting transfers between devices, body(): after = lax.ppermute(block[:2], 'gx', down)  4.61 us
    ppermute x1, waiting for transfers between devices, body(): before = lax.ppermute(block[-2:], 'gx', up)  3.51 us
    slice x2, local copies, waits for them, and re-layouts, body(): middle = block[quarter - 2:cells_x - quarter + 2]  1.46 us
  transfers between devices with their start and end apart: 12, of which 7 were waited for; matrix products, arithmetic and copies ran while one was open for 3% of the time, Pallas kernels for 32%

profile of v7, /device:TPU:0, one launch (start us, length us, event | category | flops | bytes accessed | tf_op | source)
XLA Modules:
  0.0 58.5 jit_solution(5886301140007453919)
XLA Ops:
  0.6 1.2 %slice.88 = bf16[14,3,16,2,128]{4,3,1,2,0:T(2,128)(2,1)S(1)} slice(bf16[16,3,16,2,128]{4,3,1,2,0:T(2,128)(2,1)} %bitcast.14), slice={[1:15], [0:3], [0:16], [0:2], [0:128]} | slice | bytes 688128 | tf_op jit(solution)/shard_map/slice | solution.py:340
  2.1 3.0 %collective-permute-start = (bf16[14,3,32,128]{3,2,1,0:T(8,128)(2,1)S(1)}, bf16[14,3,32,128]{3,2,1,0:T(8,128)(2,1)S(1)}, u32[]{:S(2)}, u32[]{:S(2)}) collective-permute-start(bf16[14,3,32,128]{3,2,1,0:T(8,128)(2,1)S(1)} %bitcast.10), channel_id=1, source_target_pairs={{0,2},{1,3},{2,0},{3,1},{4,6},{5,7},{6,4},{7,5},{8,10},{9,11},{10,... | collective-permute-start | bytes 1032200 | tf_op jit(solution)/shard_map/ppermute | solution.py:27
  5.1 0.9 %fusion = (bf16[2,3,16,2,128]{4,3,1,2,0:T(2,128)(2,1)S(1)}, bf16[2,3,16,2,128]{4,3,1,2,0:T(2,128)(2,1)S(1)}) fusion(bf16[16,3,16,2,128]{4,3,1,2,0:T(2,128)(2,1)} %bitcast.15), kind=kLoop, calls=%fused_computation.13 | loop fusion | bytes 196608 | tf_op jit(solution)/shard_map/slice | solution.py:342
  6.0 4.6 %collective-permute-start.4 = (bf16[2,3,32,128]{3,2,1,0:T(8,128)(2,1)S(1)}, bf16[2,3,32,128]{3,2,1,0:T(8,128)(2,1)S(1)}, u32[]{:S(2)}, u32[]{:S(2)}) collective-permute-start(bf16[2,3,32,128]{3,2,1,0:T(8,128)(2,1)S(1)} %bitcast.19), channel_id=1, source_target_pairs={{4,0},{8,4},{12,8},{16,12},{20,16},{24,20},{28,24},{0,28},{5,1},{9... | collective-permute-start | bytes 147464 | tf_op jit(solution)/shard_map/ppermute | solution.py:343
  10.8 2.4 %collective-permute-done.refs_1_ = bf16[14,3,32,128]{3,2,1,0:T(8,128)(2,1)S(1)} collective-permute-done((bf16[14,3,32,128]{3,2,1,0:T(8,128)(2,1)S(1)}, bf16[14,3,32,128]{3,2,1,0:T(8,128)(2,1)S(1)}, u32[]{:S(2)}, u32[]{:S(2)}) %collective-permute-start) | collective-permute-done | bytes 344096 | tf_op jit(solution)/shard_map/ppermute | solution.py:27
  13.2 0.8 %fusion.1 = (bf16[1,3,16,2,128]{4,3,1,2,0:T(2,128)(2,1)S(1)}, bf16[1,3,16,2,128]{4,3,1,2,0:T(2,128)(2,1)S(1)}) fusion(bf16[16,3,16,2,128]{4,3,1,2,0:T(2,128)(2,1)} %bitcast.16), kind=kLoop, calls=%fused_computation.14 | loop fusion | bytes 98304 | tf_op jit(solution)/shard_map/slice | solution.py:358
  14.0 3.5 %collective-permute-done.3 = bf16[2,3,32,128]{3,2,1,0:T(8,128)(2,1)S(1)} collective-permute-done((bf16[2,3,32,128]{3,2,1,0:T(8,128)(2,1)S(1)}, bf16[2,3,32,128]{3,2,1,0:T(8,128)(2,1)S(1)}, u32[]{:S(2)}, u32[]{:S(2)}) %collective-permute-start.3) | collective-permute-done | bytes 49184 | tf_op jit(solution)/shard_map/ppermute | solution.py:342
  17.6 0.6 %collective-permute-start.5 = (bf16[1,6,3,32,128]{4,3,2,1,0:T(8,128)(2,1)S(1)}, bf16[1,6,3,32,128]{4,3,2,1,0:T(8,128)(2,1)S(1)}, u32[]{:S(2)}, u32[]{:S(2)}) collective-permute-start(bf16[1,6,3,32,128]{4,3,2,1,0:T(8,128)(2,1)S(1)} %maximum_bitcast_fusion), channel_id=1, source_target_pairs={{0,2},{1,3},{2,0},{3,1},{4,6},{5,7},{6,4},{7,5},{8,10},{9,11},{10,... | collective-permute-start | bytes 442376 | tf_op jit(solution)/shard_map/ppermute | solution.py:27
  18.2 3.6 %prepare.2 = (bf16[14,3,128,128]{3,2,1,0:T(8,128)(2,1)S(1)}, f32[14,3,16,8,128]{4,3,2,1,0:T(8,128)S(1)}, f32[10,3,32,128]{3,2,1,0:T(8,128)S(1)}, bf16[10,2,3,32,128]{4,3,2,1,0:T(8,128)(2,1)S(1)}, f32[128,32]{1,0:T(8,128)S(1)}) custom-call(s32[2]{0:T(128)S(1)} %pad_add_fusion.idx_ref, bf16[14,3,32,128]{3,2,1,0:T(8,128)(2,1)S(1)} %bitcast.12, ...), custom_call_target="tpu_custom_call" | custom-call | tf_op jit(solution)/shard_map/prepare/pallas_call | solution.py:265
  21.9 0.9 %collective-permute-done.5 = bf16[1,6,3,32,128]{4,3,2,1,0:T(8,128)(2,1)S(1)} collective-permute-done((bf16[1,6,3,32,128]{4,3,2,1,0:T(8,128)(2,1)S(1)}, bf16[1,6,3,32,128]{4,3,2,1,0:T(8,128)(2,1)S(1)}, u32[]{:S(2)}, u32[]{:S(2)}) %collective-permute-start.5) | collective-permute-done | bytes 147488 | tf_op jit(solution)/shard_map/ppermute | solution.py:27
  22.9 5.1 %project.5 = (f32[4,256,128]{2,1,0:T(8,128)S(1)}, f32[4,256,128]{2,1,0:T(8,128)S(1)}) custom-call(s32[2]{0:T(128)S(1)} %pad_add_fusion.idx_ref, bf16[14,3,128,128]{3,2,1,0:T(8,128)(2,1)S(1)} %get-tuple-element.36.refs_0_, f32[14,3,16,8,128]{4,3,2,1,0:T(8,128)S(1)} %get-tuple-element.30.refs_5_.refs_1_, f32[10,3,32,128]{3,2,1,0:T(8,128)S(1)} %get-tuple-element.37.refs_2_, ...), custom_call_target="tpu_custom_call" | custom-call | flops 8053063680 | bytes 1048576 | tf_op jit(solution)/shard_map/project/pallas_call | solution.py:296
  28.0 2.5 %prepare.3 = (bf16[14,3,128,128]{3,2,1,0:T(8,128)(2,1)S(1)}, f32[14,3,16,8,128]{4,3,2,1,0:T(8,128)S(1)}, f32[6,3,32,128]{3,2,1,0:T(8,128)S(1)}, bf16[6,2,3,32,128]{4,3,2,1,0:T(8,128)(2,1)S(1)}, f32[128,32]{1,0:T(8,128)S(1)}) custom-call(s32[2]{0:T(128)S(1)} %pad_add_fusion.idx_ref, bf16[14,3,32,128]{3,2,1,0:T(8,128)(2,1)S(1)} %bitcast.13, ...), custom_call_target="tpu_custom_call" | custom-call | tf_op jit(solution)/shard_map/prepare/pallas_call | solution.py:265
  30.5 3.8 %project.6 = (bf16[4,272,128]{2,1,0:T(8,128)(2,1)S(1)}, bf16[4,256,128]{2,1,0:T(8,128)(2,1)S(1)}) custom-call(s32[2]{0:T(128)S(1)} %pad_add_fusion.idx_ref, bf16[14,3,128,128]{3,2,1,0:T(8,128)(2,1)S(1)} %get-tuple-element.31.refs_0_.refs_5_, f32[14,3,16,8,128]{4,3,2,1,0:T(8,128)S(1)} %get-tuple-element.32.refs_1_.refs_6_, ...), custom_call_target="tpu_custom_call" | custom-call | flops 4831838208 | bytes 1048576 | tf_op jit(solution)/shard_map/project/pallas_call | solution.py:296
  34.3 1.0 %collective-permute-start.8 = (bf16[4,256,128]{2,1,0:T(8,128)(2,1)S(1)}, bf16[4,256,128]{2,1,0:T(8,128)(2,1)S(1)}, u32[]{:S(2)}, u32[]{:S(2)}) collective-permute-start(bf16[4,256,128]{2,1,0:T(8,128)(2,1)S(1)} %get-tuple-element.42), channel_id=1, source_target_pairs={{0,8},{4,12},{8,0},{12,4},{16,24},{20,28},{24,16},{28,20},{1,9},{5... | collective-permute-start | bytes 786440 | tf_op jit(solution)/shard_map/ppermute | solution.py:27
  35.3 4.7 %project.7 = (f32[2,272,128]{2,1,0:T(8,128)S(1)}, f32[2,256,128]{2,1,0:T(8,128)S(1)}) custom-call(s32[2]{0:T(128)S(1)} %pad_add_fusion.idx_ref, bf16[14,3,128,128]{3,2,1,0:T(8,128)(2,1)S(1)} %get-tuple-element.36.refs_0_, f32[14,3,16,8,128]{4,3,2,1,0:T(8,128)S(1)} %get-tuple-element.30.refs_5_.refs_1_, f32[10,3,32,128]{3,2,1,0:T(8,128)S(1)} %get-tuple-element.37.refs_2_, ...), custom_call_target="tpu_custom_call" | custom-call | flops 6442450944 | bytes 1048576 | tf_op jit(solution)/shard_map/project/pallas_call | solution.py:296
  40.1 3.1 %collective-permute-done.8.refs_4_ = bf16[4,256,128]{2,1,0:T(8,128)(2,1)S(1)} collective-permute-done((bf16[4,256,128]{2,1,0:T(8,128)(2,1)S(1)}, bf16[4,256,128]{2,1,0:T(8,128)(2,1)S(1)}, u32[]{:S(2)}, u32[]{:S(2)}) %collective-permute-start.8) | collective-permute-done | bytes 262176 | tf_op jit(solution)/shard_map/ppermute | solution.py:27
  43.2 1.7 %collective-permute-start.10 = (bf16[2,256,128]{2,1,0:T(8,128)(2,1)S(1)}, bf16[2,256,128]{2,1,0:T(8,128)(2,1)S(1)}, u32[]{:S(2)}, u32[]{:S(2)}) collective-permute-start(bf16[2,256,128]{2,1,0:T(8,128)(2,1)S(1)} %pad_maximum_fusion.4), channel_id=1, source_target_pairs={{0,4},{4,0},{8,12},{12,8},{16,20},{20,16},{24,28},{28,24},{1,5},{5... | collective-permute-start | bytes 393224 | tf_op jit(solution)/shard_map/ppermute | solution.py:27
  45.3 2.6 %project.8 = (f32[1,272,128]{2,1,0:T(8,128)S(1)}, f32[1,256,128]{2,1,0:T(8,128)S(1)}) custom-call(s32[2]{0:T(128)S(1)} %pad_add_fusion.idx_ref, bf16[14,3,128,128]{3,2,1,0:T(8,128)(2,1)S(1)} %get-tuple-element.36.refs_0_, f32[14,3,16,8,128]{4,3,2,1,0:T(8,128)S(1)} %get-tuple-element.30.refs_5_.refs_1_, f32[10,3,32,128]{3,2,1,0:T(8,128)S(1)} %get-tuple-element.37.refs_2_, ...), custom_call_target="tpu_custom_call" | custom-call | flops 3221225472 | bytes 1048576 | tf_op jit(solution)/shard_map/project/pallas_call | solution.py:296
  47.9 0.4 collective-permute-done.10.refs_5_
  48.4 1.7 %collective-permute-done.9.refs_2_ = bf16[2,272,128]{2,1,0:T(8,128)(2,1)S(1)} collective-permute-done((bf16[2,272,128]{2,1,0:T(8,128)(2,1)S(1)}, bf16[2,272,128]{2,1,0:T(8,128)(2,1)S(1)}, u32[]{:S(2)}, u32[]{:S(2)}) %collective-permute-start.9) | collective-permute-done | bytes 139296 | tf_op jit(solution)/shard_map/ppermute | solution.py:27
  50.1 0.5 collective-permute-start.11
  50.7 2.6 %project.9 = (f32[1,272,128]{2,1,0:T(8,128)S(1)}, f32[1,256,128]{2,1,0:T(8,128)S(1)}) custom-call(s32[2]{0:T(128)S(1)} %pad_add_fusion.idx_ref, bf16[14,3,128,128]{3,2,1,0:T(8,128)(2,1)S(1)} %get-tuple-element.36.refs_0_, f32[14,3,16,8,128]{4,3,2,1,0:T(8,128)S(1)} %get-tuple-element.30.refs_5_.refs_1_, f32[10,3,32,128]{3,2,1,0:T(8,128)S(1)} %get-tuple-element.37.refs_2_, ...), custom_call_target="tpu_custom_call" | custom-call | flops 3221225472 | bytes 1048576 | tf_op jit(solution)/shard_map/project/pallas_call | solution.py:296
  53.3 4.4 %collective-permute-done.11.refs_6_ = bf16[1,528,128]{2,1,0:T(8,128)(2,1)S(1)} collective-permute-done((bf16[1,528,128]{2,1,0:T(8,128)(2,1)S(1)}, bf16[1,528,128]{2,1,0:T(8,128)(2,1)S(1)}, u32[]{:S(2)}, u32[]{:S(2)}) %collective-permute-start.11) | collective-permute-done | bytes 135200 | tf_op jit(solution)/shard_map/ppermute | solution.py:27
  57.8 0.8 %finish.1 = (f32[16,32,128]{2,1,0:T(8,128)}, f32[16,32]{1,0:T(8,128)}) custom-call(f32[1,272,128]{2,1,0:T(8,128)S(1)} %get-tuple-element.50.refs_0_, bf16[4,272,128]{2,1,0:T(8,128)(2,1)S(1)} %collective-permute-done.7.refs_1_, bf16[2,272,128]{2,1,0:T(8,128)(2,1)S(1)} %collective-permute-done.9.refs_2_, f32[1,256,128]{2,1,0:T(8,128)S(1)} %get-tuple-element.51.refs_3_, ...), custom_call_target="tpu_custom_call" | custom-call | tf_op jit(solution)/shard_map/finish/pallas_call | solution.py:391
  (27 shorter events, 1.3 us)
Async XLA Ops:
  2.1 11.1 %collective-permute-start = (bf16[14,3,32,128]{3,2,1,0:T(8,128)(2,1)S(1)}, bf16[14,3,32,128]{3,2,1,0:T(8,128)(2,1)S(1)}, u32[]{:S(2)}, u32[]{:S(2)}) collective-permute-start(bf16[14,3,32,128]{3,2,1,0:T(8,128)(2,1)S(1)} %bitcast.10), channel_id=1, source_target_pairs={{0,2},{1,3},{2,0},{3,1},{4,6},{5,7},{6,4},{7,5},{8,10},{9,11},{10,... | collective-permute-start | bytes 1032200 | tf_op jit(solution)/shard_map/ppermute | solution.py:27
  5.1 13.1 %collective-permute-start.1 = (bf16[14,3,32,128]{3,2,1,0:T(8,128)(2,1)S(1)}, bf16[14,3,32,128]{3,2,1,0:T(8,128)(2,1)S(1)}, u32[]{:S(2)}, u32[]{:S(2)}) collective-permute-start(bf16[14,3,32,128]{3,2,1,0:T(8,128)(2,1)S(1)} %bitcast.11), channel_id=1, source_target_pairs={{0,1},{1,0},{2,3},{3,2},{4,5},{5,4},{6,7},{7,6},{8,9},{9,8},{10,11... | collective-permute-start | bytes 1032200 | tf_op jit(solution)/shard_map/ppermute | solution.py:27
  6.0 8.0 %collective-permute-start.4 = (bf16[2,3,32,128]{3,2,1,0:T(8,128)(2,1)S(1)}, bf16[2,3,32,128]{3,2,1,0:T(8,128)(2,1)S(1)}, u32[]{:S(2)}, u32[]{:S(2)}) collective-permute-start(bf16[2,3,32,128]{3,2,1,0:T(8,128)(2,1)S(1)} %bitcast.19), channel_id=1, source_target_pairs={{4,0},{8,4},{12,8},{16,12},{20,16},{24,20},{28,24},{0,28},{5,1},{9... | collective-permute-start | bytes 147464 | tf_op jit(solution)/shard_map/ppermute | solution.py:343
  10.7 6.8 %collective-permute-start.3 = (bf16[2,3,32,128]{3,2,1,0:T(8,128)(2,1)S(1)}, bf16[2,3,32,128]{3,2,1,0:T(8,128)(2,1)S(1)}, u32[]{:S(2)}, u32[]{:S(2)}) collective-permute-start(bf16[2,3,32,128]{3,2,1,0:T(8,128)(2,1)S(1)} %bitcast.20), channel_id=1, source_target_pairs={{0,4},{4,8},{8,12},{12,16},{16,20},{20,24},{24,28},{28,0},{1,5},{5... | collective-permute-start | bytes 147464 | tf_op jit(solution)/shard_map/ppermute | solution.py:342
  13.2 5.1 %collective-permute-start.2 = (bf16[14,3,32,128]{3,2,1,0:T(8,128)(2,1)S(1)}, bf16[14,3,32,128]{3,2,1,0:T(8,128)(2,1)S(1)}, u32[]{:S(2)}, u32[]{:S(2)}) collective-permute-start(bf16[14,3,32,128]{3,2,1,0:T(8,128)(2,1)S(1)} %collective-permute-done.refs_1_), channel_id=1, source_target_pairs={{0,1},{1,0},{2,3},{3,2},{4,5},{5,4},{6,7},{7,6},{8,9},{9,8},{10,11... | collective-permute-start | bytes 1032200 | tf_op jit(solution)/shard_map/ppermute | solution.py:27
  17.6 5.2 %collective-permute-start.5 = (bf16[1,6,3,32,128]{4,3,2,1,0:T(8,128)(2,1)S(1)}, bf16[1,6,3,32,128]{4,3,2,1,0:T(8,128)(2,1)S(1)}, u32[]{:S(2)}, u32[]{:S(2)}) collective-permute-start(bf16[1,6,3,32,128]{4,3,2,1,0:T(8,128)(2,1)S(1)} %maximum_bitcast_fusion), channel_id=1, source_target_pairs={{0,2},{1,3},{2,0},{3,1},{4,6},{5,7},{6,4},{7,5},{8,10},{9,11},{10,... | collective-permute-start | bytes 442376 | tf_op jit(solution)/shard_map/ppermute | solution.py:27
  22.8 5.1 %collective-permute-start.6 = (bf16[2,6,3,32,128]{4,3,2,1,0:T(8,128)(2,1)S(1)}, bf16[2,6,3,32,128]{4,3,2,1,0:T(8,128)(2,1)S(1)}, u32[]{:S(2)}, u32[]{:S(2)}) collective-permute-start(bf16[2,6,3,32,128]{4,3,2,1,0:T(8,128)(2,1)S(1)} %pad_maximum_fusion.1), channel_id=1, source_target_pairs={{0,1},{1,0},{2,3},{3,2},{4,5},{5,4},{6,7},{7,6},{8,9},{9,8},{10,11... | collective-permute-start | bytes 884744 | tf_op jit(solution)/shard_map/ppermute | solution.py:27
  34.3 10.6 %collective-permute-start.7 = (bf16[4,272,128]{2,1,0:T(8,128)(2,1)S(1)}, bf16[4,272,128]{2,1,0:T(8,128)(2,1)S(1)}, u32[]{:S(2)}, u32[]{:S(2)}) collective-permute-start(bf16[4,272,128]{2,1,0:T(8,128)(2,1)S(1)} %get-tuple-element.41), channel_id=1, source_target_pairs={{0,4},{4,0},{8,12},{12,8},{16,20},{20,16},{24,28},{28,24},{1,5},{5... | collective-permute-start | bytes 835592 | tf_op jit(solution)/shard_map/ppermute | solution.py:27
  34.3 8.8 %collective-permute-start.8 = (bf16[4,256,128]{2,1,0:T(8,128)(2,1)S(1)}, bf16[4,256,128]{2,1,0:T(8,128)(2,1)S(1)}, u32[]{:S(2)}, u32[]{:S(2)}) collective-permute-start(bf16[4,256,128]{2,1,0:T(8,128)(2,1)S(1)} %get-tuple-element.42), channel_id=1, source_target_pairs={{0,8},{4,12},{8,0},{12,4},{16,24},{20,28},{24,16},{28,20},{1,9},{5... | collective-permute-start | bytes 786440 | tf_op jit(solution)/shard_map/ppermute | solution.py:27
  43.2 5.2 %collective-permute-start.10 = (bf16[2,256,128]{2,1,0:T(8,128)(2,1)S(1)}, bf16[2,256,128]{2,1,0:T(8,128)(2,1)S(1)}, u32[]{:S(2)}, u32[]{:S(2)}) collective-permute-start(bf16[2,256,128]{2,1,0:T(8,128)(2,1)S(1)} %pad_maximum_fusion.4), channel_id=1, source_target_pairs={{0,4},{4,0},{8,12},{12,8},{16,20},{20,16},{24,28},{28,24},{1,5},{5... | collective-permute-start | bytes 393224 | tf_op jit(solution)/shard_map/ppermute | solution.py:27
  45.0 5.1 %collective-permute-start.9 = (bf16[2,272,128]{2,1,0:T(8,128)(2,1)S(1)}, bf16[2,272,128]{2,1,0:T(8,128)(2,1)S(1)}, u32[]{:S(2)}, u32[]{:S(2)}) collective-permute-start(bf16[2,272,128]{2,1,0:T(8,128)(2,1)S(1)} %pad_maximum_fusion.2), channel_id=1, source_target_pairs={{0,8},{4,12},{8,0},{12,4},{16,24},{20,28},{24,16},{28,20},{1,9},{5... | collective-permute-start | bytes 417800 | tf_op jit(solution)/shard_map/ppermute | solution.py:27
  50.1 7.6 %collective-permute-start.11 = (bf16[1,528,128]{2,1,0:T(8,128)(2,1)S(1)}, bf16[1,528,128]{2,1,0:T(8,128)(2,1)S(1)}, u32[]{:S(2)}, u32[]{:S(2)}) collective-permute-start(bf16[1,528,128]{2,1,0:T(8,128)(2,1)S(1)} %pad_maximum_fusion.3), channel_id=1, source_target_pairs={{0,16},{4,20},{8,24},{12,28},{16,0},{20,4},{24,8},{28,12},{1,17},{... | collective-permute-start | bytes 405512 | tf_op jit(solution)/shard_map/ppermute | solution.py:27

commit v8 on v7

--- a/solution.py
+++ b/solution.py
@@ -27,14 +27,18 @@
     return lax.ppermute(x, axis, [(i, i ^ mask) for i in range(lax.axis_size(axis))])
 
 
-def gathered(x, axis):
-    pieces, mask = [x], lax.axis_size(axis) // 2
-    masks = [0]
+def gathered(x, axis, beside):
+    pieces, masks, mask = [x], [0], lax.axis_size(axis) // 2
+    first = True
     while mask:
-        pieces += [swap(piece, axis, mask) for piece in pieces]
+        got = [swap(piece, axis, mask) for piece in pieces]
+        if first:
+            got, beside = lax.optimization_barrier((got, beside))
+            first = False
+        pieces += got
         masks += [m ^ mask for m in masks]
         mask //= 2
-    return pieces, masks
+    return pieces, masks, beside
 
 
 def gathered_stack(x, axis, behind):
@@ -115,25 +119,35 @@
                     first_ref[at, comp] = tiled.astype(F32)
                 else:
                     grad_ref[at, b - 1, comp] = tiled
-        column = pl.ds(pl.multiple_of(slot * (comps * comps * lanes), lanes), comps * comps * lanes)
+        column = slot * (comps * comps * lanes)
+        if not isinstance(slot, int):
+            column = pl.multiple_of(column, lanes)
+        column = pl.ds(column, comps * comps * lanes)
         every_ref[:, column] = jnp.concatenate(every, 1)
         mine_ref[:, column] = jnp.concatenate(mine, 1)
 
     batch = mine_ref.shape[1] // (comps * comps * lanes)
-    steps = [(row, min(row + batch, stop)) for start, stop in interior for row in range(start, stop, batch)]
+    if lanes <= 128:
+        steps = [[row for start, stop in interior for row in range(start, stop)]]
+    else:
+        steps = [list(range(row, min(row + batch, stop))) for start, stop in interior for row in range(start, stop, batch)]
     at = 0
-    for start, stop in steps:
-        def one(step, carry, start=start, at=at):
-            slopes(at + step, step, start + step)
-            return carry
-
-        lax.fori_loop(0, stop - start, one, 0, unroll=5 if (stop - start) % 5 == 0 else min(4, stop - start))
-        used = (stop - start) * comps * comps * lanes
+    for rows_now in steps:
+        if lanes <= 128:
+            for slot, row in enumerate(rows_now):
+                slopes(at + slot, slot, row)
+        else:
+            def one(step, carry, start=rows_now[0], at=at):
+                slopes(at + step, step, start + step)
+                return carry
+
+            lax.fori_loop(0, len(rows_now), one, 0)
+        used = len(rows_now) * comps * comps * lanes
         term = lax.dot_general(
             every_ref[:, :used], mine_ref[:, :used], (((1,), (1,)), ((), ())), preferred_element_type=F32
         )
         visc_ref[...] = term if at == 0 else visc_ref[...] + term
-        at += stop - start
+        at += len(rows_now)
 
 
 def code_of(part, stage, j):
@@ -261,7 +275,7 @@
     _, comps, part, width = sources[0].shape
     lanes = part * len(masks)
     tile = max(own, 16)
-    batch = max(1, min(max(stop - start for start, stop in interior), 2048 // lanes))
+    batch = count if lanes <= 128 else max(1, 2048 // lanes)
     return pl.pallas_call(
         functools.partial(prepare_kernel, plan, masks, cells_z, tile // own),
         out_shape=(
@@ -336,11 +350,11 @@
     block = modes.transpose(0, 3, 1, 2, 4).reshape(cells_x, comps, cells_y * cells_z, width)
     up = [(i, (i + 1) % peers_x) for i in range(peers_x)]
     down = [(j, i) for i, j in up]
-    quarter = max(2, cells_x // 5)
+    quarter = cells_x // 4
     middle = block[quarter - 2:cells_x - quarter + 2]
-    pieces, masks = gathered(middle, "gy")
     before = lax.ppermute(block[-2:], "gx", up)
     after = lax.ppermute(block[:2], "gx", down)
+    pieces, masks, (before, after) = gathered(middle, "gy", (before, after))
     length = middle.shape[0]
     plans = (
         (((0, 0, length, 0),), ((2, length - 2),)),
@@ -354,11 +368,11 @@
     both = tuple(range(PARTS))
     results = [[], []]
     states = [prepare(plans[0], masks, cells_z, idx, pieces, (), own)]
+    begun = project(plans[:1], 0, both, idx, states, own, peers_x, F32, viscous=False)
     rim = gathered_stack(
         jnp.concatenate([before, block[:quarter - 2], block[cells_x - quarter + 2:], after], 0),
-        "gy", states[0][4],
+        "gy", begun[0],
     )
-    begun = project(plans[:1], 0, both, idx, states, own, peers_x, F32, viscous=False)
     states.append(prepare(plans[1], masks, cells_z, idx, pieces, (rim, states[0][1]), own))
     sends = project(plans[1:], 0, both, idx, states[1:], own, peers_x, BF16, prior=begun, earlier=states[:1])
     for part in both:

time: 58.8 us -> 54.5 us (0.927)
  waiting for transfers between devices: 16.5 us -> 7.86 us
  starting transfers between devices: 12 us -> 18 us
  local copies, waits for them, and re-layouts: 3.25 us -> 2.34 us
  Pallas kernels: 25.6 us -> 25 us
    ppermute x10, waiting for transfers between devices: 12.9 us -> 5.89 us  [swap(): lax.ppermute(x, axis, [(i, i ^ mask) for i in range(lax.axis_size(axis))])]
    ppermute x10, starting transfers between devices: 7.33 us -> 13.2 us  [swap(): lax.ppermute(x, axis, [(i, i ^ mask) for i in range(lax.axis_size(axis))])]
    ppermute x1, waiting for transfers between devices: 3.51 us -> 1.97 us  [body(): before = lax.ppermute(block[-2:], 'gx', up)]
    ppermute x1, starting transfers between devices: 0.06 us -> 1.57 us  [body(): before = lax.ppermute(block[-2:], 'gx', up)]
    ppermute x1, starting transfers between devices: 4.61 us -> 3.26 us  [body(): after = lax.ppermute(block[:2], 'gx', down)]
    slice x2 -> x1, local copies, waits for them, and re-layouts: 0.93 us -> 0.04 us  [body(): before = lax.ppermute(block[-2:], 'gx', up)]
    slice x1 -> x2, local copies, waits for them, and re-layouts: 0.04 us -> 0.93 us  [body(): after = lax.ppermute(block[:2], 'gx', down)]
    slice x3 -> x0, local copies, waits for them, and re-layouts: 0.83 us -> none  [the longest x2 0.81 us: body(): block[:quarter - 2]]
  transfers between devices with their start and end apart: 12 -> 12, of which waited for: 7 -> 6; matrix products, arithmetic and copies ran while one was open for 3% -> 2% of each run, Pallas kernels for 32% -> 31%
where the time goes in v8:
time: 54.5 us; the launch traced here: 54.3 us
  Pallas kernels  25 us (46%)
  starting transfers between devices  18 us (33%)
  waiting for transfers between devices  7.86 us (14%)
  local copies, waits for them, and re-layouts  2.34 us (4%)
  between operations  0.8 us (1%)
    pallas_call x5, Pallas kernels, project(): pl.pallas_call(functools.partial(main_kernel, plans, own, stage, layout,...  18.9 us
    ppermute x10, starting transfers between devices, swap(): lax.ppermute(x, axis, [(i, i ^ mask) for i in range(lax.axis_size(axis))])  13.2 us
    ppermute x10, waiting for transfers between devices, swap(): lax.ppermute(x, axis, [(i, i ^ mask) for i in range(lax.axis_size(axis))])  5.89 us
    pallas_call x2, Pallas kernels, prepare(): pl.pallas_call(functools.partial(prepare_kernel, plan, masks, cells_z, ti...  5.34 us
    ppermute x1, starting transfers between devices, body(): after = lax.ppermute(block[:2], 'gx', down)  3.26 us
    ppermute x1, waiting for transfers between devices, body(): before = lax.ppermute(block[-2:], 'gx', up)  1.97 us
    ppermute x1, starting transfers between devices, body(): before = lax.ppermute(block[-2:], 'gx', up)  1.57 us
    slice x2, local copies, waits for them, and re-layouts, body(): middle = block[quarter - 2:cells_x - quarter + 2]  1.37 us
  transfers between devices with their start and end apart: 12, of which 6 were waited for; matrix products, arithmetic and copies ran while one was open for 2% of the time, Pallas kernels for 31%

profile of v8, /device:TPU:0, one launch (start us, length us, event | category | flops | bytes accessed | tf_op | source)
XLA Modules:
  0.0 54.3 jit_solution(8611164235678255959)
XLA Ops:
  0.6 1.2 %slice.74 = bf16[12,3,16,2,128]{4,3,1,2,0:T(2,128)(2,1)S(1)} slice(bf16[16,3,16,2,128]{4,3,1,2,0:T(2,128)(2,1)} %bitcast.12), slice={[2:14], [0:3], [0:16], [0:2], [0:128]} | slice | bytes 589824 | tf_op jit(solution)/shard_map/slice | solution.py:354
  2.0 3.0 %collective-permute-start = (bf16[12,3,32,128]{3,2,1,0:T(8,128)(2,1)S(1)}, bf16[12,3,32,128]{3,2,1,0:T(8,128)(2,1)S(1)}, u32[]{:S(2)}, u32[]{:S(2)}) collective-permute-start(bf16[12,3,32,128]{3,2,1,0:T(8,128)(2,1)S(1)} %bitcast.8), channel_id=1, source_target_pairs={{0,2},{1,3},{2,0},{3,1},{4,6},{5,7},{6,4},{7,5},{8,10},{9,11},{10,... | collective-permute-start | bytes 884744 | tf_op jit(solution)/shard_map/ppermute | solution.py:27
  5.0 0.9 %fusion = (bf16[2,3,16,2,128]{4,3,1,2,0:T(2,128)(2,1)S(1)}, bf16[2,3,16,2,128]{4,3,1,2,0:T(2,128)(2,1)S(1)}) fusion(bf16[16,3,16,2,128]{4,3,1,2,0:T(2,128)(2,1)} %bitcast.13), kind=kLoop, calls=%fused_computation.13 | loop fusion | bytes 196608 | tf_op jit(solution)/shard_map/slice | solution.py:356
  6.0 1.6 %collective-permute-start.1 = (bf16[2,3,32,128]{3,2,1,0:T(8,128)(2,1)S(1)}, bf16[2,3,32,128]{3,2,1,0:T(8,128)(2,1)S(1)}, u32[]{:S(2)}, u32[]{:S(2)}) collective-permute-start(bf16[2,3,32,128]{3,2,1,0:T(8,128)(2,1)S(1)} %bitcast.14), channel_id=1, source_target_pairs={{0,4},{4,8},{8,12},{12,16},{16,20},{20,24},{24,28},{28,0},{1,5},{5... | collective-permute-start | bytes 147464 | tf_op jit(solution)/shard_map/ppermute | solution.py:355
  7.6 3.3 %collective-permute-start.2 = (bf16[2,3,32,128]{3,2,1,0:T(8,128)(2,1)S(1)}, bf16[2,3,32,128]{3,2,1,0:T(8,128)(2,1)S(1)}, u32[]{:S(2)}, u32[]{:S(2)}) collective-permute-start(bf16[2,3,32,128]{3,2,1,0:T(8,128)(2,1)S(1)} %bitcast.16), channel_id=1, source_target_pairs={{4,0},{8,4},{12,8},{16,12},{20,16},{24,20},{28,24},{0,28},{5,1},{9... | collective-permute-start | bytes 147464 | tf_op jit(solution)/shard_map/ppermute | solution.py:356
  10.8 2.0 %collective-permute-done.1 = bf16[2,3,32,128]{3,2,1,0:T(8,128)(2,1)S(1)} collective-permute-done((bf16[2,3,32,128]{3,2,1,0:T(8,128)(2,1)S(1)}, bf16[2,3,32,128]{3,2,1,0:T(8,128)(2,1)S(1)}, u32[]{:S(2)}, u32[]{:S(2)}) %collective-permute-start.1) | collective-permute-done | bytes 49184 | tf_op jit(solution)/shard_map/ppermute | solution.py:355
  12.9 1.0 %collective-permute-start.5 = (bf16[1,8,3,32,128]{4,3,2,1,0:T(8,128)(2,1)S(1)}, bf16[1,8,3,32,128]{4,3,2,1,0:T(8,128)(2,1)S(1)}, u32[]{:S(2)}, u32[]{:S(2)}) collective-permute-start(bf16[1,8,3,32,128]{4,3,2,1,0:T(8,128)(2,1)S(1)} %maximum_bitcast_fusion), channel_id=1, source_target_pairs={{0,2},{1,3},{2,0},{3,1},{4,6},{5,7},{6,4},{7,5},{8,10},{9,11},{10,... | collective-permute-start | bytes 589832 | tf_op jit(solution)/shard_map/ppermute | solution.py:27
  14.4 2.8 %prepare.2 = (bf16[12,3,128,128]{3,2,1,0:T(8,128)(2,1)S(1)}, f32[12,3,16,8,128]{4,3,2,1,0:T(8,128)S(1)}, f32[8,3,32,128]{3,2,1,0:T(8,128)S(1)}, bf16[8,2,3,32,128]{4,3,2,1,0:T(8,128)(2,1)S(1)}, f32[128,32]{1,0:T(8,128)S(1)}) custom-call(s32[2]{0:T(128)S(1)} %pad_add_fusion.idx_ref, bf16[12,3,32,128]{3,2,1,0:T(8,128)(2,1)S(1)} %bitcast.10, ...), custom_call_target="tpu_custom_call" | custom-call | tf_op jit(solution)/shard_map/prepare/pallas_call | solution.py:279
  17.2 4.2 %project.5 = (f32[4,256,128]{2,1,0:T(8,128)S(1)}, f32[4,256,128]{2,1,0:T(8,128)S(1)}) custom-call(s32[2]{0:T(128)S(1)} %pad_add_fusion.idx_ref, bf16[12,3,128,128]{3,2,1,0:T(8,128)(2,1)S(1)} %get-tuple-element.33.refs_0_, f32[12,3,16,8,128]{4,3,2,1,0:T(8,128)S(1)} %get-tuple-element.34.refs_1_.refs_5_, f32[8,3,32,128]{3,2,1,0:T(8,128)S(1)} %get-tuple-element.35.refs_2_, ...), custom_call_target="tpu_custom_call" | custom-call | flops 6442450944 | bytes 1048576 | tf_op jit(solution)/shard_map/project/pallas_call | solution.py:310
  21.7 1.6 %collective-permute-done.6 = bf16[2,8,3,32,128]{4,3,2,1,0:T(8,128)(2,1)S(1)} collective-permute-done((bf16[2,8,3,32,128]{4,3,2,1,0:T(8,128)(2,1)S(1)}, bf16[2,8,3,32,128]{4,3,2,1,0:T(8,128)(2,1)S(1)}, u32[]{:S(2)}, u32[]{:S(2)}) %collective-permute-start.6) | collective-permute-done | bytes 393248 | tf_op jit(solution)/shard_map/ppermute | solution.py:27
  23.3 2.5 %prepare.3 = (bf16[16,3,128,128]{3,2,1,0:T(8,128)(2,1)S(1)}, f32[16,3,16,8,128]{4,3,2,1,0:T(8,128)S(1)}, f32[8,3,32,128]{3,2,1,0:T(8,128)S(1)}, bf16[8,2,3,32,128]{4,3,2,1,0:T(8,128)(2,1)S(1)}, f32[128,32]{1,0:T(8,128)S(1)}) custom-call(s32[2]{0:T(128)S(1)} %pad_add_fusion.idx_ref, bf16[12,3,32,128]{3,2,1,0:T(8,128)(2,1)S(1)} %bitcast.11, ...), custom_call_target="tpu_custom_call" | custom-call | tf_op jit(solution)/shard_map/prepare/pallas_call | solution.py:279
  25.9 4.8 %project.6 = (bf16[4,272,128]{2,1,0:T(8,128)(2,1)S(1)}, bf16[4,256,128]{2,1,0:T(8,128)(2,1)S(1)}) custom-call(s32[2]{0:T(128)S(1)} %pad_add_fusion.idx_ref, bf16[16,3,128,128]{3,2,1,0:T(8,128)(2,1)S(1)} %get-tuple-element.41.refs_0_.refs_5_, f32[16,3,16,8,128]{4,3,2,1,0:T(8,128)S(1)} %get-tuple-element.42.refs_1_.refs_6_, ...), custom_call_target="tpu_custom_call" | custom-call | flops 6442450944 | bytes 1048576 | tf_op jit(solution)/shard_map/project/pallas_call | solution.py:310
  30.7 1.2 %collective-permute-start.8 = (bf16[4,256,128]{2,1,0:T(8,128)(2,1)S(1)}, bf16[4,256,128]{2,1,0:T(8,128)(2,1)S(1)}, u32[]{:S(2)}, u32[]{:S(2)}) collective-permute-start(bf16[4,256,128]{2,1,0:T(8,128)(2,1)S(1)} %get-tuple-element.48), channel_id=1, source_target_pairs={{0,8},{4,12},{8,0},{12,4},{16,24},{20,28},{24,16},{28,20},{1,9},{5... | collective-permute-start | bytes 786440 | tf_op jit(solution)/shard_map/ppermute | solution.py:27
  31.9 1.8 %collective-permute-start.7 = (bf16[4,272,128]{2,1,0:T(8,128)(2,1)S(1)}, bf16[4,272,128]{2,1,0:T(8,128)(2,1)S(1)}, u32[]{:S(2)}, u32[]{:S(2)}) collective-permute-start(bf16[4,272,128]{2,1,0:T(8,128)(2,1)S(1)} %get-tuple-element.47), channel_id=1, source_target_pairs={{0,4},{4,0},{8,12},{12,8},{16,20},{20,16},{24,28},{28,24},{1,5},{5... | collective-permute-start | bytes 835592 | tf_op jit(solution)/shard_map/ppermute | solution.py:27
  33.6 4.7 %project.7 = (f32[2,272,128]{2,1,0:T(8,128)S(1)}, f32[2,256,128]{2,1,0:T(8,128)S(1)}) custom-call(s32[2]{0:T(128)S(1)} %pad_add_fusion.idx_ref, bf16[12,3,128,128]{3,2,1,0:T(8,128)(2,1)S(1)} %get-tuple-element.33.refs_0_, f32[12,3,16,8,128]{4,3,2,1,0:T(8,128)S(1)} %get-tuple-element.34.refs_1_.refs_5_, f32[8,3,32,128]{3,2,1,0:T(8,128)S(1)} %get-tuple-element.35.refs_2_, ...), custom_call_target="tpu_custom_call" | custom-call | flops 6442450944 | bytes 1048576 | tf_op jit(solution)/shard_map/project/pallas_call | solution.py:310
  38.3 0.8 %collective-permute-done.8.refs_4_ = bf16[4,256,128]{2,1,0:T(8,128)(2,1)S(1)} collective-permute-done((bf16[4,256,128]{2,1,0:T(8,128)(2,1)S(1)}, bf16[4,256,128]{2,1,0:T(8,128)(2,1)S(1)}, u32[]{:S(2)}, u32[]{:S(2)}) %collective-permute-start.8) | collective-permute-done | bytes 262176 | tf_op jit(solution)/shard_map/ppermute | solution.py:27
  39.1 1.4 %collective-permute-start.10 = (bf16[2,256,128]{2,1,0:T(8,128)(2,1)S(1)}, bf16[2,256,128]{2,1,0:T(8,128)(2,1)S(1)}, u32[]{:S(2)}, u32[]{:S(2)}) collective-permute-start(bf16[2,256,128]{2,1,0:T(8,128)(2,1)S(1)} %pad_maximum_fusion.4), channel_id=1, source_target_pairs={{0,4},{4,0},{8,12},{12,8},{16,20},{20,16},{24,28},{28,24},{1,5},{5... | collective-permute-start | bytes 393224 | tf_op jit(solution)/shard_map/ppermute | solution.py:27
  40.6 1.6 %collective-permute-start.9 = (bf16[2,272,128]{2,1,0:T(8,128)(2,1)S(1)}, bf16[2,272,128]{2,1,0:T(8,128)(2,1)S(1)}, u32[]{:S(2)}, u32[]{:S(2)}) collective-permute-start(bf16[2,272,128]{2,1,0:T(8,128)(2,1)S(1)} %pad_maximum_fusion.2), channel_id=1, source_target_pairs={{0,8},{4,12},{8,0},{12,4},{16,24},{20,28},{24,16},{28,20},{1,9},{5... | collective-permute-start | bytes 417800 | tf_op jit(solution)/shard_map/ppermute | solution.py:27
  42.2 2.6 %project.8 = (f32[1,272,128]{2,1,0:T(8,128)S(1)}, f32[1,256,128]{2,1,0:T(8,128)S(1)}) custom-call(s32[2]{0:T(128)S(1)} %pad_add_fusion.idx_ref, bf16[12,3,128,128]{3,2,1,0:T(8,128)(2,1)S(1)} %get-tuple-element.33.refs_0_, f32[12,3,16,8,128]{4,3,2,1,0:T(8,128)S(1)} %get-tuple-element.34.refs_1_.refs_5_, f32[8,3,32,128]{3,2,1,0:T(8,128)S(1)} %get-tuple-element.35.refs_2_, ...), custom_call_target="tpu_custom_call" | custom-call | flops 3221225472 | bytes 1048576 | tf_op jit(solution)/shard_map/project/pallas_call | solution.py:310
  44.9 0.8 %collective-permute-done.9.refs_2_ = bf16[2,272,128]{2,1,0:T(8,128)(2,1)S(1)} collective-permute-done((bf16[2,272,128]{2,1,0:T(8,128)(2,1)S(1)}, bf16[2,272,128]{2,1,0:T(8,128)(2,1)S(1)}, u32[]{:S(2)}, u32[]{:S(2)}) %collective-permute-start.9) | collective-permute-done | bytes 139296 | tf_op jit(solution)/shard_map/ppermute | solution.py:27
  45.8 2.9 %collective-permute-start.11 = (bf16[1,528,128]{2,1,0:T(8,128)(2,1)S(1)}, bf16[1,528,128]{2,1,0:T(8,128)(2,1)S(1)}, u32[]{:S(2)}, u32[]{:S(2)}) collective-permute-start(bf16[1,528,128]{2,1,0:T(8,128)(2,1)S(1)} %pad_maximum_fusion.3), channel_id=1, source_target_pairs={{0,16},{4,20},{8,24},{12,28},{16,0},{20,4},{24,8},{28,12},{1,17},{... | collective-permute-start | bytes 405512 | tf_op jit(solution)/shard_map/ppermute | solution.py:27
  48.7 2.6 %project.9 = (f32[1,272,128]{2,1,0:T(8,128)S(1)}, f32[1,256,128]{2,1,0:T(8,128)S(1)}) custom-call(s32[2]{0:T(128)S(1)} %pad_add_fusion.idx_ref, bf16[12,3,128,128]{3,2,1,0:T(8,128)(2,1)S(1)} %get-tuple-element.33.refs_0_, f32[12,3,16,8,128]{4,3,2,1,0:T(8,128)S(1)} %get-tuple-element.34.refs_1_.refs_5_, f32[8,3,32,128]{3,2,1,0:T(8,128)S(1)} %get-tuple-element.35.refs_2_, ...), custom_call_target="tpu_custom_call" | custom-call | flops 3221225472 | bytes 1048576 | tf_op jit(solution)/shard_map/project/pallas_call | solution.py:310
  51.3 2.2 %collective-permute-done.11.refs_6_ = bf16[1,528,128]{2,1,0:T(8,128)(2,1)S(1)} collective-permute-done((bf16[1,528,128]{2,1,0:T(8,128)(2,1)S(1)}, bf16[1,528,128]{2,1,0:T(8,128)(2,1)S(1)}, u32[]{:S(2)}, u32[]{:S(2)}) %collective-permute-start.11) | collective-permute-done | bytes 135200 | tf_op jit(solution)/shard_map/ppermute | solution.py:27
  53.6 0.8 %finish.1 = (f32[16,32,128]{2,1,0:T(8,128)}, f32[16,32]{1,0:T(8,128)}) custom-call(f32[1,272,128]{2,1,0:T(8,128)S(1)} %get-tuple-element.56.refs_0_, bf16[4,272,128]{2,1,0:T(8,128)(2,1)S(1)} %collective-permute-done.7.refs_1_, bf16[2,272,128]{2,1,0:T(8,128)(2,1)S(1)} %collective-permute-done.9.refs_2_, f32[1,256,128]{2,1,0:T(8,128)S(1)} %get-tuple-element.57.refs_3_, ...), custom_call_target="tpu_custom_call" | custom-call | tf_op jit(solution)/shard_map/finish/pallas_call | solution.py:405
  (24 shorter events, 1.3 us)
Async XLA Ops:
  2.0 10.8 %collective-permute-start = (bf16[12,3,32,128]{3,2,1,0:T(8,128)(2,1)S(1)}, bf16[12,3,32,128]{3,2,1,0:T(8,128)(2,1)S(1)}, u32[]{:S(2)}, u32[]{:S(2)}) collective-permute-start(bf16[12,3,32,128]{3,2,1,0:T(8,128)(2,1)S(1)} %bitcast.8), channel_id=1, source_target_pairs={{0,2},{1,3},{2,0},{3,1},{4,6},{5,7},{6,4},{7,5},{8,10},{9,11},{10,... | collective-permute-start | bytes 884744 | tf_op jit(solution)/shard_map/ppermute | solution.py:27
  6.0 6.8 %collective-permute-start.1 = (bf16[2,3,32,128]{3,2,1,0:T(8,128)(2,1)S(1)}, bf16[2,3,32,128]{3,2,1,0:T(8,128)(2,1)S(1)}, u32[]{:S(2)}, u32[]{:S(2)}) collective-permute-start(bf16[2,3,32,128]{3,2,1,0:T(8,128)(2,1)S(1)} %bitcast.14), channel_id=1, source_target_pairs={{0,4},{4,8},{8,12},{12,16},{16,20},{20,24},{24,28},{28,0},{1,5},{5... | collective-permute-start | bytes 147464 | tf_op jit(solution)/shard_map/ppermute | solution.py:355
  7.6 5.2 %collective-permute-start.2 = (bf16[2,3,32,128]{3,2,1,0:T(8,128)(2,1)S(1)}, bf16[2,3,32,128]{3,2,1,0:T(8,128)(2,1)S(1)}, u32[]{:S(2)}, u32[]{:S(2)}) collective-permute-start(bf16[2,3,32,128]{3,2,1,0:T(8,128)(2,1)S(1)} %bitcast.16), channel_id=1, source_target_pairs={{4,0},{8,4},{12,8},{16,12},{20,16},{24,20},{28,24},{0,28},{5,1},{9... | collective-permute-start | bytes 147464 | tf_op jit(solution)/shard_map/ppermute | solution.py:356
  10.8 3.1 %collective-permute-start.3 = (bf16[12,3,32,128]{3,2,1,0:T(8,128)(2,1)S(1)}, bf16[12,3,32,128]{3,2,1,0:T(8,128)(2,1)S(1)}, u32[]{:S(2)}, u32[]{:S(2)}) collective-permute-start(bf16[12,3,32,128]{3,2,1,0:T(8,128)(2,1)S(1)} %bitcast.9), channel_id=1, source_target_pairs={{0,1},{1,0},{2,3},{3,2},{4,5},{5,4},{6,7},{7,6},{8,9},{9,8},{10,11... | collective-permute-start | bytes 884744 | tf_op jit(solution)/shard_map/ppermute | solution.py:27
  12.8 1.6 %collective-permute-start.4 = (bf16[12,3,32,128]{3,2,1,0:T(8,128)(2,1)S(1)}, bf16[12,3,32,128]{3,2,1,0:T(8,128)(2,1)S(1)}, u32[]{:S(2)}, u32[]{:S(2)}) collective-permute-start(bf16[12,3,32,128]{3,2,1,0:T(8,128)(2,1)S(1)} %collective-permute-done.refs_1_), channel_id=1, source_target_pairs={{0,1},{1,0},{2,3},{3,2},{4,5},{5,4},{6,7},{7,6},{8,9},{9,8},{10,11... | collective-permute-start | bytes 884744 | tf_op jit(solution)/shard_map/ppermute | solution.py:27
  12.9 8.5 %collective-permute-start.5 = (bf16[1,8,3,32,128]{4,3,2,1,0:T(8,128)(2,1)S(1)}, bf16[1,8,3,32,128]{4,3,2,1,0:T(8,128)(2,1)S(1)}, u32[]{:S(2)}, u32[]{:S(2)}) collective-permute-start(bf16[1,8,3,32,128]{4,3,2,1,0:T(8,128)(2,1)S(1)} %maximum_bitcast_fusion), channel_id=1, source_target_pairs={{0,2},{1,3},{2,0},{3,1},{4,6},{5,7},{6,4},{7,5},{8,10},{9,11},{10,... | collective-permute-start | bytes 589832 | tf_op jit(solution)/shard_map/ppermute | solution.py:27
  21.4 1.8 %collective-permute-start.6 = (bf16[2,8,3,32,128]{4,3,2,1,0:T(8,128)(2,1)S(1)}, bf16[2,8,3,32,128]{4,3,2,1,0:T(8,128)(2,1)S(1)}, u32[]{:S(2)}, u32[]{:S(2)}) collective-permute-start(bf16[2,8,3,32,128]{4,3,2,1,0:T(8,128)(2,1)S(1)} %pad_maximum_fusion.1), channel_id=1, source_target_pairs={{0,1},{1,0},{2,3},{3,2},{4,5},{5,4},{6,7},{7,6},{8,9},{9,8},{10,11... | collective-permute-start | bytes 1179656 | tf_op jit(solution)/shard_map/ppermute | solution.py:27
  30.7 8.4 %collective-permute-start.8 = (bf16[4,256,128]{2,1,0:T(8,128)(2,1)S(1)}, bf16[4,256,128]{2,1,0:T(8,128)(2,1)S(1)}, u32[]{:S(2)}, u32[]{:S(2)}) collective-permute-start(bf16[4,256,128]{2,1,0:T(8,128)(2,1)S(1)} %get-tuple-element.48), channel_id=1, source_target_pairs={{0,8},{4,12},{8,0},{12,4},{16,24},{20,28},{24,16},{28,20},{1,9},{5... | collective-permute-start | bytes 786440 | tf_op jit(solution)/shard_map/ppermute | solution.py:27
  31.9 8.6 %collective-permute-start.7 = (bf16[4,272,128]{2,1,0:T(8,128)(2,1)S(1)}, bf16[4,272,128]{2,1,0:T(8,128)(2,1)S(1)}, u32[]{:S(2)}, u32[]{:S(2)}) collective-permute-start(bf16[4,272,128]{2,1,0:T(8,128)(2,1)S(1)} %get-tuple-element.47), channel_id=1, source_target_pairs={{0,4},{4,0},{8,12},{12,8},{16,20},{20,16},{24,28},{28,24},{1,5},{5... | collective-permute-start | bytes 835592 | tf_op jit(solution)/shard_map/ppermute | solution.py:27
  39.1 5.7 %collective-permute-start.10 = (bf16[2,256,128]{2,1,0:T(8,128)(2,1)S(1)}, bf16[2,256,128]{2,1,0:T(8,128)(2,1)S(1)}, u32[]{:S(2)}, u32[]{:S(2)}) collective-permute-start(bf16[2,256,128]{2,1,0:T(8,128)(2,1)S(1)} %pad_maximum_fusion.4), channel_id=1, source_target_pairs={{0,4},{4,0},{8,12},{12,8},{16,20},{20,16},{24,28},{28,24},{1,5},{5... | collective-permute-start | bytes 393224 | tf_op jit(solution)/shard_map/ppermute | solution.py:27
  40.6 5.1 %collective-permute-start.9 = (bf16[2,272,128]{2,1,0:T(8,128)(2,1)S(1)}, bf16[2,272,128]{2,1,0:T(8,128)(2,1)S(1)}, u32[]{:S(2)}, u32[]{:S(2)}) collective-permute-start(bf16[2,272,128]{2,1,0:T(8,128)(2,1)S(1)} %pad_maximum_fusion.2), channel_id=1, source_target_pairs={{0,8},{4,12},{8,0},{12,4},{16,24},{20,28},{24,16},{28,20},{1,9},{5... | collective-permute-start | bytes 417800 | tf_op jit(solution)/shard_map/ppermute | solution.py:27
  45.8 7.8 %collective-permute-start.11 = (bf16[1,528,128]{2,1,0:T(8,128)(2,1)S(1)}, bf16[1,528,128]{2,1,0:T(8,128)(2,1)S(1)}, u32[]{:S(2)}, u32[]{:S(2)}) collective-permute-start(bf16[1,528,128]{2,1,0:T(8,128)(2,1)S(1)} %pad_maximum_fusion.3), channel_id=1, source_target_pairs={{0,16},{4,20},{8,24},{12,28},{16,0},{20,4},{24,8},{28,12},{1,17},{... | collective-permute-start | bytes 405512 | tf_op jit(solution)/shard_map/ppermute | solution.py:27

commit v9 on v8

--- a/solution.py
+++ b/solution.py
@@ -368,7 +368,9 @@
     both = tuple(range(PARTS))
     results = [[], []]
     states = [prepare(plans[0], masks, cells_z, idx, pieces, (), own)]
-    begun = project(plans[:1], 0, both, idx, states, own, peers_x, F32, viscous=False)
+    begun = []
+    for part in both:
+        begun += project(plans[:1], 0, (part,), idx, states, own, peers_x, F32, viscous=False)
     rim = gathered_stack(
         jnp.concatenate([before, block[:quarter - 2], block[cells_x - quarter + 2:], after], 0),
         "gy", begun[0],

time: 54.5 us -> 55.3 us (1.015)
  starting transfers between devices: 18 us -> 16.7 us
  waiting for transfers between devices: 7.86 us -> 8.94 us
  Pallas kernels: 25 us -> 25.9 us
    ppermute x10, starting transfers between devices: 13.2 us -> 11.9 us  [swap(): lax.ppermute(x, axis, [(i, i ^ mask) for i in range(lax.axis_size(axis))])]
    ppermute x10, waiting for transfers between devices: 5.89 us -> 6.97 us  [swap(): lax.ppermute(x, axis, [(i, i ^ mask) for i in range(lax.axis_size(axis))])]
    pallas_call x5 -> x6, Pallas kernels: 18.9 us -> 19.8 us  [project(): pl.pallas_call(functools.partial(main_kernel, plans, own, stage, layout,...]
  transfers between devices with their start and end apart: 12 -> 12, of which waited for: 6 -> 7; matrix products, arithmetic and copies ran while one was open for 2% -> 2% of each run, Pallas kernels for 31% -> 32%
where the time goes in v9:
time: 55.3 us; the launch traced here: 55.1 us
  Pallas kernels  25.9 us (47%)
  starting transfers between devices  16.7 us (30%)
  waiting for transfers between devices  8.94 us (16%)
  local copies, waits for them, and re-layouts  2.34 us (4%)
  between operations  0.8 us (1%)
    pallas_call x6, Pallas kernels, project(): pl.pallas_call(functools.partial(main_kernel, plans, own, stage, layout,...  19.8 us
    ppermute x10, starting transfers between devices, swap(): lax.ppermute(x, axis, [(i, i ^ mask) for i in range(lax.axis_size(axis))])  11.9 us
    ppermute x10, waiting for transfers between devices, swap(): lax.ppermute(x, axis, [(i, i ^ mask) for i in range(lax.axis_size(axis))])  6.97 us
    pallas_call x2, Pallas kernels, prepare(): pl.pallas_call(functools.partial(prepare_kernel, plan, masks, cells_z, ti...  5.34 us
    ppermute x1, starting transfers between devices, body(): after = lax.ppermute(block[:2], 'gx', down)  3.26 us
    ppermute x1, waiting for transfers between devices, body(): before = lax.ppermute(block[-2:], 'gx', up)  1.97 us
    ppermute x1, starting transfers between devices, body(): before = lax.ppermute(block[-2:], 'gx', up)  1.57 us
    slice x2, local copies, waits for them, and re-layouts, body(): middle = block[quarter - 2:cells_x - quarter + 2]  1.37 us
  transfers between devices with their start and end apart: 12, of which 7 were waited for; matrix products, arithmetic and copies ran while one was open for 2% of the time, Pallas kernels for 32%

profile of v9, /device:TPU:0, one launch (start us, length us, event | category | flops | bytes accessed | tf_op | source)
XLA Modules:
  0.0 55.1 jit_solution(12317517799978696949)
XLA Ops:
  0.6 1.2 %slice.74 = bf16[12,3,16,2,128]{4,3,1,2,0:T(2,128)(2,1)S(1)} slice(bf16[16,3,16,2,128]{4,3,1,2,0:T(2,128)(2,1)} %bitcast.12), slice={[2:14], [0:3], [0:16], [0:2], [0:128]} | slice | bytes 589824 | tf_op jit(solution)/shard_map/slice | solution.py:354
  2.0 3.0 %collective-permute-start = (bf16[12,3,32,128]{3,2,1,0:T(8,128)(2,1)S(1)}, bf16[12,3,32,128]{3,2,1,0:T(8,128)(2,1)S(1)}, u32[]{:S(2)}, u32[]{:S(2)}) collective-permute-start(bf16[12,3,32,128]{3,2,1,0:T(8,128)(2,1)S(1)} %bitcast.8), channel_id=1, source_target_pairs={{0,2},{1,3},{2,0},{3,1},{4,6},{5,7},{6,4},{7,5},{8,10},{9,11},{10,... | collective-permute-start | bytes 884744 | tf_op jit(solution)/shard_map/ppermute | solution.py:27
  5.0 0.9 %fusion = (bf16[2,3,16,2,128]{4,3,1,2,0:T(2,128)(2,1)S(1)}, bf16[2,3,16,2,128]{4,3,1,2,0:T(2,128)(2,1)S(1)}) fusion(bf16[16,3,16,2,128]{4,3,1,2,0:T(2,128)(2,1)} %bitcast.13), kind=kLoop, calls=%fused_computation.13 | loop fusion | bytes 196608 | tf_op jit(solution)/shard_map/slice | solution.py:356
  6.0 1.6 %collective-permute-start.1 = (bf16[2,3,32,128]{3,2,1,0:T(8,128)(2,1)S(1)}, bf16[2,3,32,128]{3,2,1,0:T(8,128)(2,1)S(1)}, u32[]{:S(2)}, u32[]{:S(2)}) collective-permute-start(bf16[2,3,32,128]{3,2,1,0:T(8,128)(2,1)S(1)} %bitcast.14), channel_id=1, source_target_pairs={{0,4},{4,8},{8,12},{12,16},{16,20},{20,24},{24,28},{28,0},{1,5},{5... | collective-permute-start | bytes 147464 | tf_op jit(solution)/shard_map/ppermute | solution.py:355
  7.6 3.3 %collective-permute-start.2 = (bf16[2,3,32,128]{3,2,1,0:T(8,128)(2,1)S(1)}, bf16[2,3,32,128]{3,2,1,0:T(8,128)(2,1)S(1)}, u32[]{:S(2)}, u32[]{:S(2)}) collective-permute-start(bf16[2,3,32,128]{3,2,1,0:T(8,128)(2,1)S(1)} %bitcast.16), channel_id=1, source_target_pairs={{4,0},{8,4},{12,8},{16,12},{20,16},{24,20},{28,24},{0,28},{5,1},{9... | collective-permute-start | bytes 147464 | tf_op jit(solution)/shard_map/ppermute | solution.py:356
  10.8 2.0 %collective-permute-done.1 = bf16[2,3,32,128]{3,2,1,0:T(8,128)(2,1)S(1)} collective-permute-done((bf16[2,3,32,128]{3,2,1,0:T(8,128)(2,1)S(1)}, bf16[2,3,32,128]{3,2,1,0:T(8,128)(2,1)S(1)}, u32[]{:S(2)}, u32[]{:S(2)}) %collective-permute-start.1) | collective-permute-done | bytes 49184 | tf_op jit(solution)/shard_map/ppermute | solution.py:355
  12.9 1.0 %collective-permute-start.5 = (bf16[1,8,3,32,128]{4,3,2,1,0:T(8,128)(2,1)S(1)}, bf16[1,8,3,32,128]{4,3,2,1,0:T(8,128)(2,1)S(1)}, u32[]{:S(2)}, u32[]{:S(2)}) collective-permute-start(bf16[1,8,3,32,128]{4,3,2,1,0:T(8,128)(2,1)S(1)} %maximum_bitcast_fusion), channel_id=1, source_target_pairs={{0,2},{1,3},{2,0},{3,1},{4,6},{5,7},{6,4},{7,5},{8,10},{9,11},{10,... | collective-permute-start | bytes 589832 | tf_op jit(solution)/shard_map/ppermute | solution.py:27
  14.4 2.8 %prepare.2 = (bf16[12,3,128,128]{3,2,1,0:T(8,128)(2,1)S(1)}, f32[12,3,16,8,128]{4,3,2,1,0:T(8,128)S(1)}, f32[8,3,32,128]{3,2,1,0:T(8,128)S(1)}, bf16[8,2,3,32,128]{4,3,2,1,0:T(8,128)(2,1)S(1)}, f32[128,32]{1,0:T(8,128)S(1)}) custom-call(s32[2]{0:T(128)S(1)} %pad_add_fusion.idx_ref, bf16[12,3,32,128]{3,2,1,0:T(8,128)(2,1)S(1)} %bitcast.10, ...), custom_call_target="tpu_custom_call" | custom-call | tf_op jit(solution)/shard_map/prepare/pallas_call | solution.py:279
  17.2 2.6 %project.6.refs_5_ = f32[4,256,128]{2,1,0:T(8,128)S(1)} custom-call(s32[2]{0:T(128)S(1)} %pad_add_fusion.idx_ref, bf16[12,3,128,128]{3,2,1,0:T(8,128)(2,1)S(1)} %get-tuple-element.31.refs_0_, f32[12,3,16,8,128]{4,3,2,1,0:T(8,128)S(1)} %get-tuple-element.32.refs_1_.refs_5_, f32[8,3,32,128]{3,2,1,0:T(8,128)S(1)} %get-tuple-element.33.refs_2_, ...), custom_call_target="tpu_custom_call" | custom-call | flops 3221225472 | bytes 1048576 | tf_op jit(solution)/shard_map/project/pallas_call | solution.py:310
  20.4 2.6 %project.7.refs_6_ = f32[4,256,128]{2,1,0:T(8,128)S(1)} custom-call(s32[2]{0:T(128)S(1)} %pad_add_fusion.idx_ref, bf16[12,3,128,128]{3,2,1,0:T(8,128)(2,1)S(1)} %get-tuple-element.31.refs_0_, f32[12,3,16,8,128]{4,3,2,1,0:T(8,128)S(1)} %get-tuple-element.32.refs_1_.refs_5_, f32[8,3,32,128]{3,2,1,0:T(8,128)S(1)} %get-tuple-element.33.refs_2_, ...), custom_call_target="tpu_custom_call" | custom-call | flops 3221225472 | bytes 1048576 | tf_op jit(solution)/shard_map/project/pallas_call | solution.py:310
  23.1 2.5 %prepare.3 = (bf16[16,3,128,128]{3,2,1,0:T(8,128)(2,1)S(1)}, f32[16,3,16,8,128]{4,3,2,1,0:T(8,128)S(1)}, f32[8,3,32,128]{3,2,1,0:T(8,128)S(1)}, bf16[8,2,3,32,128]{4,3,2,1,0:T(8,128)(2,1)S(1)}, f32[128,32]{1,0:T(8,128)S(1)}) custom-call(s32[2]{0:T(128)S(1)} %pad_add_fusion.idx_ref, bf16[12,3,32,128]{3,2,1,0:T(8,128)(2,1)S(1)} %bitcast.11, ...), custom_call_target="tpu_custom_call" | custom-call | tf_op jit(solution)/shard_map/prepare/pallas_call | solution.py:279
  25.6 4.8 %project.8 = (bf16[4,272,128]{2,1,0:T(8,128)(2,1)S(1)}, bf16[4,256,128]{2,1,0:T(8,128)(2,1)S(1)}) custom-call(s32[2]{0:T(128)S(1)} %pad_add_fusion.idx_ref, bf16[16,3,128,128]{3,2,1,0:T(8,128)(2,1)S(1)} %get-tuple-element.38.refs_0_.refs_5_, f32[16,3,16,8,128]{4,3,2,1,0:T(8,128)S(1)} %get-tuple-element.39.refs_1_.refs_6_, ...), custom_call_target="tpu_custom_call" | custom-call | flops 6442450944 | bytes 1048576 | tf_op jit(solution)/shard_map/project/pallas_call | solution.py:310
  30.4 1.4 %collective-permute-start.7 = (bf16[4,272,128]{2,1,0:T(8,128)(2,1)S(1)}, bf16[4,272,128]{2,1,0:T(8,128)(2,1)S(1)}, u32[]{:S(2)}, u32[]{:S(2)}) collective-permute-start(bf16[4,272,128]{2,1,0:T(8,128)(2,1)S(1)} %get-tuple-element.43), channel_id=1, source_target_pairs={{0,4},{4,0},{8,12},{12,8},{16,20},{20,16},{24,28},{28,24},{1,5},{5... | collective-permute-start | bytes 835592 | tf_op jit(solution)/shard_map/ppermute | solution.py:27
  31.8 1.6 %collective-permute-start.8 = (bf16[4,256,128]{2,1,0:T(8,128)(2,1)S(1)}, bf16[4,256,128]{2,1,0:T(8,128)(2,1)S(1)}, u32[]{:S(2)}, u32[]{:S(2)}) collective-permute-start(bf16[4,256,128]{2,1,0:T(8,128)(2,1)S(1)} %get-tuple-element.44), channel_id=1, source_target_pairs={{0,8},{4,12},{8,0},{12,4},{16,24},{20,28},{24,16},{28,20},{1,9},{5... | collective-permute-start | bytes 786440 | tf_op jit(solution)/shard_map/ppermute | solution.py:27
  33.4 4.7 %project.9 = (f32[2,272,128]{2,1,0:T(8,128)S(1)}, f32[2,256,128]{2,1,0:T(8,128)S(1)}) custom-call(s32[2]{0:T(128)S(1)} %pad_add_fusion.idx_ref, bf16[12,3,128,128]{3,2,1,0:T(8,128)(2,1)S(1)} %get-tuple-element.31.refs_0_, f32[12,3,16,8,128]{4,3,2,1,0:T(8,128)S(1)} %get-tuple-element.32.refs_1_.refs_5_, f32[8,3,32,128]{3,2,1,0:T(8,128)S(1)} %get-tuple-element.33.refs_2_, ...), custom_call_target="tpu_custom_call" | custom-call | flops 6442450944 | bytes 1048576 | tf_op jit(solution)/shard_map/project/pallas_call | solution.py:310
  38.1 2.2 %collective-permute-done.8.refs_4_ = bf16[4,256,128]{2,1,0:T(8,128)(2,1)S(1)} collective-permute-done((bf16[4,256,128]{2,1,0:T(8,128)(2,1)S(1)}, bf16[4,256,128]{2,1,0:T(8,128)(2,1)S(1)}, u32[]{:S(2)}, u32[]{:S(2)}) %collective-permute-start.8) | collective-permute-done | bytes 262176 | tf_op jit(solution)/shard_map/ppermute | solution.py:27
  40.3 0.7 %collective-permute-start.10 = (bf16[2,256,128]{2,1,0:T(8,128)(2,1)S(1)}, bf16[2,256,128]{2,1,0:T(8,128)(2,1)S(1)}, u32[]{:S(2)}, u32[]{:S(2)}) collective-permute-start(bf16[2,256,128]{2,1,0:T(8,128)(2,1)S(1)} %pad_maximum_fusion.4), channel_id=1, source_target_pairs={{0,4},{4,0},{8,12},{12,8},{16,20},{20,16},{24,28},{28,24},{1,5},{5... | collective-permute-start | bytes 393224 | tf_op jit(solution)/shard_map/ppermute | solution.py:27
  41.1 1.3 %collective-permute-start.9 = (bf16[2,272,128]{2,1,0:T(8,128)(2,1)S(1)}, bf16[2,272,128]{2,1,0:T(8,128)(2,1)S(1)}, u32[]{:S(2)}, u32[]{:S(2)}) collective-permute-start(bf16[2,272,128]{2,1,0:T(8,128)(2,1)S(1)} %pad_maximum_fusion.2), channel_id=1, source_target_pairs={{0,8},{4,12},{8,0},{12,4},{16,24},{20,28},{24,16},{28,20},{1,9},{5... | collective-permute-start | bytes 417800 | tf_op jit(solution)/shard_map/ppermute | solution.py:27
  42.4 2.6 %project.10 = (f32[1,272,128]{2,1,0:T(8,128)S(1)}, f32[1,256,128]{2,1,0:T(8,128)S(1)}) custom-call(s32[2]{0:T(128)S(1)} %pad_add_fusion.idx_ref, bf16[12,3,128,128]{3,2,1,0:T(8,128)(2,1)S(1)} %get-tuple-element.31.refs_0_, f32[12,3,16,8,128]{4,3,2,1,0:T(8,128)S(1)} %get-tuple-element.32.refs_1_.refs_5_, f32[8,3,32,128]{3,2,1,0:T(8,128)S(1)} %get-tuple-element.33.refs_2_, ...), custom_call_target="tpu_custom_call" | custom-call | flops 3221225472 | bytes 1048576 | tf_op jit(solution)/shard_map/project/pallas_call | solution.py:310
  45.4 0.9 %collective-permute-done.9.refs_2_ = bf16[2,272,128]{2,1,0:T(8,128)(2,1)S(1)} collective-permute-done((bf16[2,272,128]{2,1,0:T(8,128)(2,1)S(1)}, bf16[2,272,128]{2,1,0:T(8,128)(2,1)S(1)}, u32[]{:S(2)}, u32[]{:S(2)}) %collective-permute-start.9) | collective-permute-done | bytes 139296 | tf_op jit(solution)/shard_map/ppermute | solution.py:27
  46.3 2.7 %collective-permute-start.11 = (bf16[1,528,128]{2,1,0:T(8,128)(2,1)S(1)}, bf16[1,528,128]{2,1,0:T(8,128)(2,1)S(1)}, u32[]{:S(2)}, u32[]{:S(2)}) collective-permute-start(bf16[1,528,128]{2,1,0:T(8,128)(2,1)S(1)} %pad_maximum_fusion.3), channel_id=1, source_target_pairs={{0,16},{4,20},{8,24},{12,28},{16,0},{20,4},{24,8},{28,12},{1,17},{... | collective-permute-start | bytes 405512 | tf_op jit(solution)/shard_map/ppermute | solution.py:27
  49.0 2.6 %project.11 = (f32[1,272,128]{2,1,0:T(8,128)S(1)}, f32[1,256,128]{2,1,0:T(8,128)S(1)}) custom-call(s32[2]{0:T(128)S(1)} %pad_add_fusion.idx_ref, bf16[12,3,128,128]{3,2,1,0:T(8,128)(2,1)S(1)} %get-tuple-element.31.refs_0_, f32[12,3,16,8,128]{4,3,2,1,0:T(8,128)S(1)} %get-tuple-element.32.refs_1_.refs_5_, f32[8,3,32,128]{3,2,1,0:T(8,128)S(1)} %get-tuple-element.33.refs_2_, ...), custom_call_target="tpu_custom_call" | custom-call | flops 3221225472 | bytes 1048576 | tf_op jit(solution)/shard_map/project/pallas_call | solution.py:310
  51.6 2.7 %collective-permute-done.11.refs_6_ = bf16[1,528,128]{2,1,0:T(8,128)(2,1)S(1)} collective-permute-done((bf16[1,528,128]{2,1,0:T(8,128)(2,1)S(1)}, bf16[1,528,128]{2,1,0:T(8,128)(2,1)S(1)}, u32[]{:S(2)}, u32[]{:S(2)}) %collective-permute-start.11) | collective-permute-done | bytes 135200 | tf_op jit(solution)/shard_map/ppermute | solution.py:27
  54.3 0.8 %finish.1 = (f32[16,32,128]{2,1,0:T(8,128)}, f32[16,32]{1,0:T(8,128)}) custom-call(f32[1,272,128]{2,1,0:T(8,128)S(1)} %get-tuple-element.52.refs_0_, bf16[4,272,128]{2,1,0:T(8,128)(2,1)S(1)} %collective-permute-done.7.refs_1_, bf16[2,272,128]{2,1,0:T(8,128)(2,1)S(1)} %collective-permute-done.9.refs_2_, f32[1,256,128]{2,1,0:T(8,128)S(1)} %get-tuple-element.53.refs_3_, ...), custom_call_target="tpu_custom_call" | custom-call | tf_op jit(solution)/shard_map/finish/pallas_call | solution.py:407
  (25 shorter events, 2.0 us)
Async XLA Ops:
  2.0 10.8 %collective-permute-start = (bf16[12,3,32,128]{3,2,1,0:T(8,128)(2,1)S(1)}, bf16[12,3,32,128]{3,2,1,0:T(8,128)(2,1)S(1)}, u32[]{:S(2)}, u32[]{:S(2)}) collective-permute-start(bf16[12,3,32,128]{3,2,1,0:T(8,128)(2,1)S(1)} %bitcast.8), channel_id=1, source_target_pairs={{0,2},{1,3},{2,0},{3,1},{4,6},{5,7},{6,4},{7,5},{8,10},{9,11},{10,... | collective-permute-start | bytes 884744 | tf_op jit(solution)/shard_map/ppermute | solution.py:27
  6.0 6.8 %collective-permute-start.1 = (bf16[2,3,32,128]{3,2,1,0:T(8,128)(2,1)S(1)}, bf16[2,3,32,128]{3,2,1,0:T(8,128)(2,1)S(1)}, u32[]{:S(2)}, u32[]{:S(2)}) collective-permute-start(bf16[2,3,32,128]{3,2,1,0:T(8,128)(2,1)S(1)} %bitcast.14), channel_id=1, source_target_pairs={{0,4},{4,8},{8,12},{12,16},{16,20},{20,24},{24,28},{28,0},{1,5},{5... | collective-permute-start | bytes 147464 | tf_op jit(solution)/shard_map/ppermute | solution.py:355
  7.6 5.2 %collective-permute-start.2 = (bf16[2,3,32,128]{3,2,1,0:T(8,128)(2,1)S(1)}, bf16[2,3,32,128]{3,2,1,0:T(8,128)(2,1)S(1)}, u32[]{:S(2)}, u32[]{:S(2)}) collective-permute-start(bf16[2,3,32,128]{3,2,1,0:T(8,128)(2,1)S(1)} %bitcast.16), channel_id=1, source_target_pairs={{4,0},{8,4},{12,8},{16,12},{20,16},{24,20},{28,24},{0,28},{5,1},{9... | collective-permute-start | bytes 147464 | tf_op jit(solution)/shard_map/ppermute | solution.py:356
  10.8 3.1 %collective-permute-start.3 = (bf16[12,3,32,128]{3,2,1,0:T(8,128)(2,1)S(1)}, bf16[12,3,32,128]{3,2,1,0:T(8,128)(2,1)S(1)}, u32[]{:S(2)}, u32[]{:S(2)}) collective-permute-start(bf16[12,3,32,128]{3,2,1,0:T(8,128)(2,1)S(1)} %bitcast.9), channel_id=1, source_target_pairs={{0,1},{1,0},{2,3},{3,2},{4,5},{5,4},{6,7},{7,6},{8,9},{9,8},{10,11... | collective-permute-start | bytes 884744 | tf_op jit(solution)/shard_map/ppermute | solution.py:27
  12.8 1.6 %collective-permute-start.4 = (bf16[12,3,32,128]{3,2,1,0:T(8,128)(2,1)S(1)}, bf16[12,3,32,128]{3,2,1,0:T(8,128)(2,1)S(1)}, u32[]{:S(2)}, u32[]{:S(2)}) collective-permute-start(bf16[12,3,32,128]{3,2,1,0:T(8,128)(2,1)S(1)} %collective-permute-done.refs_1_), channel_id=1, source_target_pairs={{0,1},{1,0},{2,3},{3,2},{4,5},{5,4},{6,7},{7,6},{8,9},{9,8},{10,11... | collective-permute-start | bytes 884744 | tf_op jit(solution)/shard_map/ppermute | solution.py:27
  12.9 7.4 %collective-permute-start.5 = (bf16[1,8,3,32,128]{4,3,2,1,0:T(8,128)(2,1)S(1)}, bf16[1,8,3,32,128]{4,3,2,1,0:T(8,128)(2,1)S(1)}, u32[]{:S(2)}, u32[]{:S(2)}) collective-permute-start(bf16[1,8,3,32,128]{4,3,2,1,0:T(8,128)(2,1)S(1)} %maximum_bitcast_fusion), channel_id=1, source_target_pairs={{0,2},{1,3},{2,0},{3,1},{4,6},{5,7},{6,4},{7,5},{8,10},{9,11},{10,... | collective-permute-start | bytes 589832 | tf_op jit(solution)/shard_map/ppermute | solution.py:27
  20.3 2.6 %collective-permute-start.6 = (bf16[2,8,3,32,128]{4,3,2,1,0:T(8,128)(2,1)S(1)}, bf16[2,8,3,32,128]{4,3,2,1,0:T(8,128)(2,1)S(1)}, u32[]{:S(2)}, u32[]{:S(2)}) collective-permute-start(bf16[2,8,3,32,128]{4,3,2,1,0:T(8,128)(2,1)S(1)} %pad_maximum_fusion.1), channel_id=1, source_target_pairs={{0,1},{1,0},{2,3},{3,2},{4,5},{5,4},{6,7},{7,6},{8,9},{9,8},{10,11... | collective-permute-start | bytes 1179656 | tf_op jit(solution)/shard_map/ppermute | solution.py:27
  30.4 10.6 %collective-permute-start.7 = (bf16[4,272,128]{2,1,0:T(8,128)(2,1)S(1)}, bf16[4,272,128]{2,1,0:T(8,128)(2,1)S(1)}, u32[]{:S(2)}, u32[]{:S(2)}) collective-permute-start(bf16[4,272,128]{2,1,0:T(8,128)(2,1)S(1)} %get-tuple-element.43), channel_id=1, source_target_pairs={{0,4},{4,0},{8,12},{12,8},{16,20},{20,16},{24,28},{28,24},{1,5},{5... | collective-permute-start | bytes 835592 | tf_op jit(solution)/shard_map/ppermute | solution.py:27
  31.8 8.4 %collective-permute-start.8 = (bf16[4,256,128]{2,1,0:T(8,128)(2,1)S(1)}, bf16[4,256,128]{2,1,0:T(8,128)(2,1)S(1)}, u32[]{:S(2)}, u32[]{:S(2)}) collective-permute-start(bf16[4,256,128]{2,1,0:T(8,128)(2,1)S(1)} %get-tuple-element.44), channel_id=1, source_target_pairs={{0,8},{4,12},{8,0},{12,4},{16,24},{20,28},{24,16},{28,20},{1,9},{5... | collective-permute-start | bytes 786440 | tf_op jit(solution)/shard_map/ppermute | solution.py:27
  40.3 5.0 %collective-permute-start.10 = (bf16[2,256,128]{2,1,0:T(8,128)(2,1)S(1)}, bf16[2,256,128]{2,1,0:T(8,128)(2,1)S(1)}, u32[]{:S(2)}, u32[]{:S(2)}) collective-permute-start(bf16[2,256,128]{2,1,0:T(8,128)(2,1)S(1)} %pad_maximum_fusion.4), channel_id=1, source_target_pairs={{0,4},{4,0},{8,12},{12,8},{16,20},{20,16},{24,28},{28,24},{1,5},{5... | collective-permute-start | bytes 393224 | tf_op jit(solution)/shard_map/ppermute | solution.py:27
  41.1 5.1 %collective-permute-start.9 = (bf16[2,272,128]{2,1,0:T(8,128)(2,1)S(1)}, bf16[2,272,128]{2,1,0:T(8,128)(2,1)S(1)}, u32[]{:S(2)}, u32[]{:S(2)}) collective-permute-start(bf16[2,272,128]{2,1,0:T(8,128)(2,1)S(1)} %pad_maximum_fusion.2), channel_id=1, source_target_pairs={{0,8},{4,12},{8,0},{12,4},{16,24},{20,28},{24,16},{28,20},{1,9},{5... | collective-permute-start | bytes 417800 | tf_op jit(solution)/shard_map/ppermute | solution.py:27
  46.3 8.0 %collective-permute-start.11 = (bf16[1,528,128]{2,1,0:T(8,128)(2,1)S(1)}, bf16[1,528,128]{2,1,0:T(8,128)(2,1)S(1)}, u32[]{:S(2)}, u32[]{:S(2)}) collective-permute-start(bf16[1,528,128]{2,1,0:T(8,128)(2,1)S(1)} %pad_maximum_fusion.3), channel_id=1, source_target_pairs={{0,16},{4,20},{8,24},{12,28},{16,0},{20,4},{24,8},{28,12},{1,17},{... | collective-permute-start | bytes 405512 | tf_op jit(solution)/shard_map/ppermute | solution.py:27
